TPU v7x, 32 devices: a whole 2x2x4 slice. The times are simulated.
32 devices in a mesh: seq: 8 (over y, x, core), batch: 4 (over z).
Axes of the slice: x: 2, y: 2, z: 4, core: 2. Of those that a mesh axis runs over, the one named last changes fastest.
Arguments:
- tokens: bfloat16 [4, 2048, 2048], P('batch', 'seq'), may hold values from -6 to 6
- out_cotangent: bfloat16 [4, 2048, 2048], P('batch', 'seq'), may hold values from -6 to 6
- group_ids: int32 [4, 2048], P('batch', 'seq'), may hold values from 0 to 15, as said below
- attn_gain: bfloat16 [2048], P(('seq', 'batch')), may hold values from 0.5 to 1.5
- query_weight: bfloat16 [2048, 2048], P(('seq', 'batch')), may hold values from -0.125 to 0.125
- key_weight: bfloat16 [2048, 2048], P(('seq', 'batch')), may hold values from -0.125 to 0.125
- value_weight: bfloat16 [2048, 2048], P(('seq', 'batch')), may hold values from -0.125 to 0.125
- out_weight: bfloat16 [2048, 2048], P(('seq', 'batch')), may hold values from -0.5 to 0.5
- ffn_gain: bfloat16 [2048], P(('seq', 'batch')), may hold values from 0.5 to 1.5
- gate_weight: bfloat16 [2048, 5632], P(('seq', 'batch')), may hold values from -0.125 to 0.125
- up_weight: bfloat16 [2048, 5632], P(('seq', 'batch')), may hold values from -0.125 to 0.125
- down_weight: bfloat16 [5632, 2048], P(('seq', 'batch')), may hold values from -0.078125 to 0.078125
Outputs:
- block_out: bfloat16 [4, 2048, 2048], P('batch', 'seq')
- tokens_grad: float32 [4, 2048, 2048], P('batch', 'seq')
- attn_gain_grad: float32 [2048], P(('seq', 'batch'))
- query_grad: float32 [2048, 2048], P(('seq', 'batch'))
- key_grad: float32 [2048, 2048], P(('seq', 'batch'))
- value_grad: float32 [2048, 2048], P(('seq', 'batch'))
- out_grad: float32 [2048, 2048], P(('seq', 'batch'))
- ffn_gain_grad: float32 [2048], P(('seq', 'batch'))
- gate_grad: float32 [2048, 5632], P(('seq', 'batch'))
- up_grad: float32 [2048, 5632], P(('seq', 'batch'))
- down_grad: float32 [5632, 2048], P(('seq', 'batch'))
Inputs may be any that keep to these rules, and one draw needn't show every extreme that they name: `group_ids`: sequence s (its index along the first dimension) carries only the ids s * 4 to s * 4 + 3, and each of them.
All inputs are finite; a program needn't handle non-finite values.
Results may differ from a plain program's by a relative error of at most 0.015.
Values may be sent and summed in bfloat16 or wider, within the bound.
No kernel may reach another device: no remote copies, remote signals or barrier semaphores. Data moves between devices by JAX's collectives and lax.ppermute only.
A program may use at most 704 MiB of HBM per device.

v0:
```python
import jax
import jax.numpy as jnp
from jax import lax
from jax.sharding import PartitionSpec as P

HEAD = 128
WINDOW = 64
GPS = 4


EPS = 1e-05
NEGATIVE = -1e30
ROWS_DIMS = (((0,), (0,)), ((), ()))
COLS_DIMS = (((1,), (1,)), ((), ()))


def shifted(value, axis, steps):
    count = lax.axis_size(axis)
    first, last = (max(0, -steps), min(count, count - steps))
    return lax.ppermute(value, axis, [(source, source + steps) for source in range(first, last)])


def to_heads(values):
    return values.reshape(values.shape[:-1] + (values.shape[-1] // HEAD, HEAD))


def blocks_with_rim(values, rim, block_rows):
    seq_count, tok_count, features = values.shape
    rim_rows = rim.shape[1]
    owned = values.reshape(seq_count, tok_count // block_rows, block_rows, features)
    before = jnp.concatenate([rim[:, None], owned[:, :-1, block_rows - rim_rows :]], axis=1)
    return jnp.concatenate([before, owned], axis=2)


def window_allowed(block_count, block_rows, rim_rows, position):
    query_place = jnp.arange(block_rows, dtype=jnp.int32)[:, None]
    key_place = jnp.arange(block_rows + rim_rows, dtype=jnp.int32)[None, :] - rim_rows
    distance = query_place - key_place
    inside = (distance >= 0) & (distance < rim_rows)
    block_index = jnp.arange(block_count, dtype=jnp.int32)[:, None, None]
    reach = (block_index > 0) | (key_place[None] >= 0) | (position > 0)
    return inside[None] & reach


def window_scores(query_blocks, key_blocks, allowed):
    scores = jnp.einsum(
        "snqhe,snkhe->snhqk", query_blocks, key_blocks, preferred_element_type=jnp.float32
    ) * HEAD ** (-0.5)
    return jnp.where(allowed[None, :, None], scores, NEGATIVE)


def attend(query_blocks, key_blocks, value_blocks, allowed):
    scores = window_scores(query_blocks, key_blocks, allowed)
    top = jnp.max(scores, axis=-1, keepdims=True)
    expo = jnp.exp(scores - top)
    total = jnp.sum(expo, axis=-1, keepdims=True)
    probs_low = (expo / total).astype(jnp.bfloat16)
    mixed = jnp.einsum(
        "snhqk,snkhe->snqhe", probs_low, value_blocks, preferred_element_type=jnp.float32
    )
    return (mixed, top + jnp.log(total))


def attend_back(query_blocks, key_blocks, value_blocks, allowed, log_total, d_mixed_blocks):
    probs = jnp.exp(window_scores(query_blocks, key_blocks, allowed) - log_total)
    probs_again = probs.astype(jnp.bfloat16)
    d_probs = jnp.einsum(
        "snqhe,snkhe->snhqk", d_mixed_blocks, value_blocks, preferred_element_type=jnp.float32
    )
    d_scores = (probs * (d_probs - jnp.sum(probs * d_probs, axis=-1, keepdims=True))).astype(
        jnp.bfloat16
    )
    factor = HEAD ** (-0.5)
    d_query = (
        jnp.einsum("snhqk,snkhe->snqhe", d_scores, key_blocks, preferred_element_type=jnp.float32)
        * factor
    )
    d_keys = (
        jnp.einsum("snhqk,snqhe->snkhe", d_scores, query_blocks, preferred_element_type=jnp.float32)
        * factor
    )
    d_values = jnp.einsum(
        "snhqk,snqhe->snkhe", probs_again, d_mixed_blocks, preferred_element_type=jnp.float32
    )
    return (d_query, d_keys, d_values)


def fold_rims(d_blocks, arrived, block_rows):
    later = jnp.concatenate([d_blocks[:, :, 1:, :WINDOW], arrived[:, :, None]], axis=2)
    padded = jnp.pad(later, ((0, 0), (0, 0), (0, 0), (block_rows - WINDOW, 0), (0, 0)))
    return d_blocks[:, :, :, WINDOW:] + padded


def norm_back(d_act, gain, normed, inverse, upstream):
    scaled = d_act * gain
    result = upstream + inverse * (
        scaled - normed * jnp.mean(scaled * normed, axis=-1, keepdims=True)
    )
    return (result, jnp.sum(d_act * normed, axis=0))


def per_device(
    tokens,
    out_cotangent,
    group_ids,
    attn_gain,
    query_weight,
    key_weight,
    value_weight,
    out_weight,
    ffn_gain,
    gate_weight,
    up_weight,
    down_weight,
):
    seq_count, tok_count, features = tokens.shape
    all_rows = seq_count * tok_count
    flat_in = tokens.reshape(all_rows, features).astype(jnp.float32)
    inverse_one = lax.rsqrt(jnp.mean(flat_in * flat_in, axis=-1, keepdims=True) + EPS)
    normed_one = flat_in * inverse_one
    group_span = seq_count * GPS * lax.axis_size("batch")
    onehot = (
        group_ids[:, :, None] == jnp.arange(group_span, dtype=jnp.int32)[None, None, :]
    ).astype(jnp.float32)
    group_total = lax.psum(jnp.sum(onehot, axis=(0, 1)), ("seq", "batch"))
    own_total = jnp.sum(onehot * group_total, axis=-1).reshape(all_rows, 1)
    weighting = tok_count * lax.axis_size("seq") / (GPS * own_total)
    d_final = out_cotangent.reshape(all_rows, features).astype(jnp.float32) * weighting
    d_ffn = d_final.astype(jnp.bfloat16)
    block_rows = 128
    block_count = tok_count // block_rows
    gain_low_one, query_whole, key_whole, value_whole, out_whole = (
        lax.all_gather(attn_gain, ("seq", "batch"), axis=0, tiled=True),
        lax.all_gather(query_weight, ("seq", "batch"), axis=0, tiled=True),
        lax.all_gather(key_weight, ("seq", "batch"), axis=0, tiled=True),
        lax.all_gather(value_weight, ("seq", "batch"), axis=0, tiled=True),
        lax.all_gather(out_weight, ("seq", "batch"), axis=0, tiled=True),
    )
    gain_one = gain_low_one.astype(jnp.float32)
    act_one = (normed_one * gain_one).astype(jnp.bfloat16)
    queries = jnp.dot(act_one, query_whole, preferred_element_type=jnp.float32).astype(jnp.bfloat16)
    keys_low = jnp.dot(act_one, key_whole, preferred_element_type=jnp.float32).astype(jnp.bfloat16)
    values_low = jnp.dot(act_one, value_whole, preferred_element_type=jnp.float32).astype(
        jnp.bfloat16
    )
    keys_low = keys_low.reshape(seq_count, tok_count, features)
    values_low = values_low.reshape(seq_count, tok_count, features)
    tails = jnp.stack([keys_low[:, tok_count - WINDOW :], values_low[:, tok_count - WINDOW :]])
    rims = shifted(tails, "seq", 1)
    key_blocks = to_heads(blocks_with_rim(keys_low, rims[0], block_rows))
    value_blocks = to_heads(blocks_with_rim(values_low, rims[1], block_rows))
    query_blocks = to_heads(queries.reshape(seq_count, block_count, block_rows, features))
    allowed = window_allowed(block_count, block_rows, WINDOW, lax.axis_index("seq"))
    mixed, log_total = attend(query_blocks, key_blocks, value_blocks, allowed)
    mixed_low = mixed.reshape(all_rows, features).astype(jnp.bfloat16)
    resid = flat_in + jnp.dot(mixed_low, out_whole, preferred_element_type=jnp.float32)
    inverse_two = lax.rsqrt(jnp.mean(resid * resid, axis=-1, keepdims=True) + EPS)
    normed_two = resid * inverse_two
    gain_low_two, gate_whole, up_whole, down_view = (
        lax.all_gather(ffn_gain, ("seq", "batch"), axis=0, tiled=True),
        lax.all_gather(gate_weight, ("seq", "batch"), axis=0, tiled=True),
        lax.all_gather(up_weight, ("seq", "batch"), axis=0, tiled=True),
        lax.all_gather(
            down_weight.reshape(gate_weight.shape[0], -1), ("seq", "batch"), axis=0, tiled=True
        ),
    )
    inner_width = gate_whole.shape[1]
    down_whole = down_view.reshape(inner_width, features)
    gain_two = gain_low_two.astype(jnp.float32)
    act_two = (normed_two * gain_two).astype(jnp.bfloat16)
    gate = jnp.dot(act_two, gate_whole, preferred_element_type=jnp.float32)
    upward = jnp.dot(act_two, up_whole, preferred_element_type=jnp.float32)
    sigma = jax.nn.sigmoid(gate)
    hidden = (gate * sigma * upward).astype(jnp.bfloat16)
    ffn_out = jnp.dot(hidden, down_whole, preferred_element_type=jnp.float32)
    block_out = (resid + ffn_out).astype(jnp.bfloat16)
    d_hidden = lax.dot_general(d_ffn, down_whole, COLS_DIMS, preferred_element_type=jnp.float32)
    d_gate = (d_hidden * upward * sigma * (1.0 + gate * (1.0 - sigma))).astype(jnp.bfloat16)
    d_up = (d_hidden * gate * sigma).astype(jnp.bfloat16)
    d_gate_up = jnp.concatenate([d_gate, d_up], axis=1)
    d_act_two = lax.dot_general(d_gate, gate_whole, COLS_DIMS, preferred_element_type=jnp.float32)
    d_act_two = d_act_two + lax.dot_general(
        d_up, up_whole, COLS_DIMS, preferred_element_type=jnp.float32
    )
    front = lax.dot_general(act_two, d_gate_up, ROWS_DIMS, preferred_element_type=jnp.float32)
    back = lax.dot_general(hidden, d_ffn, ROWS_DIMS, preferred_element_type=jnp.float32)
    ffn_grad = lax.psum_scatter(
        jnp.concatenate(
            [
                front,
                back.reshape(gate_weight.shape[0] * lax.axis_size(("seq", "batch")), inner_width),
            ],
            axis=1,
        ),
        ("seq", "batch"),
        scatter_dimension=0,
        tiled=True,
    )
    gate_grad = ffn_grad[:, :inner_width]
    up_grad = ffn_grad[:, inner_width : 2 * inner_width]
    down_grad = ffn_grad[:, 2 * inner_width :].reshape(down_weight.shape)
    d_resid, ffn_gain_part = norm_back(d_act_two, gain_two, normed_two, inverse_two, d_final)
    d_attn = d_resid.astype(jnp.bfloat16)
    d_mixed = lax.dot_general(
        d_attn, out_whole, COLS_DIMS, preferred_element_type=jnp.float32
    ).astype(jnp.bfloat16)
    d_mixed_blocks = to_heads(d_mixed.reshape(seq_count, block_count, block_rows, features))
    d_query, d_key_blocks, d_value_blocks = attend_back(
        query_blocks, key_blocks, value_blocks, allowed, log_total, d_mixed_blocks
    )
    d_both = jnp.stack([d_key_blocks, d_value_blocks]).reshape(
        2, seq_count, block_count, block_rows + WINDOW, features
    )
    returned = shifted(d_both[:, :, 0, :WINDOW].astype(jnp.bfloat16), "seq", -1).astype(jnp.float32)
    d_owned = fold_rims(d_both, returned, block_rows)
    d_query_low = d_query.reshape(all_rows, features).astype(jnp.bfloat16)
    d_key_low = d_owned[0].reshape(all_rows, features).astype(jnp.bfloat16)
    d_value_low = d_owned[1].reshape(all_rows, features).astype(jnp.bfloat16)
    d_act_one = lax.dot_general(
        d_query_low, query_whole, COLS_DIMS, preferred_element_type=jnp.float32
    )
    d_act_one = d_act_one + lax.dot_general(
        d_key_low, key_whole, COLS_DIMS, preferred_element_type=jnp.float32
    )
    d_act_one = d_act_one + lax.dot_general(
        d_value_low, value_whole, COLS_DIMS, preferred_element_type=jnp.float32
    )
    d_qkv = jnp.concatenate([d_query_low, d_key_low, d_value_low], axis=1)
    left_part = lax.dot_general(act_one, d_qkv, ROWS_DIMS, preferred_element_type=jnp.float32)
    right_part = lax.dot_general(mixed_low, d_attn, ROWS_DIMS, preferred_element_type=jnp.float32)
    attn_grad = lax.psum_scatter(
        jnp.concatenate([left_part, right_part], axis=1),
        ("seq", "batch"),
        scatter_dimension=0,
        tiled=True,
    )
    query_grad = attn_grad[:, :features]
    key_grad = attn_grad[:, features : 2 * features]
    value_grad = attn_grad[:, 2 * features : 3 * features]
    out_grad = attn_grad[:, 3 * features :]
    tokens_grad, attn_gain_part = norm_back(d_act_one, gain_one, normed_one, inverse_one, d_resid)
    attn_gain_grad, ffn_gain_grad = (
        lax.psum_scatter(attn_gain_part, ("seq", "batch"), scatter_dimension=0, tiled=True),
        lax.psum_scatter(ffn_gain_part, ("seq", "batch"), scatter_dimension=0, tiled=True),
    )
    return (
        block_out.reshape(seq_count, tok_count, features),
        tokens_grad.reshape(seq_count, tok_count, features),
        attn_gain_grad,
        query_grad,
        key_grad,
        value_grad,
        out_grad,
        ffn_gain_grad,
        gate_grad,
        up_grad,
        down_grad,
    )


def solution(mesh):
    return jax.shard_map(
        per_device,
        mesh=mesh,
        in_specs=(
            P("batch", "seq", None),
            P("batch", "seq", None),
            P("batch", "seq"),
            P(("seq", "batch")),
            P(("seq", "batch"), None),
            P(("seq", "batch"), None),
            P(("seq", "batch"), None),
            P(("seq", "batch"), None),
            P(("seq", "batch")),
            P(("seq", "batch"), None),
            P(("seq", "batch"), None),
            P(("seq", "batch"), None),
        ),
        out_specs=(
            P("batch", "seq", None),
            P("batch", "seq", None),
            P(("seq", "batch")),
            P(("seq", "batch"), None),
            P(("seq", "batch"), None),
            P(("seq", "batch"), None),
            P(("seq", "batch"), None),
            P(("seq", "batch")),
            P(("seq", "batch"), None),
            P(("seq", "batch"), None),
            P(("seq", "batch"), None),
        ),
        check_vma=False,
    )
```

profile of v0, /device:TPU:0, one launch (start us, length us, event | category | flops | bytes accessed | tf_op | source)
XLA Modules:
  0.0 4376.2 jit_solution(14465990133946538995)
XLA Ops:
  14.3 42.2 psum.7
  57.0 41.2 all-reduce.7
  106.5 64.7 %all-gather.10.cloned.1.call-done = bf16[2048,2048]{1,0:T(8,128)(2,1)} async-done(((bf16[64,2048]{1,0:T(8,128)(2,1)}), bf16[2048,2048]{1,0:T(8,128)(2,1)}) %all-gather.10.cloned.1.call-update) | async-done | bytes 8388624 | tf_op jit(solution)/shard_map/all_gather | solution.py:136
  181.2 69.4 %all-gather.12.cloned.1.call-done = bf16[2048,2048]{1,0:T(8,128)(2,1)} async-done(((bf16[64,2048]{1,0:T(8,128)(2,1)}), bf16[2048,2048]{1,0:T(8,128)(2,1)}) %all-gather.12.cloned.1.call-update) | async-done | bytes 8388624 | tf_op jit(solution)/shard_map/all_gather | solution.py:134
  264.5 64.9 %all-gather.14.cloned.1.call-done = bf16[2048,2048]{1,0:T(8,128)(2,1)} async-done(((bf16[64,2048]{1,0:T(8,128)(2,1)}), bf16[2048,2048]{1,0:T(8,128)(2,1)}) %all-gather.14.cloned.1.call-update) | async-done | bytes 8388624 | tf_op jit(solution)/shard_map/all_gather | solution.py:137
  336.9 138.5 %all-gather.16.cloned.1.call-done = bf16[2048,5632]{1,0:T(8,128)(2,1)} async-done(((bf16[64,5632]{1,0:T(8,128)(2,1)}), bf16[2048,5632]{1,0:T(8,128)(2,1)}) %all-gather.16.cloned.1.call-update) | async-done | bytes 23068688 | tf_op jit(solution)/shard_map/all_gather | solution.py:161
  475.3 13.2 fusion.89
  488.5 132.3 %all-gather.18.cloned.1.call-done = bf16[2048,5632]{1,0:T(8,128)(2,1)} async-done(((bf16[64,5632]{1,0:T(8,128)(2,1)}), bf16[2048,5632]{1,0:T(8,128)(2,1)}) %all-gather.18.cloned.1.call-update) | async-done | bytes 23068688 | tf_op jit(solution)/shard_map/all_gather | solution.py:162
  620.8 13.3 fusion.90
  634.1 133.0 %all-gather.20.cloned.1.call-done = bf16[2048,5632]{1,0:T(8,128)(2,1)} async-done(((bf16[64,5632]{1,0:T(8,128)(2,1)}), bf16[2048,5632]{1,0:T(8,128)(2,1)}) %all-gather.20.cloned.1.call-update) | async-done | bytes 23068688 | tf_op jit(solution)/shard_map/all_gather | solution.py:163
  767.1 38.3 reshape.395
  805.4 25.0 multiply_convert_fusion
  832.0 18.2 fusion.52
  850.2 47.3 %reshape.399 = f32[2048,5632]{1,0:T(8,128)} reshape(f32[5632,2048]{1,0:T(8,128)} %fusion.52) | data formatting | bytes 92274688 | tf_op jit(solution)/shard_map/reshape | solution.py:191
  897.5 34.3 fusion
  931.8 89.0 %pad_maximum_fusion = f32[2048,16896]{1,0:T(8,128)} fusion(f32[2048,5632]{1,0:T(8,128)} %reshape.399, f32[2048,11264]{1,0:T(8,128)} %fusion), kind=kLoop, calls=%fused_computation | loop fusion | flops 34603008 | bytes 276824064 | tf_op jit(solution)/shard_map/concatenate | solution.py:188
  1024.3 14.3 fusion.91
  1038.7 14.0 multiply_reduce_fusion.1
  1105.7 23.9 fusion.7
  1129.6 45.1 %pad_maximum_fusion.1 = f32[2048,8192]{1,0:T(8,128)} fusion(f32[2048,2048]{1,0:T(8,128)} %fusion.54, f32[2048,6144]{1,0:T(8,128)} %fusion.7), kind=kLoop, calls=%fused_computation.1 | loop fusion | flops 16777216 | bytes 134217728 | tf_op jit(solution)/shard_map/concatenate | solution.py:232
  1181.1 13.0 fusion.19
  1204.1 42.8 all-reduce.6
  1251.6 1700.7 %all-reduce.10.cloned.1.call-done = f32[2048,16896]{1,0:T(8,128)} async-done(((f32[2048,16896]{1,0:T(8,128)}), f32[2048,16896]{1,0:T(8,128)}) %all-reduce.10.cloned.1.call-update) | async-done | bytes 138412048
  2958.4 1407.9 %reduce-scatter.2.cloned.1.call-done = f32[64,8192]{1,0:T(8,128)} async-done(((f32[2048,8192]{1,0:T(8,128)}), f32[64,8192]{1,0:T(8,128)}) %reduce-scatter.2.cloned.1.call-update) | async-done | bytes 2097168 | tf_op jit(solution)/shard_map/reduce_scatter | solution.py:231
  (202 shorter events, 134.6 us)
Async XLA Ops:
  7.2 49.3 %copy-start.47 = (bf16[64]{0:T(256)(128)(2,1)S(1)}, bf16[64]{0:T(256)(128)(2,1)}, u32[]{:S(2)}) copy-start(bf16[64]{0:T(256)(128)(2,1)} %param.15) | copy-start | bytes 388
  7.2 49.6 %copy-start.48 = (bf16[64]{0:T(256)(128)(2,1)S(1)}, bf16[64]{0:T(256)(128)(2,1)}, u32[]{:S(2)}) copy-start(bf16[64]{0:T(256)(128)(2,1)} %param.20) | copy-start | bytes 388
  7.2 91.2 %copy-start.4 = (bf16[1,256,2048]{2,1,0:T(8,128)(2,1)S(1)}, bf16[1,256,2048]{2,1,0:T(8,128)(2,1)}, u32[]{:S(2)}) copy-start(bf16[1,256,2048]{2,1,0:T(8,128)(2,1)} %param.12) | copy-start | bytes 3145732
  7.2 91.8 %all-gather.8.cloned.1.call-start = ((), (), s32[]{:S(2)}) async-start(), calls=%async_computation.1 | async-start | bytes 8650752 | tf_op jit(solution)/shard_map/all_gather | solution.py:135
  8.0 163.2 %all-gather.10.cloned.1.call-start = ((), (), s32[]{:S(2)}) async-start(), calls=%async_computation.2 | async-start | bytes 8650752 | tf_op jit(solution)/shard_map/all_gather | solution.py:136
  8.7 241.9 %all-gather.12.cloned.1.call-start = ((), (), s32[]{:S(2)}) async-start(), calls=%async_computation.3 | async-start | bytes 8650752 | tf_op jit(solution)/shard_map/all_gather | solution.py:134
  9.4 320.0 %all-gather.14.cloned.1.call-start = ((), (), s32[]{:S(2)}) async-start(), calls=%async_computation.4 | async-start | bytes 8650752 | tf_op jit(solution)/shard_map/all_gather | solution.py:137
  10.0 465.3 %all-gather.16.cloned.1.call-start = ((), (), s32[]{:S(2)}) async-start(), calls=%async_computation.5 | async-start | bytes 23789568 | tf_op jit(solution)/shard_map/all_gather | solution.py:161
  10.6 610.2 %all-gather.18.cloned.1.call-start = ((), (), s32[]{:S(2)}) async-start(), calls=%async_computation.6 | async-start | bytes 23789568 | tf_op jit(solution)/shard_map/all_gather | solution.py:162
  11.2 755.9 %all-gather.20.cloned.1.call-start = ((), (), s32[]{:S(2)}) async-start(), calls=%async_computation.7 | async-start | bytes 23789568 | tf_op jit(solution)/shard_map/all_gather | solution.py:163
  14.1 2938.2 %all-reduce.10.cloned.1.call-start = ((), (), s32[]{:S(2)}) async-start(), calls=%async_computation.9 | async-start | bytes 276824064
  98.3 152.4 %copy-start.30 = (f32[2048]{0:T(1024)}, f32[2048]{0:T(1024)S(1)}, u32[]{:S(2)}) copy-start(f32[2048]{0:T(1024)S(1)} %convert_element_type.134) | copy-start | bytes 24580
  98.3 237.1 %copy-start.34 = (f32[2048]{0:T(1024)}, f32[2048]{0:T(1024)S(1)}, u32[]{:S(2)}) copy-start(f32[2048]{0:T(1024)S(1)} %convert_element_type.144) | copy-start | bytes 24580
  98.7 151.9 %copy-start.36 = (f32[256]{0:T(256)}, f32[256]{0:T(256)S(1)}, u32[]{:S(2)}) copy-start(f32[256]{0:T(256)S(1)} %add_rsqrt_fusion.1) | copy-start | bytes 3076
  98.7 731.7 %copy-start.42 = (f32[256]{0:T(256)}, f32[256]{0:T(256)S(1)}, u32[]{:S(2)}) copy-start(f32[256]{0:T(256)S(1)} %multiply_divide_fusion) | copy-start | bytes 3076
  177.8 79.4 %collective-permute-start = (bf16[2,1,64,2048]{3,2,1,0:T(8,128)(2,1)}, bf16[2,1,64,2048]{3,2,1,0:T(8,128)(2,1)}, u32[]{:S(2)}, u32[]{:S(2)}) collective-permute-start(bf16[2,1,64,2048]{3,2,1,0:T(8,128)(2,1)} %pad_maximum_fusion.3), channel_id=1, source_target_pairs={{0,4},{4,8},{8,12},{12,16},{16,20},{20,24},{24,28},{1,5},{5,9},{9,... | collective-permute-start | bytes 1572872 | tf_op jit(solution)/shard_map/ppermute | solution.py:20
  264.5 70.8 %copy-start.20 = (bf16[1,2,128,16,128]{4,3,2,1,0:T(8,128)(2,1)}, bf16[1,2,128,16,128]{4,3,2,1,0:T(8,128)(2,1)S(1)}, u32[]{:S(2)}) copy-start(bf16[1,2,128,16,128]{4,3,2,1,0:T(8,128)(2,1)S(1)} %copy.86) | copy-start | bytes 3145732
  335.3 153.2 %copy-start.44 = (f32[256]{0:T(256)}, f32[256]{0:T(256)S(1)}, u32[]{:S(2)}) copy-start(f32[256]{0:T(256)S(1)} %add_rsqrt_fusion) | copy-start | bytes 3076
  634.1 171.3 %copy-start.16 = (bf16[1,256,2048]{2,1,0:T(8,128)(2,1)S(1)}, bf16[1,256,2048]{2,1,0:T(8,128)(2,1)}, u32[]{:S(2)}) copy-start(bf16[1,256,2048]{2,1,0:T(8,128)(2,1)} %param.13) | copy-start | bytes 3145732
  1020.8 3345.6 %reduce-scatter.2.cloned.1.call-start = ((), (), s32[]{:S(2)}) async-start(), calls=%async_computation.8 | async-start | bytes 69206016 | tf_op jit(solution)/shard_map/reduce_scatter | solution.py:231
  1024.3 14.3 copy-start.10
  1024.3 14.3 copy-start.35
  1076.8 12.8 collective-permute-start.1
  1174.7 19.4 slice-start
  (38 other events, 172.7 us)
Sparse Core Ops, SparseCore 0:
  11.0 81.0 all-gather.7
  95.0 76.0 all-gather.9
  174.1 76.5 all-gather.11
  253.4 75.9 all-gather.13
  332.1 143.1 all-gather.15
  478.0 142.7 all-gather.17
  624.2 142.7 all-gather.19
  1020.9 1931.3 all-reduce.9
  2954.7 1411.6 reduce-scatter.1
where the time goes:
time: 4380 us
  waiting for transfers between devices  3720 us (85%)
  matrix products  231 us (5%)
  other arithmetic  156 us (4%)
  local copies, waits for them, and re-layouts  128 us (3%)
  blocking collectives  126 us (3%)
    unnamed x10, waiting for transfers between devices  1700 us
    reduce_scatter x1, waiting for transfers between devices, per_device(): lax.psum_scatter(jnp.concatenate([left_part, right_part], axis=1), ('seq'...  1410 us
    all_gather x1, waiting for transfers between devices, per_device(): lax.all_gather(gate_weight, ('seq', 'batch'), axis=0, tiled=True)  138 us
    all_gather x1, waiting for transfers between devices, per_device(): lax.all_gather(down_weight.reshape(gate_weight.shape[0], -1), ('seq', 'ba...  133 us
    all_gather x1, waiting for transfers between devices, per_device(): lax.all_gather(up_weight, ('seq', 'batch'), axis=0, tiled=True)  132 us
    concatenate x1, other arithmetic, per_device(): jnp.concatenate([front, back.reshape(gate_weight.shape[0] * lax.axis_size...  89 us
  transfers between devices with their start and end apart: 11, of which 8 were waited for; matrix products, arithmetic and copies ran while one was open for 6% of the time, Pallas kernels for 0%

commit v1 on v0

v1 whole, which is shorter than its diff:
```python
import jax
import jax.numpy as jnp
from jax import lax
from jax.sharding import PartitionSpec as P

HEAD = 128
WINDOW = 64
GPS = 4
CORES = 2

EPS = 1e-05
NEGATIVE = -1e30
ROWS_DIMS = (((0,), (0,)), ((), ()))
COLS_DIMS = (((1,), (1,)), ((), ()))
BLOCK = 128
F32 = jnp.float32
LOW = jnp.bfloat16


def matmul(left, right):
    return jnp.dot(left, right, preferred_element_type=F32)


def matmul_rows(left, right):
    return lax.dot_general(left, right, ROWS_DIMS, preferred_element_type=F32)


def matmul_cols(left, right):
    return lax.dot_general(left, right, COLS_DIMS, preferred_element_type=F32)


def exchange(value, flip):
    count = lax.axis_size("seq")
    return lax.ppermute(value, "seq", [(place, place ^ flip) for place in range(count)])


def swap_core(value):
    return exchange(value, 1)


def chip_count():
    return lax.axis_size("seq") // CORES


def own_chip():
    return lax.axis_index("seq") // CORES


def own_core():
    return lax.axis_index("seq") % CORES


def chips_gather(value):
    return [value] + [exchange(value, CORES * k) for k in range(1, chip_count())]


def chips_scatter(blocks):
    return [blocks[0]] + [exchange(blocks[k], CORES * k) for k in range(1, chip_count())]


def in_order(blocks):
    chip = own_chip()
    bit = 1
    while bit < len(blocks):
        flipped = (chip & bit) > 0
        blocks = [jnp.where(flipped, blocks[i ^ bit], blocks[i]) for i in range(len(blocks))]
        bit *= 2
    return blocks


def to_chips(value):
    chip = own_chip()
    blocks = [
        lax.dynamic_index_in_dim(value, chip ^ k, axis=0, keepdims=False)
        for k in range(chip_count())
    ]
    return jnp.stack(in_order(chips_scatter(blocks)))


def to_own(values):
    rows = values.shape[:-1]
    parts = values.reshape(rows + (chip_count(), CORES, -1))
    flipped = own_core() > 0
    first, second = parts[..., 0, :], parts[..., 1, :]
    mine = jnp.where(flipped, second, first).reshape(rows + (-1,))
    other = jnp.where(flipped, first, second).reshape(rows + (-1,))
    return jnp.concatenate([mine, other], axis=-1)


def from_own(values):
    rows = values.shape[:-1]
    half = values.shape[-1] // CORES
    mine, other = values[..., :half], values[..., half:]
    flipped = own_core() > 0
    first = jnp.where(flipped, other, mine).reshape(rows + (chip_count(), 1, -1))
    second = jnp.where(flipped, mine, other).reshape(rows + (chip_count(), 1, -1))
    return jnp.concatenate([first, second], axis=-2).reshape(values.shape)


def core_rows(mine, other):
    flipped = own_core() > 0
    return jnp.concatenate(
        [jnp.where(flipped, other, mine), jnp.where(flipped, mine, other)], axis=0
    )


def core_reduce(first, second):
    flipped = own_core() > 0
    mine = jnp.where(flipped, second, first)
    other = jnp.where(flipped, first, second).astype(LOW)
    return mine + swap_core(other).astype(F32)


def batch_gather(value, axis):
    return lax.all_gather(value, "batch", axis=axis, tiled=True)


def batch_scatter(value, axis):
    return lax.psum_scatter(value, "batch", scatter_dimension=axis, tiled=True)


def to_heads(values):
    return values.reshape(values.shape[:-1] + (values.shape[-1] // HEAD, HEAD))


def blocks_with_rim(values, rim, block_rows):
    seq_count, tok_count, features = values.shape
    rim_rows = rim.shape[1]
    owned = values.reshape(seq_count, tok_count // block_rows, block_rows, features)
    before = jnp.concatenate([rim[:, None], owned[:, :-1, block_rows - rim_rows :]], axis=1)
    return jnp.concatenate([before, owned], axis=2)


def window_allowed(block_count, block_rows, rim_rows, preceded):
    query_place = jnp.arange(block_rows, dtype=jnp.int32)[:, None]
    key_place = jnp.arange(block_rows + rim_rows, dtype=jnp.int32)[None, :] - rim_rows
    distance = query_place - key_place
    inside = (distance >= 0) & (distance < rim_rows)
    block_index = jnp.arange(block_count, dtype=jnp.int32)[:, None, None]
    reach = (
        (block_index > 0)[None] | (key_place[None, None] >= 0) | preceded[:, None, None, None]
    )
    return inside[None, None] & reach


def window_scores(query_blocks, key_blocks, allowed):
    scores = jnp.einsum(
        "snqhe,snkhe->snhqk", query_blocks, key_blocks, preferred_element_type=F32
    ) * HEAD ** (-0.5)
    return jnp.where(allowed[:, :, None], scores, NEGATIVE)


def attend(query_blocks, key_blocks, value_blocks, allowed):
    scores = window_scores(query_blocks, key_blocks, allowed)
    top = jnp.max(scores, axis=-1, keepdims=True)
    expo = jnp.exp(scores - top)
    total = jnp.sum(expo, axis=-1, keepdims=True)
    probs_low = (expo / total).astype(LOW)
    mixed = jnp.einsum("snhqk,snkhe->snqhe", probs_low, value_blocks, preferred_element_type=F32)
    return (mixed, top + jnp.log(total))


def attend_back(query_blocks, key_blocks, value_blocks, allowed, log_total, d_mixed_blocks):
    probs = jnp.exp(window_scores(query_blocks, key_blocks, allowed) - log_total)
    probs_again = probs.astype(LOW)
    d_probs = jnp.einsum(
        "snqhe,snkhe->snhqk", d_mixed_blocks, value_blocks, preferred_element_type=F32
    )
    d_scores = (probs * (d_probs - jnp.sum(probs * d_probs, axis=-1, keepdims=True))).astype(LOW)
    factor = HEAD ** (-0.5)
    d_query = (
        jnp.einsum("snhqk,snkhe->snqhe", d_scores, key_blocks, preferred_element_type=F32) * factor
    )
    d_keys = (
        jnp.einsum("snhqk,snqhe->snkhe", d_scores, query_blocks, preferred_element_type=F32)
        * factor
    )
    d_values = jnp.einsum(
        "snhqk,snqhe->snkhe", probs_again, d_mixed_blocks, preferred_element_type=F32
    )
    return (d_query, d_keys, d_values)


def fold_rims(d_blocks, arrived, block_rows):
    later = jnp.concatenate([d_blocks[:, :, 1:, :WINDOW], arrived[:, :, None]], axis=2)
    padded = jnp.pad(later, ((0, 0), (0, 0), (0, 0), (block_rows - WINDOW, 0), (0, 0)))
    return d_blocks[:, :, :, WINDOW:] + padded


def norm_back(d_act, gain, normed, inverse, upstream):
    scaled = d_act * gain
    return upstream + inverse * (
        scaled - normed * jnp.mean(scaled * normed, axis=-1, keepdims=True)
    )


def rms(values):
    inverse = lax.rsqrt(jnp.mean(values * values, axis=-1, keepdims=True) + EPS)
    return inverse, values * inverse


def per_device(
    tokens,
    out_cotangent,
    group_ids,
    attn_gain,
    query_weight,
    key_weight,
    value_weight,
    out_weight,
    ffn_gain,
    gate_weight,
    up_weight,
    down_weight,
):
    tok_count, features = tokens.shape[1:]
    weight_rows, inner = gate_weight.shape
    chips = chip_count()
    chip, core = own_chip(), own_core()
    ids = lax.iota(jnp.int32, chips)
    head_width, inner_width = features // chips, inner // chips

    gains = jnp.concatenate(
        [
            jnp.broadcast_to(attn_gain[:, None], (weight_rows, HEAD // 2)),
            jnp.broadcast_to(ffn_gain[:, None], (weight_rows, HEAD // 2)),
        ],
        axis=1,
    )

    def by_chip(weight):
        return weight.reshape(weight_rows, chips, -1).transpose(1, 0, 2)

    qkv_rows = to_chips(
        jnp.concatenate(
            [by_chip(query_weight), by_chip(key_weight), by_chip(value_weight)]
            + [jnp.broadcast_to(gains, (chips,) + gains.shape)],
            axis=2,
        )
    )
    qkv_mine = batch_gather(qkv_rows, 1).reshape(features // CORES, -1)
    out_mine = batch_gather(out_weight, 0)
    inner_rows = to_chips(jnp.concatenate([by_chip(gate_weight), by_chip(up_weight)], axis=2))
    inner_mine = batch_gather(inner_rows, 1).reshape(features // CORES, -1)
    down_mine = batch_gather(down_weight, 0)

    qkv_whole = jnp.concatenate([qkv_mine, swap_core(qkv_mine)], axis=0)
    qkv_own = qkv_whole[:, : 3 * head_width]
    gain_one_own = qkv_whole[:, 3 * head_width].astype(F32)
    gain_two = from_own(qkv_whole[:, 3 * head_width + HEAD // 2].astype(F32))
    out_own = core_rows(out_mine, swap_core(out_mine))
    inner_own = jnp.concatenate([inner_mine, swap_core(inner_mine)], axis=0)
    down_own = core_rows(down_mine, swap_core(down_mine))

    group_span = GPS * lax.axis_size("batch")
    onehot = (group_ids[0, :, None] == jnp.arange(group_span, dtype=jnp.int32)[None, :]).astype(F32)
    group_total = lax.psum(jnp.sum(onehot, axis=0), "seq")
    own_total = jnp.sum(onehot * group_total, axis=-1)[:, None]
    weighting = tok_count * lax.axis_size("seq") / (GPS * own_total)
    d_final = out_cotangent[0].astype(F32) * weighting
    d_ffn = jnp.concatenate(chips_gather(d_final.astype(LOW)), axis=0)

    flat = tokens[0].astype(F32)
    inverse_one, normed_one = rms(flat)
    gathered = jnp.concatenate(chips_gather(to_own(tokens[0])), axis=0).astype(F32)
    _, normed_all = rms(gathered)
    act_one = (normed_all * gain_one_own).astype(LOW)
    qkv = matmul(act_one, qkv_own).astype(LOW).reshape(chips, tok_count, -1)
    queries, keys_low, values_low = (
        qkv[..., :head_width],
        qkv[..., head_width : 2 * head_width],
        qkv[..., 2 * head_width :],
    )
    place = chip ^ ids
    tails = swap_core(qkv[:, tok_count - WINDOW :, head_width:])
    before = jnp.where(core > 0, ids, chip ^ jnp.maximum(place - 1, 0))
    after = jnp.where(core > 0, chip ^ jnp.minimum(place + 1, chips - 1), ids)
    preceded = (core > 0) | (place > 0)
    followed = (core == 0) | (place < chips - 1)
    rims = jnp.take(tails, before, axis=0)
    key_blocks = to_heads(blocks_with_rim(keys_low, rims[..., :head_width], BLOCK))
    value_blocks = to_heads(blocks_with_rim(values_low, rims[..., head_width:], BLOCK))
    block_count = tok_count // BLOCK
    query_blocks = to_heads(queries.reshape(chips, block_count, BLOCK, head_width))
    allowed = window_allowed(block_count, BLOCK, WINDOW, preceded)
    mixed, log_total = attend(query_blocks, key_blocks, value_blocks, allowed)
    mixed_low = mixed.reshape(chips * tok_count, head_width).astype(LOW)

    def chips_sum(parts):
        parts = parts.reshape(chips, tok_count, -1)
        arrived = chips_scatter([parts[0]] + [parts[k].astype(LOW) for k in range(1, chips)])
        return sum(part.astype(F32) for part in arrived)

    resid = flat + chips_sum(matmul(mixed_low, out_own))

    inverse_two, normed_two = rms(resid)
    act_two_own = (normed_two * gain_two).astype(LOW)
    act_two = jnp.concatenate(chips_gather(to_own(act_two_own)), axis=0)
    gate_up = matmul(act_two, inner_own)
    gate, upward = gate_up[:, :inner_width], gate_up[:, inner_width:]
    sigma = jax.nn.sigmoid(gate)
    hidden = (gate * sigma * upward).astype(LOW)
    d_hidden = matmul_cols(d_ffn, down_own)
    d_gate = (d_hidden * upward * sigma * (1.0 + gate * (1.0 - sigma))).astype(LOW)
    d_up = (d_hidden * gate * sigma).astype(LOW)
    d_gate_up = jnp.concatenate([d_gate, d_up], axis=1)
    d_act_two = from_own(chips_sum(matmul_cols(d_gate_up, inner_own)))
    d_resid = norm_back(d_act_two, gain_two, normed_two, inverse_two, d_final)
    gain_two_part = to_own(jnp.sum(d_act_two * normed_two, axis=0))
    block_out = (resid + chips_sum(matmul(hidden, down_own))).astype(LOW)

    down_part = matmul_rows(hidden, d_ffn)
    down_half = inner_width // CORES
    down_sum = core_reduce(down_part[:down_half], down_part[down_half:])
    down_grad = batch_scatter(down_sum.astype(LOW), 0).astype(F32)

    def own_reduce(part):
        half = features // CORES
        summed = part[:half] + swap_core(part[half:].astype(LOW)).astype(F32)
        return batch_scatter(summed.astype(LOW).reshape(chips, half // chips, -1), 1)

    inner_grad = to_chips(own_reduce(matmul_rows(act_two, d_gate_up))).astype(F32)
    gate_grad = inner_grad[..., :inner_width].transpose(1, 0, 2).reshape(weight_rows, inner)
    up_grad = inner_grad[..., inner_width:].transpose(1, 0, 2).reshape(weight_rows, inner)

    d_attn = jnp.concatenate(chips_gather(d_resid.astype(LOW)), axis=0)
    d_mixed = matmul_cols(d_attn, out_own).astype(LOW)
    d_mixed_blocks = to_heads(d_mixed.reshape(chips, block_count, BLOCK, head_width))
    d_query, d_key_blocks, d_value_blocks = attend_back(
        query_blocks, key_blocks, value_blocks, allowed, log_total, d_mixed_blocks
    )
    d_both = jnp.stack([d_key_blocks, d_value_blocks]).reshape(
        2, chips, block_count, BLOCK + WINDOW, head_width
    )
    lent = swap_core(d_both[:, :, 0, :WINDOW].astype(LOW))
    returned = jnp.where(
        followed[None, :, None, None], jnp.take(lent, after, axis=1).astype(F32), 0.0
    )
    d_owned = fold_rims(d_both, returned, BLOCK).reshape(2, chips * tok_count, head_width)
    d_qkv = jnp.concatenate(
        [d_query.reshape(chips * tok_count, head_width), d_owned[0], d_owned[1]], axis=1
    ).astype(LOW)
    d_act_one = matmul_cols(d_qkv, qkv_own)
    gain_one_part = jnp.sum(d_act_one * normed_all, axis=0)
    tokens_grad = norm_back(
        from_own(chips_sum(d_act_one)), from_own(gain_one_own), normed_one, inverse_one, d_resid
    )
    gain_parts = jnp.concatenate(
        [
            jnp.broadcast_to(gain_one_part[:, None], (features, HEAD // 2)),
            jnp.broadcast_to(gain_two_part[:, None], (features, HEAD // 2)),
        ],
        axis=1,
    )
    qkv_grad = to_chips(
        own_reduce(jnp.concatenate([matmul_rows(act_one, d_qkv), gain_parts], axis=1))
    ).astype(F32)

    def whole_columns(first):
        part = qkv_grad[..., first : first + head_width]
        return part.transpose(1, 0, 2).reshape(weight_rows, features)

    gain_grads = jnp.sum(qkv_grad[..., 3 * head_width :], axis=0)
    out_part = matmul_rows(mixed_low, d_attn)
    out_half = head_width // CORES
    out_sum = core_reduce(out_part[:out_half], out_part[out_half:])
    out_grad = batch_scatter(out_sum.astype(LOW), 0).astype(F32)

    return (
        block_out[None],
        tokens_grad[None],
        gain_grads[:, 0],
        whole_columns(0),
        whole_columns(head_width),
        whole_columns(2 * head_width),
        out_grad,
        gain_grads[:, HEAD // 2],
        gate_grad,
        up_grad,
        down_grad,
    )


def solution(mesh):
    rows = P(("seq", "batch"), None)
    vector = P(("seq", "batch"))
    cells = P("batch", "seq", None)
    return jax.shard_map(
        per_device,
        mesh=mesh,
        in_specs=(cells, cells, P("batch", "seq"))
        + (vector, rows, rows, rows, rows, vector, rows, rows, rows),
        out_specs=(cells, cells, vector, rows, rows, rows, rows, vector, rows, rows, rows),
        check_vma=False,
    )
```

time: 4380 us -> 1000 us (0.23)
  waiting for transfers between devices: 3720 us -> 457 us
  blocking collectives: 126 us -> 54.8 us
  matrix products: 231 us -> 161 us
  starting transfers between devices: 5.09 us -> 62.6 us
  other arithmetic: 156 us -> 109 us
    unnamed x10 -> x8, waiting for transfers between devices: 1700 us -> 1.47 us
    reduce_scatter x1 -> x4, waiting for transfers between devices: 1410 us -> 74.6 us  [batch_scatter(): return lax.psum_scatter(value, 'batch', scatter_dimension=axis, tiled=True)]
    all_gather x7 -> x4, waiting for transfers between devices: 603 us -> 128 us  [batch_gather(): return lax.all_gather(value, 'batch', axis=axis, tiled=True)]
    ppermute x2 -> x46, waiting for transfers between devices: 0.01 us -> 253 us  [exchange(): lax.ppermute(value, 'seq', [(place, place ^ flip) for place in range(coun...]
    concatenate x4 -> x11, other arithmetic: 135 us -> 20.1 us  [the longest x4 8.19 us: from_own(): return jnp.concatenate([first, second], axis=-2).reshape(values.shape)]
    unnamed x2 -> x0, blocking collectives: 84 us -> none
    dot_general x18 -> x12, matrix products: 224 us -> 151 us  [the longest x4 56.1 us: matmul_cols(): return lax.dot_general(left, right, COLS_DIMS, preferred_element_type=F32)]
    ppermute x2 -> x46, starting transfers between devices: 4.74 us -> 61.9 us  [exchange(): lax.ppermute(value, 'seq', [(place, place ^ flip) for place in range(coun...]
  transfers between devices with their start and end apart: 11 -> 54, of which waited for: 8 -> 29; matrix products, arithmetic and copies ran while one was open for 6% -> 33% of each run, Pallas kernels for 0% -> 0%
where the time goes in v1:
time: 1000 us; the launch traced here: 993 us
  waiting for transfers between devices  457 us (46%)
  matrix products  161 us (16%)
  local copies, waits for them, and re-layouts  132 us (13%)
  other arithmetic  109 us (11%)
  starting transfers between devices  62.6 us (6%)
  blocking collectives  54.8 us (5%)
  between operations  16 us (2%)
    ppermute x46, waiting for transfers between devices, exchange(): lax.ppermute(value, 'seq', [(place, place ^ flip) for place in range(coun...  253 us
    all_gather x4, waiting for transfers between devices, batch_gather(): return lax.all_gather(value, 'batch', axis=axis, tiled=True)  128 us
    reduce_scatter x4, waiting for transfers between devices, batch_scatter(): return lax.psum_scatter(value, 'batch', scatter_dimension=axis, tiled=True)  74.6 us
    ppermute x46, starting transfers between devices, exchange(): lax.ppermute(value, 'seq', [(place, place ^ flip) for place in range(coun...  61.9 us
    dot_general x4, matrix products, matmul_cols(): return lax.dot_general(left, right, COLS_DIMS, preferred_element_type=F32)  56.1 us
    psum x1, blocking collectives, per_device(): group_total = lax.psum(jnp.sum(onehot, axis=0), 'seq')  54.8 us
    dot_general x4, matrix products, matmul(): return jnp.dot(left, right, preferred_element_type=F32)  48.1 us
    dot_general x4, matrix products, matmul_rows(): return lax.dot_general(left, right, ROWS_DIMS, preferred_element_type=F32)  46.7 us
  transfers between devices with their start and end apart: 54, of which 29 were waited for; matrix products, arithmetic and copies ran while one was open for 33% of the time, Pallas kernels for 0%

profile of v1, /device:TPU:0, one launch (start us, length us, event | category | flops | bytes accessed | tf_op | source)
XLA Modules:
  0.0 993.2 jit_solution(12137236622815716125)
XLA Ops:
  58.0 40.2 %all-gather.5.cloned.1.call-done = bf16[4,256,1664]{2,1,0:T(8,128)(2,1)} async-done(((bf16[4,64,1664]{2,1,0:T(8,128)(2,1)}), bf16[4,256,1664]{2,1,0:T(8,128)(2,1)}) %all-gather.5.cloned.1.call-update) | async-done | bytes 3407888 | tf_op jit(solution)/shard_map/all_gather | solution.py:115
  108.6 54.8 %psum.7 = f32[16]{0:T(128)S(1)} all-reduce(f32[16]{0:T(128)S(1)} %convert_reduce_fusion.1), channel_id=1, replica_groups=mesh['seq'=8,'batch'=4] {'seq'}, use_global_device_ids=true, to_apply=%region_5.6 | all-reduce | flops 16 | bytes 128 | tf_op jit(solution)/shard_map/psum | solution.py:257
  173.7 13.1 %all-gather.11.cloned.1.call-done = bf16[704,2048]{1,0:T(8,128)(2,1)} async-done(((bf16[176,2048]{1,0:T(8,128)(2,1)}), bf16[704,2048]{1,0:T(8,128)(2,1)}) %all-gather.11.cloned.1.call-update) | async-done | bytes 2883600 | tf_op jit(solution)/shard_map/all_gather | solution.py:115
  188.8 11.0 %convolution_convert_fusion = bf16[1024,1536]{1,0:T(8,128)(2,1)} fusion(f32[2048]{0:T(1024)S(1)} %bitcast.285, f32[1024]{0:T(1024)S(1)} %add_rsqrt_fusion, bf16[1024,1664]{0,1:T(8,128)(2,1)S(1)} %copy-done.7, bf16[1024,1664]{0,1:T(8,128)(2,1)} %collective-permute-done.6, bf16[256,2048]{1,0:T(8,128)(2,1)S(1)} %collective-permute-done.2, ...), kind=kOutput, calls=%fused_computation.38 | convolution fusion | flops 6483869696 | bytes 14168064 | tf_op jit(solution)/shard_map/dot_general | solution.py:21
  219.8 74.4 %all-gather.9.cloned.1.call-done = bf16[4,256,2816]{2,1,0:T(8,128)(2,1)} async-done(((bf16[4,64,2816]{2,1,0:T(8,128)(2,1)}), bf16[4,256,2816]{2,1,0:T(8,128)(2,1)}) %all-gather.9.cloned.1.call-update) | async-done | bytes 5767184 | tf_op jit(solution)/shard_map/all_gather | solution.py:115
  319.5 20.8 %collective-permute-done.9 = bf16[256,2048]{1,0:T(8,128)(2,1)S(1)} collective-permute-done((bf16[256,2048]{1,0:T(8,128)(2,1)}, bf16[256,2048]{1,0:T(8,128)(2,1)S(1)}, u32[]{:S(2)}, u32[]{:S(2)}) %collective-permute-start.9) | collective-permute-done | bytes 1048608 | tf_op jit(solution)/shard_map/ppermute | solution.py:34
  340.3 23.0 %collective-permute-done.11 = bf16[256,2048]{1,0:T(8,128)(2,1)S(1)} collective-permute-done((bf16[256,2048]{1,0:T(8,128)(2,1)}, bf16[256,2048]{1,0:T(8,128)(2,1)S(1)}, u32[]{:S(2)}, u32[]{:S(2)}) %collective-permute-start.11) | collective-permute-done | bytes 1048608 | tf_op jit(solution)/shard_map/ppermute | solution.py:34
  382.0 16.8 %collective-permute-done.14 = bf16[256,2048]{0,1:T(8,128)(2,1)S(1)} collective-permute-done((bf16[256,2048]{0,1:T(8,128)(2,1)S(1)}, bf16[256,2048]{0,1:T(8,128)(2,1)S(1)}, u32[]{:S(2)}, u32[]{:S(2)}) %collective-permute-start.14) | collective-permute-done | bytes 1048608 | tf_op jit(solution)/shard_map/ppermute | solution.py:34
  399.4 22.0 %collective-permute-done.13 = bf16[256,2048]{0,1:T(8,128)(2,1)S(1)} collective-permute-done((bf16[256,2048]{0,1:T(8,128)(2,1)S(1)}, bf16[256,2048]{0,1:T(8,128)(2,1)S(1)}, u32[]{:S(2)}, u32[]{:S(2)}) %collective-permute-start.13) | collective-permute-done | bytes 1048608 | tf_op jit(solution)/shard_map/ppermute | solution.py:34
  421.4 20.3 %collective-permute-start.23 = (bf16[256,2048]{1,0:T(8,128)(2,1)S(1)}, bf16[256,2048]{1,0:T(8,128)(2,1)}, u32[]{:S(2)}, u32[]{:S(2)}) collective-permute-start(bf16[256,2048]{1,0:T(8,128)(2,1)S(1)} %copy-done.43), channel_id=1, source_target_pairs={{0,8},{4,12},{8,0},{12,4},{16,24},{20,28},{24,16},{28,20},{1,9},{5... | collective-permute-start | bytes 3145736 | tf_op jit(solution)/shard_map/ppermute | solution.py:34
  442.6 19.7 %fusion.7 = f32[1024,2816]{1,0:T(8,128)} fusion(bf16[1024,2816]{1,0:T(8,128)(2,1)} %collective-permute-done.18, bf16[1024,2816]{1,0:T(8,128)(2,1)} %bitcast.294, bf16[256,2048]{0,1:T(8,128)(2,1)} %copy-done.64, bf16[256,2048]{0,1:T(8,128)(2,1)} %copy-done.65, bf16[256,2048]{0,1:T(8,128)(2,1)} %copy-done.66, bf16[256,1024]{0,1:T(8,128)(2,1)S(1)} %bitcast.253, ...), kind=kOutput, calls=%fused_computation.15 | convolution fusion | flops 11855200256 | bytes 27262976 | tf_op jit(solution)/shard_map/dot_general | solution.py:21
  464.4 17.1 %multiply_convert_fusion.1 = (bf16[1024,1408]{1,0:T(8,128)(2,1)}, bf16[1024,1408]{1,0:T(8,128)(2,1)}, bf16[1024,1408]{1,0:T(8,128)(2,1)}) fusion(f32[1024,2816]{1,0:T(8,128)} %fusion.7, bf16[704,2048]{1,0:T(8,128)(2,1)} %get-tuple-element.39, bf16[704,2048]{1,0:T(8,128)(2,1)} %get-tuple-element.38, bf16[256,2048]{1,0:T(8,128)(2,1)} %collective-permute-done.25, ...), kind=kOutput, calls=%fused_computation.27 | convolution fusion | flops 5956960256 | bytes 30146560 | tf_op jit(solution)/shard_map/dot_general | solution.py:29
  481.5 19.6 %fusion.107 = (bf16[1024,2048]{1,0:T(8,128)(2,1)}, f32[1024,2048]{1,0:T(8,128)}) fusion(bf16[1024,2816]{1,0:T(8,128)(2,1)} %collective-permute-done.18, bf16[1024,2816]{1,0:T(8,128)(2,1)} %bitcast.295, bf16[1024,1408]{1,0:T(8,128)(2,1)} %get-tuple-element.32, bf16[1024,1408]{1,0:T(8,128)(2,1)} %get-tuple-element.31), kind=kOutput, calls=%fused_computation.297 | convolution fusion | flops 11847860224 | bytes 29884416 | tf_op jit(solution)/shard_map/dot_general | solution.py:29
  506.9 10.5 %fusion.108 = (bf16[1024,2048]{1,0:T(8,128)(2,1)S(1)}, f32[1024,2048]{1,0:T(8,128)}) fusion(bf16[1024,1408]{1,0:T(8,128)(2,1)} %get-tuple-element.33, bf16[704,2048]{1,0:T(8,128)(2,1)S(1)} %copy-done.31, bf16[704,2048]{1,0:T(8,128)(2,1)S(1)} %copy-done.30), kind=kOutput, calls=%fused_computation.298 | convolution fusion | flops 5919211520 | bytes 21233664 | tf_op jit(solution)/shard_map/dot_general | solution.py:21
  530.1 22.0 %collective-permute-done.28 = bf16[256,2048]{1,0:T(8,128)(2,1)S(1)} collective-permute-done((bf16[256,2048]{1,0:T(8,128)(2,1)S(1)}, bf16[256,2048]{1,0:T(8,128)(2,1)S(1)}, u32[]{:S(2)}, u32[]{:S(2)}) %collective-permute-start.28) | collective-permute-done | bytes 1048608 | tf_op jit(solution)/shard_map/ppermute | solution.py:34
  574.5 21.6 %collective-permute-done.22 = bf16[256,2048]{1,0:T(8,128)(2,1)} collective-permute-done((bf16[256,2048]{1,0:T(8,128)(2,1)}, bf16[256,2048]{1,0:T(8,128)(2,1)}, u32[]{:S(2)}, u32[]{:S(2)}) %collective-permute-start.22) | collective-permute-done | bytes 1048608 | tf_op jit(solution)/shard_map/ppermute | solution.py:34
  630.3 20.2 %collective-permute-done.30 = bf16[256,2048]{1,0:T(8,128)(2,1)} collective-permute-done((bf16[256,2048]{1,0:T(8,128)(2,1)}, bf16[256,2048]{1,0:T(8,128)(2,1)}, u32[]{:S(2)}, u32[]{:S(2)}) %collective-permute-start.30) | collective-permute-done | bytes 1048608 | tf_op jit(solution)/shard_map/ppermute | solution.py:34
  708.4 13.3 %fusion.4 = (f32[2048]{0:T(1024)S(1)}, bf16[1024,2048]{1,0:T(8,128)(2,1)}, f32[1024,2048]{1,0:T(8,128)}) fusion(f32[1024]{0:T(1024)S(1)} %copy-done.60, bf16[256,2048]{1,0:T(8,128)(2,1)} %copy-done.36, bf16[256,2048]{1,0:T(8,128)(2,1)} %collective-permute-done.1, bf16[256,2048]{1,0:T(8,128)(2,1)} %collective-permute-done, bf16[256,1024]{1,0:T(8,128)(2,1)} %copy-done.20, ...), kind=kOutput, calls=%fused_computation.12 | convolution fusion | flops 6493829120 | bytes 26750976 | tf_op jit(solution)/shard_map/dot_general | solution.py:29
  730.7 10.4 %fusion.47 = f32[2048,1536]{0,1:T(8,128)S(1)} fusion(bf16[1024,512]{1,0:T(8,128)(2,1)} %bitcast.262, bf16[1024,512]{1,0:T(8,128)(2,1)} %bitcast.260, bf16[1024,512]{1,0:T(8,128)(2,1)} %bitcast.258, f32[2048]{0:T(1024)S(1)} %bitcast.286, f32[1024]{0:T(1024)S(1)} %copy-done.60, bf16[256,2048]{1,0:T(8,128)(2,1)S(1)} %copy-done.37, ...), kind=kOutput, calls=%fused_computation.116 | convolution fusion | flops 6479151104 | bytes 19935232 | tf_op jit(solution)/shard_map/dot_general | solution.py:25
  753.4 22.7 %fusion.12 = f32[2048,2816]{1,0:T(8,128)} fusion(bf16[1024,1408]{1,0:T(8,128)(2,1)} %get-tuple-element.32, bf16[1024,1408]{1,0:T(8,128)(2,1)} %get-tuple-element.31, bf16[256,2048]{0,1:T(8,128)(2,1)} %copy-done.64, bf16[256,2048]{0,1:T(8,128)(2,1)} %copy-done.65, bf16[256,2048]{0,1:T(8,128)(2,1)} %copy-done.66, bf16[256,1024]{0,1:T(8,128)(2,1)S(1)} %bitcast.254, ...), kind=kOutput, calls=%fused_computation.39 | convolution fusion | flops 11843665920 | bytes 33030144 | tf_op jit(solution)/shard_map/dot_general | solution.py:25
  793.2 10.3 %fusion = bf16[1024,2816]{1,0:T(8,128)(2,1)} fusion(f32[2048,2816]{1,0:T(8,128)} %fusion.12, bf16[1024,2816]{1,0:T(8,128)(2,1)} %collective-permute-done.41), kind=kLoop, calls=%fused_computation.5 | loop fusion | flops 8650752 | bytes 23068672 | tf_op jit(solution)/shard_map/convert_element_type | solution.py:320
  810.8 22.6 %collective-permute-done.33 = bf16[256,2048]{1,0:T(8,128)(2,1)S(1)} collective-permute-done((bf16[256,2048]{1,0:T(8,128)(2,1)}, bf16[256,2048]{1,0:T(8,128)(2,1)S(1)}, u32[]{:S(2)}, u32[]{:S(2)}) %collective-permute-start.33) | collective-permute-done | bytes 1048608 | tf_op jit(solution)/shard_map/ppermute | solution.py:34
  833.4 21.1 %collective-permute-done.35 = bf16[256,2048]{1,0:T(8,128)(2,1)S(1)} collective-permute-done((bf16[256,2048]{1,0:T(8,128)(2,1)}, bf16[256,2048]{1,0:T(8,128)(2,1)S(1)}, u32[]{:S(2)}, u32[]{:S(2)}) %collective-permute-start.35) | collective-permute-done | bytes 1048608 | tf_op jit(solution)/shard_map/ppermute | solution.py:34
  886.8 74.6 %reduce-scatter.9.cloned.1.call-done = bf16[4,64,2816]{2,1,0:T(8,128)(2,1)} async-done(((bf16[4,256,2816]{2,1,0:T(8,128)(2,1)}), bf16[4,64,2816]{2,1,0:T(8,128)(2,1)}) %reduce-scatter.9.cloned.1.call-update) | async-done | bytes 1441808 | tf_op jit(solution)/shard_map/reduce_scatter | solution.py:119
  (415 shorter events, 375.0 us)
Async XLA Ops:
  7.2 91.1 %all-gather.5.cloned.1.call-start = ((), (), s32[]{:S(2)}) async-start(), calls=%async_computation.4 | async-start | bytes 4259840 | tf_op jit(solution)/shard_map/all_gather | solution.py:115
  29.8 134.0 %all-gather.7.cloned.1.call-start = ((), (), s32[]{:S(2)}) async-start(), calls=%async_computation.5 | async-start | bytes 1310720 | tf_op jit(solution)/shard_map/all_gather | solution.py:115
  30.5 156.2 %all-gather.11.cloned.1.call-start = ((), (), s32[]{:S(2)}) async-start(), calls=%async_computation.7 | async-start | bytes 3604480 | tf_op jit(solution)/shard_map/all_gather | solution.py:115
  31.3 262.9 %all-gather.9.cloned.1.call-start = ((), (), s32[]{:S(2)}) async-start(), calls=%async_computation.6 | async-start | bytes 7208960 | tf_op jit(solution)/shard_map/all_gather | solution.py:115
  56.9 821.0 %reduce-scatter.7.cloned.1.call-start = ((), (), s32[]{:S(2)}) async-start(), calls=%async_computation.9 | async-start | bytes 1310720 | tf_op jit(solution)/shard_map/reduce_scatter | solution.py:119
  103.9 82.9 %collective-permute-start.6 = (bf16[1024,1664]{0,1:T(8,128)(2,1)}, bf16[1024,1664]{0,1:T(8,128)(2,1)}, u32[]{:S(2)}, u32[]{:S(2)}) collective-permute-start(bf16[1024,1664]{0,1:T(8,128)(2,1)} %copy.191), channel_id=1, source_target_pairs={{0,4},{4,0},{8,12},{12,8},{16,20},{20,16},{24,28},{28,24},{1,5},{5... | collective-permute-start | bytes 10223624 | tf_op jit(solution)/shard_map/ppermute | solution.py:34
  104.9 60.0 %collective-permute-start.2 = (bf16[256,2048]{1,0:T(8,128)(2,1)}, bf16[256,2048]{1,0:T(8,128)(2,1)S(1)}, u32[]{:S(2)}, u32[]{:S(2)}) collective-permute-start(bf16[256,2048]{1,0:T(8,128)(2,1)} %pad_maximum_fusion.25), channel_id=1, source_target_pairs={{0,24},{4,28},{8,16},{12,20},{16,8},{20,12},{24,0},{28,4},{1,25},{... | collective-permute-start | bytes 3145736 | tf_op jit(solution)/shard_map/ppermute | solution.py:34
  107.3 57.6 %collective-permute-start.1 = (bf16[256,2048]{1,0:T(8,128)(2,1)}, bf16[256,2048]{1,0:T(8,128)(2,1)}, u32[]{:S(2)}, u32[]{:S(2)}) collective-permute-start(bf16[256,2048]{1,0:T(8,128)(2,1)} %pad_maximum_fusion.25), channel_id=1, source_target_pairs={{0,16},{4,20},{8,24},{12,28},{16,0},{20,4},{24,8},{28,12},{1,17},{... | collective-permute-start | bytes 3145736 | tf_op jit(solution)/shard_map/ppermute | solution.py:34
  108.0 56.9 %collective-permute-start = (bf16[256,2048]{1,0:T(8,128)(2,1)}, bf16[256,2048]{1,0:T(8,128)(2,1)}, u32[]{:S(2)}, u32[]{:S(2)}) collective-permute-start(bf16[256,2048]{1,0:T(8,128)(2,1)} %pad_maximum_fusion.25), channel_id=1, source_target_pairs={{0,8},{4,12},{8,0},{12,4},{16,24},{20,28},{24,16},{28,20},{1,9},{5... | collective-permute-start | bytes 3145736 | tf_op jit(solution)/shard_map/ppermute | solution.py:34
  186.8 189.1 %collective-permute-start.19 = (bf16[704,2048]{1,0:T(8,128)(2,1)}, bf16[704,2048]{1,0:T(8,128)(2,1)}, u32[]{:S(2)}, u32[]{:S(2)}) collective-permute-start(bf16[704,2048]{1,0:T(8,128)(2,1)} %all-gather.11.cloned.1.call-done), channel_id=1, source_target_pairs={{0,4},{4,0},{8,12},{12,8},{16,20},{20,16},{24,28},{28,24},{1,5},{5... | collective-permute-start | bytes 8650760 | tf_op jit(solution)/shard_map/ppermute | solution.py:34
  201.6 92.6 %collective-permute-start.7 = (bf16[4,64,1024]{2,1,0:T(8,128)(2,1)}, bf16[4,64,1024]{2,1,0:T(8,128)(2,1)}, u32[]{:S(2)}, u32[]{:S(2)}) collective-permute-start(bf16[4,64,1024]{2,1,0:T(8,128)(2,1)} %slice.327), channel_id=1, source_target_pairs={{0,4},{4,0},{8,12},{12,8},{16,20},{20,16},{24,28},{28,24},{1,5},{5... | collective-permute-start | bytes 1572872 | tf_op jit(solution)/shard_map/ppermute | solution.py:34
  294.2 148.4 %collective-permute-start.18 = (bf16[1024,2816]{1,0:T(8,128)(2,1)}, bf16[1024,2816]{1,0:T(8,128)(2,1)}, u32[]{:S(2)}, u32[]{:S(2)}) collective-permute-start(bf16[1024,2816]{1,0:T(8,128)(2,1)} %bitcast.293), channel_id=1, source_target_pairs={{0,4},{4,0},{8,12},{12,8},{16,20},{20,16},{24,28},{28,24},{1,5},{5... | collective-permute-start | bytes 17301512 | tf_op jit(solution)/shard_map/ppermute | solution.py:34
  374.7 66.9 %collective-permute-start.12 = (bf16[256,2048]{0,1:T(8,128)(2,1)S(1)}, bf16[256,2048]{0,1:T(8,128)(2,1)S(1)}, u32[]{:S(2)}, u32[]{:S(2)}) collective-permute-start(bf16[256,2048]{0,1:T(8,128)(2,1)S(1)} %pad_maximum_fusion.26), channel_id=1, source_target_pairs={{0,8},{4,12},{8,0},{12,4},{16,24},{20,28},{24,16},{28,20},{1,9},{5... | collective-permute-start | bytes 3145736 | tf_op jit(solution)/shard_map/ppermute | solution.py:34
  375.8 86.5 %collective-permute-start.25 = (bf16[256,2048]{1,0:T(8,128)(2,1)S(1)}, bf16[256,2048]{1,0:T(8,128)(2,1)}, u32[]{:S(2)}, u32[]{:S(2)}) collective-permute-start(bf16[256,2048]{1,0:T(8,128)(2,1)S(1)} %copy-done.43), channel_id=1, source_target_pairs={{0,24},{4,28},{8,16},{12,20},{16,8},{20,12},{24,0},{28,4},{1,25},{... | collective-permute-start | bytes 3145736 | tf_op jit(solution)/shard_map/ppermute | solution.py:34
  398.8 65.6 %collective-permute-start.24 = (bf16[256,2048]{1,0:T(8,128)(2,1)S(1)}, bf16[256,2048]{1,0:T(8,128)(2,1)}, u32[]{:S(2)}, u32[]{:S(2)}) collective-permute-start(bf16[256,2048]{1,0:T(8,128)(2,1)S(1)} %copy-done.43), channel_id=1, source_target_pairs={{0,16},{4,20},{8,24},{12,28},{16,0},{20,4},{24,8},{28,12},{1,17},{... | collective-permute-start | bytes 3145736 | tf_op jit(solution)/shard_map/ppermute | solution.py:34
  520.0 76.1 %collective-permute-start.22 = (bf16[256,2048]{1,0:T(8,128)(2,1)}, bf16[256,2048]{1,0:T(8,128)(2,1)}, u32[]{:S(2)}, u32[]{:S(2)}) collective-permute-start(bf16[256,2048]{1,0:T(8,128)(2,1)} %get-tuple-element.47), channel_id=1, source_target_pairs={{0,24},{4,28},{8,16},{12,20},{16,8},{20,12},{24,0},{28,4},{1,25},{... | collective-permute-start | bytes 3145736 | tf_op jit(solution)/shard_map/ppermute | solution.py:34
  529.4 68.0 %collective-permute-start.21 = (bf16[256,2048]{1,0:T(8,128)(2,1)}, bf16[256,2048]{1,0:T(8,128)(2,1)}, u32[]{:S(2)}, u32[]{:S(2)}) collective-permute-start(bf16[256,2048]{1,0:T(8,128)(2,1)} %get-tuple-element.48), channel_id=1, source_target_pairs={{0,16},{4,20},{8,24},{12,28},{16,0},{20,4},{24,8},{28,12},{1,17},{... | collective-permute-start | bytes 3145736 | tf_op jit(solution)/shard_map/ppermute | solution.py:34
  620.8 100.9 %collective-permute-start.45 = (bf16[704,2048]{1,0:T(8,128)(2,1)}, bf16[704,2048]{1,0:T(8,128)(2,1)}, u32[]{:S(2)}, u32[]{:S(2)}) collective-permute-start(bf16[704,2048]{1,0:T(8,128)(2,1)} %select_convert_fusion), channel_id=1, source_target_pairs={{0,4},{4,0},{8,12},{12,8},{16,20},{20,16},{24,28},{28,24},{1,5},{5... | collective-permute-start | bytes 8650760 | tf_op jit(solution)/shard_map/ppermute | solution.py:34
  708.3 171.4 %reduce-scatter.11.cloned.1.call-start = ((), (), s32[]{:S(2)}) async-start(), calls=%async_computation.11 | async-start | bytes 3604480 | tf_op jit(solution)/shard_map/reduce_scatter | solution.py:119
  730.4 151.7 %reduce-scatter.5.cloned.1.call-start = ((), (), s32[]{:S(2)}) async-start(), calls=%async_computation.8 | async-start | bytes 4259840 | tf_op jit(solution)/shard_map/reduce_scatter | solution.py:119
  792.4 169.0 %reduce-scatter.9.cloned.1.call-start = ((), (), s32[]{:S(2)}) async-start(), calls=%async_computation.10 | async-start | bytes 7208960 | tf_op jit(solution)/shard_map/reduce_scatter | solution.py:119
  883.3 82.4 %collective-permute-start.39 = (bf16[64,1664]{1,0:T(8,128)(2,1)S(1)}, bf16[64,1664]{1,0:T(8,128)(2,1)S(1)}, u32[]{:S(2)}, u32[]{:S(2)}) collective-permute-start(bf16[64,1664]{1,0:T(8,128)(2,1)S(1)} %get-tuple-element.93), channel_id=1, source_target_pairs={{0,8},{4,12},{8,0},{12,4},{16,24},{20,28},{24,16},{28,20},{1,9},{5... | collective-permute-start | bytes 638984 | tf_op jit(solution)/shard_map/ppermute | solution.py:34
  884.2 82.1 %collective-permute-start.38 = (bf16[64,1664]{1,0:T(8,128)(2,1)S(1)}, bf16[64,1664]{1,0:T(8,128)(2,1)S(1)}, u32[]{:S(2)}, u32[]{:S(2)}) collective-permute-start(bf16[64,1664]{1,0:T(8,128)(2,1)S(1)} %get-tuple-element.94), channel_id=1, source_target_pairs={{0,16},{4,20},{8,24},{12,28},{16,0},{20,4},{24,8},{28,12},{1,17},{... | collective-permute-start | bytes 638984 | tf_op jit(solution)/shard_map/ppermute | solution.py:34
  885.4 80.9 %collective-permute-start.37 = (bf16[64,1664]{1,0:T(8,128)(2,1)S(1)}, bf16[64,1664]{1,0:T(8,128)(2,1)S(1)}, u32[]{:S(2)}, u32[]{:S(2)}) collective-permute-start(bf16[64,1664]{1,0:T(8,128)(2,1)S(1)} %get-tuple-element.95), channel_id=1, source_target_pairs={{0,24},{4,28},{8,16},{12,20},{16,8},{20,12},{24,0},{28,4},{1,25},{... | collective-permute-start | bytes 638984 | tf_op jit(solution)/shard_map/ppermute | solution.py:34
  (98 other events, 2078.1 us)
Sparse Core Ops, SparseCore 0:
  29.9 68.3 all-gather.4
  99.9 26.5 all-gather.6
  128.0 58.6 all-gather.10
  188.7 105.3 all-gather.8
  708.4 24.2 reduce-scatter.6
  735.0 54.8 reduce-scatter.10
  792.5 63.8 reduce-scatter.4
  858.9 102.4 reduce-scatter.8

commit v2 on v1

v2 whole, which is shorter than its diff:
```python
import functools

import jax
import jax.numpy as jnp
from jax import lax
from jax.experimental import pallas as pl
from jax.experimental.pallas import tpu as pltpu
from jax.sharding import PartitionSpec as P

HEAD = 128
WINDOW = 64
GPS = 4
CORES = 2

EPS = 1e-05
NEGATIVE = -1e30
ROWS_DIMS = (((0,), (0,)), ((), ()))
COLS_DIMS = (((1,), (1,)), ((), ()))
BLOCK = 128
ROWS = 64
LANES = 128
F32 = jnp.float32
LOW = jnp.bfloat16


def matmul(left, right):
    return jnp.dot(left, right, preferred_element_type=F32)


def matmul_rows(left, right):
    return lax.dot_general(left, right, ROWS_DIMS, preferred_element_type=F32)


def matmul_cols(left, right):
    return lax.dot_general(left, right, COLS_DIMS, preferred_element_type=F32)


def exchange(value, flip):
    count = lax.axis_size("seq")
    return lax.ppermute(value, "seq", [(place, place ^ flip) for place in range(count)])


def swap_core(value):
    return exchange(value, 1)


def chip_count():
    return lax.axis_size("seq") // CORES


def own_chip():
    return lax.axis_index("seq") // CORES


def own_core():
    return lax.axis_index("seq") % CORES


def gather_near(value):
    if chip_count() != 4:
        return [exchange(value, CORES * k) for k in range(1, chip_count())]
    return [exchange(value, CORES), exchange(value, 2 * CORES)]


def gather_far(near):
    if chip_count() != 4:
        return []
    half = near[0].shape[0] // 2
    return [exchange(near[0][:half], 2 * CORES), exchange(near[1][half:], CORES)]


def gathered_rows(value, near, far):
    return jnp.concatenate([value] + near + far, axis=0)


def chips_scatter(blocks):
    return [blocks[0]] + [exchange(blocks[k], CORES * k) for k in range(1, chip_count())]


def chips_sum_near(parts):
    if chip_count() != 4:
        blocks = parts[0].reshape((chip_count(), -1) + parts[0].shape[1:])
        return chips_scatter([blocks[k] for k in range(chip_count())])
    return [exchange(parts[1], CORES), exchange(parts[2], 2 * CORES)]


def chips_sum_far(parts, near):
    if chip_count() != 4:
        return []
    on_second = (parts[3].astype(F32) + near[0][1].astype(F32)).astype(LOW)
    on_first = (parts[4].astype(F32) + near[1][1].astype(F32)).astype(LOW)
    return [exchange(on_second, 2 * CORES), exchange(on_first, CORES)]


def summands(parts, near, far):
    if not far:
        return near, []
    return [parts[0]], [(near[0][0], near[1][0]), tuple(far)]


def summed(parts, near, far):
    wholes, pairs = summands(parts, near, far)
    total = sum(part.astype(F32) for part in wholes)
    return total + sum(jnp.concatenate(pair, axis=0).astype(F32) for pair in pairs)


def spread_shapes(chips, rows, columns):
    if chips != 4:
        return [(rows, columns)]
    tall, low = rows // chips, rows // chips // 2
    return [(tall, columns), (2, low, columns), (2, low, columns), (low, columns), (low, columns)]


def spread_block(block, value, outs, place=slice(None)):
    own, first, second, keep_second, keep_first = outs
    low = value.shape[0] // 2
    if block == 0:
        own[:, place] = value
    if block == 1:
        first[0, :, place] = value[:low]
        keep_first[:, place] = value[low:]
    if block == 2:
        keep_second[:, place] = value[:low]
        second[0, :, place] = value[low:]
    if block == 3:
        first[1, :, place] = value[:low]
        second[1, :, place] = value[low:]


def spread_step(step, value, outs, place=slice(None)):
    if len(outs) == 1:
        outs[0][:, place] = value
        return
    for block in range(4):

        @pl.when(step == block)
        def _():
            spread_block(block, value, outs, place)


def in_order(blocks):
    chip = own_chip()
    bit = 1
    while bit < len(blocks):
        flipped = (chip & bit) > 0
        blocks = [jnp.where(flipped, blocks[i ^ bit], blocks[i]) for i in range(len(blocks))]
        bit *= 2
    return blocks


def to_chips(value):
    chip = own_chip()
    blocks = [
        lax.dynamic_index_in_dim(value, chip ^ k, axis=0, keepdims=False)
        for k in range(chip_count())
    ]
    return jnp.stack(in_order(chips_scatter(blocks)))


def after(value, *others):
    return lax.optimization_barrier((value,) + others)[0]


def seq_sum(value):
    bit = 1
    while bit < lax.axis_size("seq"):
        value = value + exchange(value, bit)
        bit *= 2
    return value


def own_first(first, second):
    flipped = own_core() > 0
    return jnp.where(flipped, second, first), jnp.where(flipped, first, second)


def core_rows(mine, other):
    return jnp.concatenate(own_first(mine, other), axis=0)


def batch_gather(value, axis):
    return lax.all_gather(value, "batch", axis=axis, tiled=True)


def batch_scatter(value, axis):
    return lax.psum_scatter(value, "batch", scatter_dimension=axis, tiled=True)


FREE = pl.CostEstimate(flops=0, bytes_accessed=0, transcendentals=0)


def params(megabytes=32):
    return pltpu.CompilerParams(vmem_limit_bytes=megabytes * 2**20)


def whole(shape):
    return pl.BlockSpec(shape, lambda *step: (0,) * len(shape))


SCALAR = pl.BlockSpec(memory_space=pltpu.SMEM)


def own_columns(values, flipped, chips):
    width = values.shape[1] // (chips * CORES)
    cells = [values[:, i * width : (i + 1) * width] for i in range(chips * CORES)]
    mine = [jnp.where(flipped, cells[2 * q + 1], cells[2 * q]) for q in range(chips)]
    other = [jnp.where(flipped, cells[2 * q], cells[2 * q + 1]) for q in range(chips)]
    return jnp.concatenate(mine + other, axis=1)


def natural_columns(values, flipped, chips):
    width = values.shape[1] // (chips * CORES)
    cells = [values[:, i * width : (i + 1) * width] for i in range(chips * CORES)]
    pairs = []
    for q in range(chips):
        mine, other = cells[q], cells[chips + q]
        pairs += [jnp.where(flipped, other, mine), jnp.where(flipped, mine, other)]
    return jnp.concatenate(pairs, axis=1)


def project_kernel(chips, core, tokens, gain, mine, other, act, out):
    flipped = core[0] > 0
    half, columns = mine.shape[0], out.shape[1]

    @pl.loop(0, tokens.shape[0], step=ROWS)
    def _(start):
        rows = pl.ds(pl.multiple_of(start, ROWS), ROWS)
        values = tokens[rows, :].astype(F32)
        inverse = lax.rsqrt(jnp.mean(values * values, axis=-1, keepdims=True) + EPS)
        act[rows, :] = (own_columns(values * inverse, flipped, chips) * gain[...]).astype(LOW)

    total = matmul(act[:, :half], mine[:, :columns]) + matmul(act[:, half:], other[:, :columns])
    out[...] = total.astype(LOW)


def project(core, tokens, gain, mine, other, columns, chips):
    rows, features = tokens.shape
    tall = rows // chips
    return pl.pallas_call(
        functools.partial(project_kernel, chips),
        grid=(chips,),
        in_specs=[
            SCALAR,
            pl.BlockSpec((tall, features), lambda i: (i, 0)),
            whole(gain.shape),
            whole(mine.shape),
            whole(other.shape),
        ],
        out_specs=[
            pl.BlockSpec((tall, features), lambda i: (i, 0)),
            pl.BlockSpec((tall, columns), lambda i: (i, 0)),
        ],
        out_shape=[
            jax.ShapeDtypeStruct((rows, features), LOW),
            jax.ShapeDtypeStruct((rows, columns), LOW),
        ],
        compiler_params=params(40),
        cost_estimate=FREE,
    )(core, tokens, gain, mine, other)


def windows(keys, rim, step):
    if step == 0:
        return jnp.concatenate([rim, keys[:BLOCK]], axis=0)
    return keys[step * BLOCK - WINDOW : (step + 1) * BLOCK]


def window_probs(queries, keys, first, preceded):
    scores = matmul_cols(queries, keys) * HEAD ** (-0.5)
    query = lax.broadcasted_iota(jnp.int32, scores.shape, 0)
    key = lax.broadcasted_iota(jnp.int32, scores.shape, 1)
    allowed = (key > query) & (key <= query + WINDOW)
    if first:
        allowed = allowed & ((key >= WINDOW) | (preceded > 0))
    scores = jnp.where(allowed, scores, NEGATIVE)
    expo = jnp.exp(scores - jnp.max(scores, axis=-1, keepdims=True))
    return expo / jnp.sum(expo, axis=-1, keepdims=True)


def attend_kernel(core, preceded, qkv, rim, out):
    flipped = core[0] > 0
    ready = preceded[pl.program_id(0)]
    width = out.shape[2]
    heads = width // HEAD
    mixed = []
    for head in range(heads):
        cell = slice(head * HEAD, (head + 1) * HEAD)
        queries, keys, values = (
            qkv[0, :, part * width + head * HEAD : part * width + (head + 1) * HEAD]
            for part in range(3)
        )
        rim_keys = rim[0, :, cell]
        rim_values = rim[0, :, width + head * HEAD : width + (head + 1) * HEAD]
        rows = []
        for step in range(queries.shape[0] // BLOCK):
            probs = window_probs(
                queries[step * BLOCK : (step + 1) * BLOCK],
                windows(keys, rim_keys, step),
                step == 0,
                ready,
            )
            rows.append(matmul(probs.astype(LOW), windows(values, rim_values, step)))
        mixed.append(jnp.concatenate(rows, axis=0).astype(LOW))
    half = heads // CORES
    for head in range(half):
        first, second = mixed[head], mixed[half + head]
        out[0, :, head * HEAD : (head + 1) * HEAD] = jnp.where(flipped, second, first)
        out[0, :, (half + head) * HEAD : (half + head + 1) * HEAD] = jnp.where(
            flipped, first, second
        )


def attention(core, preceded, qkv, rims):
    chips, rows, columns = qkv.shape
    width = columns // 3
    return pl.pallas_call(
        attend_kernel,
        grid=(chips,),
        in_specs=[
            SCALAR,
            SCALAR,
            pl.BlockSpec((1, rows, columns), lambda i: (i, 0, 0)),
            pl.BlockSpec((1,) + rims.shape[1:], lambda i: (i, 0, 0)),
        ],
        out_specs=pl.BlockSpec((1, rows, width), lambda i: (i, 0, 0)),
        out_shape=jax.ShapeDtypeStruct((chips, rows, width), LOW),
        compiler_params=params(),
        cost_estimate=FREE,
    )(core, preceded, qkv, rims)


def attend_back_kernel(core, preceded, qkv, rim, d_mixed, out, lent):
    flipped = core[0] > 0
    ready = preceded[pl.program_id(0)]
    width = d_mixed.shape[2]
    heads = width // HEAD
    half = heads // CORES
    factor = HEAD ** (-0.5)
    for head in range(heads):
        queries, keys, values = (
            qkv[0, :, part * width + head * HEAD : part * width + (head + 1) * HEAD]
            for part in range(3)
        )
        rim_keys = rim[0, :, head * HEAD : (head + 1) * HEAD]
        rim_values = rim[0, :, width + head * HEAD : width + (head + 1) * HEAD]
        there = (head + half) % heads
        upstream = jnp.where(
            flipped,
            d_mixed[0, :, there * HEAD : (there + 1) * HEAD],
            d_mixed[0, :, head * HEAD : (head + 1) * HEAD],
        )
        steps = queries.shape[0] // BLOCK
        d_queries, d_keys, d_values = [], [], []
        for step in range(steps):
            rows = slice(step * BLOCK, (step + 1) * BLOCK)
            near_keys, near_values = windows(keys, rim_keys, step), windows(values, rim_values, step)
            probs = window_probs(queries[rows], near_keys, step == 0, ready)
            d_probs = matmul_cols(upstream[rows], near_values)
            d_scores = probs * (d_probs - jnp.sum(probs * d_probs, axis=-1, keepdims=True))
            d_scores = d_scores.astype(LOW)
            d_queries.append(matmul(d_scores, near_keys) * factor)
            d_keys.append(matmul_rows(d_scores, queries[rows]) * factor)
            d_values.append(matmul_rows(probs.astype(LOW), upstream[rows]))
        out[0, :, head * HEAD : (head + 1) * HEAD] = jnp.concatenate(d_queries, axis=0).astype(LOW)
        for part, grads in ((1, d_keys), (2, d_values)):
            first = (part - 1) * width + head * HEAD
            lent[0, :, first : first + HEAD] = grads[0][:WINDOW].astype(LOW)
            for step in range(steps):
                own = grads[step][WINDOW:]
                if step + 1 < steps:
                    keep = own[: BLOCK - WINDOW]
                    own = jnp.concatenate(
                        [keep, own[BLOCK - WINDOW :] + grads[step + 1][:WINDOW]], axis=0
                    )
                out[
                    0,
                    step * BLOCK : (step + 1) * BLOCK,
                    part * width + head * HEAD : part * width + (head + 1) * HEAD,
                ] = own.astype(LOW)


def attention_back(core, preceded, qkv, rims, d_mixed):
    chips, rows, columns = qkv.shape
    width = columns // 3
    return pl.pallas_call(
        attend_back_kernel,
        grid=(chips,),
        in_specs=[
            SCALAR,
            SCALAR,
            pl.BlockSpec((1, rows, columns), lambda i: (i, 0, 0)),
            pl.BlockSpec((1,) + rims.shape[1:], lambda i: (i, 0, 0)),
            pl.BlockSpec((1, rows, width), lambda i: (i, 0, 0)),
        ],
        out_specs=[
            pl.BlockSpec((1, rows, columns), lambda i: (i, 0, 0)),
            pl.BlockSpec((1,) + rims.shape[1:], lambda i: (i, 0, 0)),
        ],
        out_shape=[
            jax.ShapeDtypeStruct(qkv.shape, LOW),
            jax.ShapeDtypeStruct(rims.shape, LOW),
        ],
        compiler_params=params(),
        cost_estimate=FREE,
    )(core, preceded, qkv, rims, d_mixed)


def out_kernel(chips, core, mixed, mine, other, tokens, gain, resid, act):
    step, steps = pl.program_id(0), pl.num_programs(0)
    flipped = core[0] > 0

    @pl.when(step == 0)
    def _():
        resid[...] = tokens[...].astype(F32)

    @pl.when(step < steps // 2)
    def _():
        resid[...] += matmul(mixed[...], mine[...])

    @pl.when(step >= steps // 2)
    def _():
        resid[...] += matmul(mixed[...], other[...])

    @pl.when(step == steps - 1)
    def _():
        @pl.loop(0, tokens.shape[0], step=ROWS)
        def _(start):
            rows = pl.ds(pl.multiple_of(start, ROWS), ROWS)
            values = resid[rows, :]
            inverse = lax.rsqrt(jnp.mean(values * values, axis=-1, keepdims=True) + EPS)
            normed = own_columns(values * inverse, flipped, chips)
            act[rows, :] = (normed * gain[...]).astype(LOW)


def out_project(core, mixed, mine, other, tokens, gain, chips):
    rows, features = tokens.shape
    depth = mine.shape[0] // chips
    return pl.pallas_call(
        functools.partial(out_kernel, chips),
        grid=(2 * chips,),
        in_specs=[
            SCALAR,
            pl.BlockSpec((rows, depth), lambda i: (0, i)),
            pl.BlockSpec((depth, features), lambda i: (jnp.minimum(i, chips - 1), 0)),
            pl.BlockSpec((depth, features), lambda i: (jnp.maximum(i - chips, 0), 0)),
            whole(tokens.shape),
            whole(gain.shape),
        ],
        out_specs=[whole(tokens.shape), whole(tokens.shape)],
        out_shape=[
            jax.ShapeDtypeStruct(tokens.shape, F32),
            jax.ShapeDtypeStruct(tokens.shape, LOW),
        ],
        compiler_params=params(),
        cost_estimate=FREE,
    )(core, mixed, mine, other, tokens, gain)


def row_specs(steps, wholes, pairs, features):
    half = steps // 2

    def spec(first, last, count):
        low = functools.partial(lambda first, last, i: jnp.clip(i - first, 0, last - 1), first, last)
        if count == 2:
            return pl.BlockSpec((ROWS, features), lambda i: (low(i), 0))
        return pl.BlockSpec((None, ROWS, features), lambda i: (0, low(i), 0))

    specs = [spec(0, steps, 2) for _ in wholes]
    for first, second in pairs:
        specs += [spec(0, half, first.ndim), spec(half, half, second.ndim)]
    return specs


def sum_rows(step, steps, count, refs):
    total = sum(ref[...].astype(F32) for ref in refs[:count])
    for i in range(count, len(refs), 2):
        part = jnp.where(step < steps // 2, refs[i][...], refs[i + 1][...])
        total = total + part.astype(F32)
    return total


def norm_back_rows(chips, flipped, d_act, values, gain, upstream):
    d_act = natural_columns(d_act, flipped, chips)
    inverse = lax.rsqrt(jnp.mean(values * values, axis=-1, keepdims=True) + EPS)
    normed = values * inverse
    scaled = d_act * natural_columns(gain, flipped, chips)
    result = upstream + inverse * (
        scaled - normed * jnp.mean(scaled * normed, axis=-1, keepdims=True)
    )
    return result, jnp.sum(d_act * normed, axis=0, keepdims=True)


def middle_kernel(chips, steps, count, size, core, *refs):
    parts, refs = refs[:size], refs[size:]
    resid, gain, d_final, mine, other, d_resid, d_attn, d_mixed, gain_part = refs
    step = pl.program_id(0)
    flipped = core[0] > 0
    tall = resid.shape[0]

    @pl.when(step < steps)
    def _():
        grad, part = norm_back_rows(
            chips,
            flipped,
            sum_rows(step, steps, count, parts),
            resid[...],
            gain[...],
            d_final[...],
        )
        d_resid[...] = grad
        d_attn[pl.ds(pl.multiple_of(step * tall, tall), tall), :] = grad.astype(LOW)

        @pl.when(step == 0)
        def _():
            gain_part[...] = part

        @pl.when(step > 0)
        def _():
            gain_part[...] += part

    @pl.when(step == steps)
    def _():
        gain_part[...] = own_columns(gain_part[...], flipped, chips)

    @pl.when((step >= steps) & (step < steps + chips))
    def _():
        d_mixed[0] = matmul_cols(d_attn[...], mine[...]).astype(LOW)

    @pl.when(step >= steps + chips)
    def _():
        d_mixed[0] = matmul_cols(d_attn[...], other[...]).astype(LOW)


def middle(core, wholes, pairs, resid, gain, d_final, mine, other, chips):
    parts = list(wholes) + [half for pair in pairs for half in pair]
    rows, features = resid.shape
    steps = rows // ROWS
    depth = mine.shape[0] // chips

    def by_rows():
        return pl.BlockSpec((ROWS, features), lambda i: (jnp.minimum(i, steps - 1), 0))

    return pl.pallas_call(
        functools.partial(middle_kernel, chips, steps, len(wholes), len(parts)),
        grid=(steps + 2 * chips,),
        in_specs=[SCALAR]
        + row_specs(steps, wholes, pairs, features)
        + [
            by_rows(),
            whole(gain.shape),
            by_rows(),
            pl.BlockSpec((depth, features), lambda i: (jnp.clip(i - steps, 0, chips - 1), 0)),
            pl.BlockSpec(
                (depth, features), lambda i: (jnp.clip(i - steps - chips, 0, chips - 1), 0)
            ),
        ],
        out_specs=[
            by_rows(),
            whole(resid.shape),
            pl.BlockSpec(
                (1, rows, depth),
                lambda i: (
                    lax.rem(jnp.maximum(i - steps, 0), chips),
                    0,
                    lax.div(jnp.maximum(i - steps, 0), chips),
                ),
            ),
            whole((1, features)),
        ],
        out_shape=[
            jax.ShapeDtypeStruct(resid.shape, F32),
            jax.ShapeDtypeStruct(resid.shape, LOW),
            jax.ShapeDtypeStruct((chips, rows, 2 * depth), LOW),
            jax.ShapeDtypeStruct((1, features), F32),
        ],
        compiler_params=params(),
        cost_estimate=FREE,
    )(core, *parts, resid, gain, d_final, mine, other)


def last_kernel(chips, steps, count, core, *refs):
    parts, refs = refs[:-4], refs[-4:]
    tokens, gain, d_resid, out = refs
    out[...], _ = norm_back_rows(
        chips,
        core[0] > 0,
        sum_rows(pl.program_id(0), steps, count, parts),
        tokens[...].astype(F32),
        gain[...],
        d_resid[...],
    )


def last(core, wholes, pairs, tokens, gain, d_resid, chips):
    parts = list(wholes) + [half for pair in pairs for half in pair]
    rows, features = tokens.shape
    steps = rows // ROWS
    by_rows = pl.BlockSpec((ROWS, features), lambda i: (i, 0))
    return pl.pallas_call(
        functools.partial(last_kernel, chips, steps, len(wholes)),
        grid=(steps,),
        in_specs=[SCALAR]
        + row_specs(steps, wholes, pairs, features)
        + [by_rows, whole(gain.shape), by_rows],
        out_specs=by_rows,
        out_shape=jax.ShapeDtypeStruct(tokens.shape, F32),
        compiler_params=params(),
        cost_estimate=FREE,
    )(core, *parts, tokens, gain, d_resid)


def inner_first_kernel(act, gate, upward, out):
    out[...] = matmul(act[...], jnp.concatenate([gate[...], upward[...]], axis=1))


def inner_second_kernel(act, gate, upward, first, hidden, slope_gate, slope_up):
    width = gate.shape[1]
    both = first[...] + matmul(act[...], jnp.concatenate([gate[...], upward[...]], axis=1))
    gate, upward = both[:, :width], both[:, width:]
    sigma = jax.nn.sigmoid(gate)
    silu = gate * sigma
    hidden[...] = (silu * upward).astype(LOW)
    slope_gate[...] = upward * sigma * (1.0 + gate * (1.0 - sigma))
    slope_up[...] = silu


def inner_specs(act, weights, part):
    rows = act.shape[0]
    half, columns = weights.shape
    tiles = columns // (2 * LANES)
    return tiles, [
        pl.BlockSpec((rows, half), lambda i: (0, part)),
        pl.BlockSpec((half, LANES), lambda i: (0, i)),
        pl.BlockSpec((half, LANES), lambda i: (0, tiles + i)),
    ]


def inner_first(act, weights):
    rows, columns = act.shape[0], weights.shape[1]
    if columns % (2 * LANES):
        return matmul(act[:, : weights.shape[0]], weights)
    tiles, specs = inner_specs(act, weights, 0)
    return pl.pallas_call(
        inner_first_kernel,
        grid=(tiles,),
        in_specs=specs,
        out_specs=pl.BlockSpec((rows, 2 * LANES), lambda i: (0, i)),
        out_shape=jax.ShapeDtypeStruct((rows, columns), F32),
        compiler_params=params(),
        cost_estimate=FREE,
    )(act, weights, weights)


def inner_second(act, weights, first):
    rows, columns = act.shape[0], weights.shape[1]
    width = columns // 2
    if columns % (2 * LANES):
        both = first + matmul(act[:, weights.shape[0] :], weights)
        gate, upward = both[:, :width], both[:, width:]
        sigma = jax.nn.sigmoid(gate)
        silu = gate * sigma
        return (silu * upward).astype(LOW), upward * sigma * (1.0 + gate * (1.0 - sigma)), silu
    tiles, specs = inner_specs(act, weights, 1)
    tile = pl.BlockSpec((rows, LANES), lambda i: (0, i))
    return pl.pallas_call(
        inner_second_kernel,
        grid=(tiles,),
        in_specs=specs + [pl.BlockSpec((rows, 2 * LANES), lambda i: (0, i))],
        out_specs=[tile] * 3,
        out_shape=[
            jax.ShapeDtypeStruct((rows, width), LOW),
            jax.ShapeDtypeStruct((rows, width), F32),
            jax.ShapeDtypeStruct((rows, width), F32),
        ],
        compiler_params=params(),
        cost_estimate=FREE,
    )(act, weights, weights, first)


def place_halves(flag, mine, other, out):
    rows = mine.shape[0]
    core = flag[0]
    out[pl.ds(pl.multiple_of(core * rows, 16), rows), :] = mine[...]
    out[pl.ds(pl.multiple_of((1 - core) * rows, 16), rows), :] = other[...]


def inner_back_kernel(flag, d_ffn, mine, other, slope_gate, slope_up, out, down):
    @pl.when(pl.program_id(0) == 0)
    def _():
        place_halves(flag, mine, other, down)

    width = down.shape[0]
    d_hidden = matmul_cols(d_ffn[...], down[...])
    out[:, :width] = (d_hidden * slope_gate[...]).astype(LOW)
    out[:, width:] = (d_hidden * slope_up[...]).astype(LOW)


def inner_back(flag, d_ffn, mine, other, slope_gate, slope_up, chips):
    rows, features = d_ffn.shape
    width = 2 * mine.shape[0]
    if width % LANES:
        d_hidden = matmul_cols(d_ffn, core_rows(mine, other))
        return jnp.concatenate([d_hidden * slope_gate, d_hidden * slope_up], axis=1).astype(LOW)
    tall = rows // chips
    flat = pl.BlockSpec((tall, width), lambda i: (i, 0))
    return pl.pallas_call(
        inner_back_kernel,
        grid=(chips,),
        in_specs=[
            SCALAR,
            pl.BlockSpec((tall, features), lambda i: (i, 0)),
            whole(mine.shape),
            whole(other.shape),
            flat,
            flat,
        ],
        out_specs=pl.BlockSpec((tall, 2 * width), lambda i: (i, 0)),
        out_shape=jax.ShapeDtypeStruct((rows, 2 * width), LOW),
        scratch_shapes=[pltpu.VMEM((width, features), LOW)],
        compiler_params=params(44),
        cost_estimate=FREE,
    )(flag, d_ffn, mine, other, slope_gate, slope_up)


def back_project_kernel(d_out, mine, other, act, total, *outs):
    half, columns = mine.shape[0], d_out.shape[1]
    step = pl.program_id(0)
    for place, weights in ((slice(0, half), mine), (slice(half, 2 * half), other)):
        grad = matmul_cols(d_out[...], weights[:, :columns])
        spread_step(step, grad.astype(LOW), outs, place)
        part = jnp.sum(grad * act[:, place].astype(F32), axis=0, keepdims=True)
        total[:, place] = part + jnp.where(step > 0, total[:, place], 0.0)


def back_project(d_out, mine, other, act, chips):
    rows, columns = d_out.shape
    features = 2 * mine.shape[0]
    tall = rows // chips
    shapes = spread_shapes(chips, rows, features)
    flat = pl.BlockSpec((tall, features), lambda i: (i, 0))
    total, *outs = pl.pallas_call(
        back_project_kernel,
        grid=(chips,),
        in_specs=[
            pl.BlockSpec((tall, columns), lambda i: (i, 0)),
            whole(mine.shape),
            whole(other.shape),
            flat,
        ],
        out_specs=[whole((1, features))]
        + ([flat] if len(shapes) == 1 else [whole(shape) for shape in shapes]),
        out_shape=[jax.ShapeDtypeStruct((1, features), F32)]
        + [jax.ShapeDtypeStruct(shape, LOW) for shape in shapes],
        compiler_params=params(48),
        cost_estimate=FREE,
    )(d_out, mine, other, act)
    return outs, total


def turned_kernel(count, left, right, *refs):
    arrived, outs = refs[:count], refs[count:]
    total = matmul_rows(left[...], right[...])
    if arrived:
        total = total + arrived[0][...].astype(F32)
    total = total.astype(LOW)
    if len(outs) == 1:
        outs[0][...] = total
        return
    tall = total.shape[0] // 4
    for block in range(4):
        spread_block(block, total[block * tall : (block + 1) * tall], outs)


def turned(left, part, right, *arrived, chips=1):
    rows, half = left.shape[0], left.shape[1] // CORES
    width = right.shape[1]
    tile = LANES if width % (2 * LANES) else 2 * LANES
    shapes = spread_shapes(chips, half, width)
    outs = pl.pallas_call(
        functools.partial(turned_kernel, len(arrived)),
        grid=(width // tile,),
        in_specs=[
            pl.BlockSpec((rows, half), lambda i: (0, part)),
            pl.BlockSpec((rows, tile), lambda i: (0, i)),
        ]
        + [pl.BlockSpec((half, tile), lambda i: (0, i)) for _ in arrived],
        out_specs=[
            pl.BlockSpec(shape[:-1] + (tile,), lambda i, n=len(shape): (0,) * (n - 1) + (i,))
            for shape in shapes
        ],
        out_shape=[jax.ShapeDtypeStruct(shape, LOW) for shape in shapes],
        compiler_params=params(),
        cost_estimate=FREE,
    )(left, right, *arrived)
    return outs[0] if chips == 1 else outs


def inner_out_kernel(flag, left, mine, other, *refs):
    outs, down = refs[:-1], refs[-1]
    step = pl.program_id(0)

    @pl.when(step == 0)
    def _():
        place_halves(flag, mine, other, down)

    spread_step(step, matmul(left[...], down[...]).astype(LOW), outs)


def inner_out(flag, hidden, mine, other, chips):
    rows, width = hidden.shape
    features = mine.shape[1]
    if width % LANES:
        return [matmul(hidden, core_rows(mine, other)).astype(LOW)]
    tall = rows // chips
    shapes = spread_shapes(chips, rows, features)
    flat = pl.BlockSpec((tall, features), lambda i: (i, 0))
    return pl.pallas_call(
        inner_out_kernel,
        grid=(chips,),
        in_specs=[
            SCALAR,
            pl.BlockSpec((tall, width), lambda i: (i, 0)),
            whole(mine.shape),
            whole(other.shape),
        ],
        out_specs=[flat] if len(shapes) == 1 else [whole(shape) for shape in shapes],
        out_shape=[jax.ShapeDtypeStruct(shape, LOW) for shape in shapes],
        scratch_shapes=[pltpu.VMEM((width, features), LOW)],
        compiler_params=params(36),
        cost_estimate=FREE,
    )(flag, hidden, mine, other)


def half_kernel(flag, left, right, *refs):
    arrived, out = refs[:-1], refs[-1]
    rows = out.shape[0]
    start = left.shape[1] - rows
    wide = -(-rows // LANES) * LANES
    second = flag[0] > 0
    first = pl.multiple_of(jnp.where(second, left.shape[1] - wide, 0), LANES)
    total = matmul_rows(left[:, pl.ds(first, wide)], right[...])
    total = jnp.where(second, total[wide - rows :], total[:rows])
    if arrived:
        total = total + arrived[0][...].astype(F32)
    out[...] = total.astype(LOW)


def half_product(flag, left, right, *arrived):
    rows, columns = left.shape
    width = right.shape[1]
    half = columns // 2
    if columns % LANES:
        total = matmul_rows(left, right)
        total = jnp.where(flag[0] > 0, total[half:], total[:half])
        return sum([part.astype(F32) for part in arrived], total).astype(LOW)
    tile = 2 * LANES
    return pl.pallas_call(
        half_kernel,
        grid=(width // tile,),
        in_specs=[SCALAR, whole(left.shape), pl.BlockSpec((rows, tile), lambda i: (0, i))]
        + [pl.BlockSpec((half, tile), lambda i: (0, i)) for _ in arrived],
        out_specs=pl.BlockSpec((half, tile), lambda i: (0, i)),
        out_shape=jax.ShapeDtypeStruct((half, width), LOW),
        compiler_params=params(),
        cost_estimate=FREE,
    )(flag, left, right, *arrived)


def per_device(
    tokens,
    out_cotangent,
    group_ids,
    attn_gain,
    query_weight,
    key_weight,
    value_weight,
    out_weight,
    ffn_gain,
    gate_weight,
    up_weight,
    down_weight,
):
    tok_count, features = tokens.shape[1:]
    weight_rows, inner = gate_weight.shape
    chips = chip_count()
    chip, core = own_chip(), own_core()
    ids = lax.iota(jnp.int32, chips)
    head_width, inner_width = features // chips, inner // chips
    half = features // CORES
    flag = jnp.full((1,), core, jnp.int32)
    tokens, out_cotangent = tokens[0], out_cotangent[0]

    gains = jnp.concatenate(
        [
            jnp.broadcast_to(attn_gain[:, None], (weight_rows, LANES // 2)),
            jnp.broadcast_to(ffn_gain[:, None], (weight_rows, LANES // 2)),
        ],
        axis=1,
    )

    def for_chip(weight, k):
        width = weight.shape[1] // chips
        return lax.dynamic_slice_in_dim(weight, (chip ^ k) * width, width, axis=1)

    def rows_of_chips(weights, *others):
        parts = [jnp.concatenate([for_chip(w, k) for w in weights], axis=1) for k in range(chips)]
        parts = [jnp.concatenate([part] + list(others), axis=1) for part in parts]
        return jnp.stack(in_order(chips_scatter(parts)))

    group_span = GPS * lax.axis_size("batch")
    onehot = (group_ids[0, :, None] == jnp.arange(group_span, dtype=jnp.int32)[None, :]).astype(F32)
    group_total = seq_sum(jnp.sum(onehot, axis=0, keepdims=True))
    own_total = jnp.sum(onehot * group_total, axis=-1)[:, None]
    weighting = tok_count * lax.axis_size("seq") / (GPS * own_total)
    d_final = out_cotangent.astype(F32) * weighting

    out_mine = batch_gather(out_weight, 0)
    qkv_rows = rows_of_chips([query_weight, key_weight, value_weight], gains)
    qkv_mine = batch_gather(after(qkv_rows, out_mine), 1).reshape(half, -1)
    tokens_sent = after(tokens, qkv_rows, group_total)
    tokens_near = gather_near(tokens_sent)
    tokens_far = gather_far(tokens_near)
    gathered = gathered_rows(tokens_sent, tokens_near, tokens_far)
    gate_weight, up_weight = after((gate_weight, up_weight), *tokens_near, *tokens_far)
    inner_rows = rows_of_chips([gate_weight, up_weight])
    inner_mine = batch_gather(inner_rows, 1).reshape(half, -1)
    down_mine = batch_gather(after(down_weight, inner_rows), 0)

    out_sent = after(out_mine, inner_rows)
    out_near = gather_near(out_sent)
    qkv_mine = after(qkv_mine, *out_near)
    qkv_other = swap_core(qkv_mine)
    out_far = gather_far(out_near)
    qkv_other = after(qkv_other, *out_far)
    columns = 3 * head_width
    gain_one, gain_two = (
        jnp.concatenate([qkv_mine[:, place], qkv_other[:, place]]).astype(F32)[None]
        for place in (columns, columns + LANES // 2)
    )
    act_one, qkv = project(flag, gathered, gain_one, qkv_mine, qkv_other, columns, chips)
    qkv = qkv.reshape(chips, tok_count, columns)
    ffn_sent = after(d_final.astype(LOW), *out_far)
    ffn_near = gather_near(ffn_sent)
    place = chip ^ ids
    tails = swap_core(qkv[:, tok_count - WINDOW :, head_width:])
    ffn_far = gather_far(ffn_near)
    before = jnp.where(core > 0, ids, chip ^ jnp.maximum(place - 1, 0))
    follow = jnp.where(core > 0, chip ^ jnp.minimum(place + 1, chips - 1), ids)
    preceded = ((core > 0) | (place > 0)).astype(jnp.int32)
    followed = (core == 0) | (place < chips - 1)
    rims = jnp.take(after(tails, *ffn_near), before, axis=0)
    mixed = attention(flag, preceded, qkv, rims)

    mixed = after(mixed, *ffn_far)
    mixed_own = chips_scatter([mixed[k] for k in range(chips)])
    cell = head_width // CORES
    mixed_own = jnp.concatenate(
        [block[:, i * cell : (i + 1) * cell] for i in range(CORES) for block in mixed_own], axis=1
    )
    out_near = after(out_near, mixed)
    out_half = gathered_rows(out_sent, out_near, out_far)
    out_other = swap_core(out_half)
    resid, act_two_own = out_project(
        flag, mixed_own, out_half, out_other, tokens, gain_two, chips
    )

    act_near = gather_near(act_two_own)
    act_far = gather_far(act_near)
    act_two = gathered_rows(act_two_own, act_near, act_far)
    d_ffn = gathered_rows(ffn_sent, after(ffn_near, act_two_own), ffn_far)
    inner_mine = after(inner_mine, *act_near, *act_far)
    inner_other = swap_core(inner_mine)
    hidden, slope_gate, slope_up = inner_second(
        act_two, inner_other, inner_first(act_two, inner_mine)
    )
    down_send = half_product(1 - flag, hidden, d_ffn)
    down_back = swap_core(down_send)
    down_sum = half_product(flag, hidden, after(d_ffn, down_send), down_back)
    down_mine = after(down_mine, down_sum)
    down_other = swap_core(down_mine)
    down_grad = batch_scatter(down_sum, 0)
    d_gate_up = inner_back(
        flag, after(d_ffn, down_sum), down_mine, down_other, slope_gate, slope_up, chips
    )
    inner_send = turned(act_two, 1, d_gate_up)
    act_parts, _ = back_project(
        after(d_gate_up, inner_send), inner_mine, inner_other, act_two, chips
    )
    act_near = chips_sum_near(act_parts)
    inner_sum = turned(
        act_two, 0, after(d_gate_up, act_parts[0], down_grad), swap_core(inner_send)
    )
    act_far = chips_sum_far(act_parts, act_near)
    inner_sum = after(inner_sum, *act_near)
    inner_grad = batch_scatter(inner_sum.reshape(chips, half // chips, -1), 1)
    d_resid, d_attn, d_mixed_own, gain_two_part = middle(
        flag,
        *summands(act_parts, act_near, act_far),
        resid,
        gain_two,
        d_final,
        out_half,
        out_other,
        chips,
    )

    d_mixed_parts = chips_scatter([d_mixed_own[k] for k in range(chips)])
    d_mixed = jnp.stack(d_mixed_parts)
    d_qkv, lent = attention_back(flag, preceded, qkv, rims, d_mixed)
    lent = swap_core(lent)
    block_parts = inner_out(flag, after(hidden, d_mixed_own), down_mine, down_other, chips)
    block_near = chips_sum_near(block_parts)

    returned = jnp.where(followed[:, None, None], jnp.take(lent, follow, axis=0), 0)
    d_qkv = d_qkv.at[:, tok_count - WINDOW :, head_width:].add(returned)
    d_qkv = after(d_qkv.reshape(chips * tok_count, columns), *block_near)
    block_far = chips_sum_far(block_parts, block_near)
    qkv_send = turned(act_one, 1, d_qkv)
    out_send = turned(mixed_own, 1, after(d_attn, qkv_send))
    qkv_sum = turned(act_one, 0, after(d_qkv, out_send), swap_core(qkv_send))
    out_parts = turned(mixed_own, 0, after(d_attn, qkv_sum), swap_core(out_send), chips=chips)
    if chips == 1:
        out_parts = [out_parts]
    out_parts = after(out_parts, *block_far)
    out_near = chips_sum_near(out_parts)
    out_far = chips_sum_far(out_parts, out_near)
    d_act_parts, gain_one_part = back_project(
        after(d_qkv, out_parts[0]), qkv_mine, qkv_other, act_one, chips
    )
    gain_one_part = gain_one_part / gain_one
    gain_parts = jnp.concatenate(
        [
            jnp.broadcast_to(part.reshape(features, 1), (features, LANES // 2))
            for part in (gain_one_part, gain_two_part)
        ],
        axis=1,
    )
    d_act_parts = after(d_act_parts, *out_far)
    d_act_near = chips_sum_near(d_act_parts)
    d_act_far = chips_sum_far(d_act_parts, d_act_near)
    gain_sum = gain_parts[:half] + swap_core(gain_parts[half:].astype(LOW)).astype(F32)
    qkv_sum = jnp.concatenate([qkv_sum, gain_sum.astype(LOW)], axis=1)
    qkv_sum = after(qkv_sum, inner_grad)
    qkv_grad = batch_scatter(qkv_sum.reshape(chips, half // chips, -1), 1)
    out_sum = summed(out_parts, out_near, out_far).astype(LOW)
    out_grad = batch_scatter(after(out_sum, qkv_grad), 0)
    tokens_grad = last(
        flag, *summands(d_act_parts, d_act_near, d_act_far), tokens, gain_one, d_resid, chips
    )
    block_out = (resid + summed(block_parts, block_near, block_far)).astype(LOW)

    def columns_of_chips(grad):
        chip_rows = [
            lax.dynamic_index_in_dim(grad, chip ^ k, axis=0, keepdims=False) for k in range(chips)
        ]
        return in_order(chips_scatter(chip_rows))

    inner_grad = columns_of_chips(inner_grad)
    qkv_grad = columns_of_chips(qkv_grad)

    def whole_columns(blocks, first, width):
        parts = [block[:, first : first + width] for block in blocks]
        return jnp.concatenate(parts, axis=1).astype(F32)

    gain_grads = sum(block[:, columns:].astype(F32) for block in qkv_grad)

    return (
        block_out[None],
        tokens_grad[None],
        gain_grads[:, 0],
        whole_columns(qkv_grad, 0, head_width),
        whole_columns(qkv_grad, head_width, head_width),
        whole_columns(qkv_grad, 2 * head_width, head_width),
        out_grad.astype(F32),
        gain_grads[:, LANES // 2],
        whole_columns(inner_grad, 0, inner_width),
        whole_columns(inner_grad, inner_width, inner_width),
        down_grad.astype(F32),
    )


def solution(mesh):
    rows = P(("seq", "batch"), None)
    vector = P(("seq", "batch"))
    cells = P("batch", "seq", None)
    return jax.shard_map(
        per_device,
        mesh=mesh,
        in_specs=(cells, cells, P("batch", "seq"))
        + (vector, rows, rows, rows, rows, vector, rows, rows, rows),
        out_specs=(cells, cells, vector, rows, rows, rows, rows, vector, rows, rows, rows),
        check_vma=False,
    )
```

time: 1000 us -> 669 us (0.67)
  waiting for transfers between devices: 457 us -> 256 us
  Pallas kernels: 0 us -> 195 us
  matrix products: 161 us -> 0 us
  other arithmetic: 109 us -> 35 us
  blocking collectives: 54.8 us -> 0 us
  local copies, waits for them, and re-layouts: 132 us -> 93.2 us
    pallas_call x0 -> x20, Pallas kernels: none -> 195 us  [the longest x6 46.3 us: turned(): pl.pallas_call(functools.partial(turned_kernel, len(arrived)), grid=(widt...]
    dot_general x18 -> x0, matrix products: 161 us -> none  [the longest x4 56.1 us: matmul_cols(): return lax.dot_general(left, right, COLS_DIMS, preferred_element_type=F32)]
    all_gather x4, waiting for transfers between devices: 128 us -> 19 us  [batch_gather(): return lax.all_gather(value, 'batch', axis=axis, tiled=True)]
    psum x1 -> x0, blocking collectives: 54.8 us -> none  [per_device(): group_total = lax.psum(jnp.sum(onehot, axis=0), 'seq')]
    reduce_scatter x4, waiting for transfers between devices: 74.6 us -> 23.2 us  [batch_scatter(): return lax.psum_scatter(value, 'batch', scatter_dimension=axis, tiled=True)]
    ppermute x46 -> x64, waiting for transfers between devices: 253 us -> 214 us  [exchange(): lax.ppermute(value, 'seq', [(place, place ^ flip) for place in range(coun...]
    reshape x20 -> x0, local copies, waits for them, and re-layouts: 36.3 us -> none  [the longest x2 6.67 us: from_own(): return jnp.concatenate([first, second], axis=-2).reshape(values.shape)]
    unnamed x150 -> x177, local copies, waits for them, and re-layouts: 22.4 us -> 55.2 us
  transfers between devices with their start and end apart: 54 -> 72, of which waited for: 29 -> 44; matrix products, arithmetic and copies ran while one was open for 33% -> 12% of each run, Pallas kernels for 0% -> 30%
where the time goes in v2:
time: 669 us; the launch traced here: 659 us
  waiting for transfers between devices  256 us (38%)
  Pallas kernels  195 us (29%)
  local copies, waits for them, and re-layouts  93.2 us (14%)
  starting transfers between devices  63.1 us (9%)
  other arithmetic  35 us (5%)
  between operations  15.9 us (2%)
    ppermute x64, waiting for transfers between devices, exchange(): lax.ppermute(value, 'seq', [(place, place ^ flip) for place in range(coun...  214 us
    ppermute x64, starting transfers between devices, exchange(): lax.ppermute(value, 'seq', [(place, place ^ flip) for place in range(coun...  62.4 us
    unnamed x177, local copies, waits for them, and re-layouts  55.2 us
    pallas_call x6, Pallas kernels, turned(): pl.pallas_call(functools.partial(turned_kernel, len(arrived)), grid=(widt...  46.3 us
    pallas_call x2, Pallas kernels, back_project(): pl.pallas_call(back_project_kernel, grid=(chips,), in_specs=[pl.BlockSpec...  35.8 us
    reduce_scatter x4, waiting for transfers between devices, batch_scatter(): return lax.psum_scatter(value, 'batch', scatter_dimension=axis, tiled=True)  23.2 us
    all_gather x4, waiting for transfers between devices, batch_gather(): return lax.all_gather(value, 'batch', axis=axis, tiled=True)  19 us
    pallas_call x1, Pallas kernels, attention_back(): pl.pallas_call(attend_back_kernel, grid=(chips,), in_specs=[SCALAR, SCALA...  16.4 us
  transfers between devices with their start and end apart: 72, of which 44 were waited for; matrix products, arithmetic and copies ran while one was open for 12% of the time, Pallas kernels for 30%

profile of v2, /device:TPU:0, one launch (start us, length us, event | category | flops | bytes accessed | tf_op | source)
XLA Modules:
  0.0 659.1 jit_solution(8145590408865903384)
XLA Ops:
  31.9 13.8 %all-gather.5.cloned.1.call-done = bf16[256,2048]{1,0:T(8,128)(2,1)} async-done(((bf16[64,2048]{1,0:T(8,128)(2,1)}), bf16[256,2048]{1,0:T(8,128)(2,1)}) %all-gather.5.cloned.1.call-update) | async-done | bytes 1048592 | tf_op jit(solution)/shard_map/all_gather | solution.py:182
  45.8 6.9 %collective-permute-done.6 = bf16[256,2048]{1,0:T(8,128)(2,1)S(1)} collective-permute-done((bf16[256,2048]{1,0:T(8,128)(2,1)S(1)}, bf16[256,2048]{1,0:T(8,128)(2,1)S(1)}, u32[]{:S(2)}, u32[]{:S(2)}) %collective-permute-start.6) | collective-permute-done | bytes 1048608 | tf_op jit(solution)/shard_map/ppermute | solution.py:40
  56.5 8.8 %collective-permute-done.8 = bf16[128,2048]{1,0:T(8,128)(2,1)} collective-permute-done((bf16[128,2048]{1,0:T(8,128)(2,1)}, bf16[128,2048]{1,0:T(8,128)(2,1)}, u32[]{:S(2)}, u32[]{:S(2)}) %collective-permute-start.8) | collective-permute-done | bytes 524320 | tf_op jit(solution)/shard_map/ppermute | solution.py:40
  72.4 7.4 %collective-permute-done.10 = bf16[64,2816]{1,0:T(8,128)(2,1)S(1)} collective-permute-done((bf16[64,2816]{1,0:T(8,128)(2,1)S(1)}, bf16[64,2816]{1,0:T(8,128)(2,1)S(1)}, u32[]{:S(2)}, u32[]{:S(2)}) %collective-permute-start.10) | collective-permute-done | bytes 360480 | tf_op jit(solution)/shard_map/ppermute | solution.py:40
  87.6 21.1 %collective-permute-done.13 = bf16[256,2048]{1,0:T(8,128)(2,1)S(1)} collective-permute-done((bf16[256,2048]{1,0:T(8,128)(2,1)}, bf16[256,2048]{1,0:T(8,128)(2,1)S(1)}, u32[]{:S(2)}, u32[]{:S(2)}) %collective-permute-start.13) | collective-permute-done | bytes 1048608 | tf_op jit(solution)/shard_map/ppermute | solution.py:40
  143.0 12.3 %shard_map.203 = (bf16[1024,2048]{1,0:T(8,128)(2,1)S(1)}, bf16[1024,1536]{1,0:T(8,128)(2,1)S(1)}) custom-call(s32[1]{0:T(128)} %bitcast.core.flag, bf16[1024,2048]{1,0:T(8,128)(2,1)} %constant_dynamic-update-slice_fusion.tokens, f32[1,2048]{1,0:T(1,128)S(1)} %maximum_convert_fusion.5.gain.refs_6_, bf16[1024,1664]{1,0:T(8,128)(2,1)S(1)} %bitcast.158, ...), custom_call_target="tpu_custom_call" | custom-call | tf_op jit(solution)/shard_map/pallas_call | solution.py:239
  168.8 11.1 %shard_map.204 = bf16[4,256,512]{2,1,0:T(8,128)(2,1)S(1)} custom-call(s32[1]{0:T(128)} %bitcast.core.flag, s32[4]{0:T(128)S(1)} %or_convert_fusion.preceded, bf16[4,256,1536]{2,1,0:T(8,128)(2,1)S(1)} %bitcast.160, bf16[4,64,1024]{2,1,0:T(8,128)(2,1)S(1)} %broadcast_select_fusion.rim), custom_call_target="tpu_custom_call" | custom-call | tf_op jit(solution)/shard_map/pallas_call | solution.py:316
  206.5 22.5 %collective-permute-done.27 = bf16[256,2048]{1,0:T(8,128)(2,1)S(1)} collective-permute-done((bf16[256,2048]{1,0:T(8,128)(2,1)S(1)}, bf16[256,2048]{1,0:T(8,128)(2,1)S(1)}, u32[]{:S(2)}, u32[]{:S(2)}) %collective-permute-start.27) | collective-permute-done | bytes 1048608 | tf_op jit(solution)/shard_map/ppermute | solution.py:40
  233.1 9.9 %collective-permute-done.29 = bf16[128,2048]{1,0:T(8,128)(2,1)} collective-permute-done((bf16[128,2048]{1,0:T(8,128)(2,1)}, bf16[128,2048]{1,0:T(8,128)(2,1)}, u32[]{:S(2)}, u32[]{:S(2)}) %collective-permute-start.29) | collective-permute-done | bytes 524320 | tf_op jit(solution)/shard_map/ppermute | solution.py:40
  252.6 9.8 %shard_map.206.first = f32[1024,2816]{1,0:T(8,128)S(1)} custom-call(bf16[1024,2048]{1,0:T(8,128)(2,1)S(1)} %constant_dynamic-update-slice_fusion.10.act.left, bf16[1024,2816]{1,0:T(8,128)(2,1)S(1)} %bitcast.149, bf16[1024,2816]{1,0:T(8,128)(2,1)S(1)} %bitcast.150), custom_call_target="tpu_custom_call" | custom-call | tf_op jit(solution)/shard_map/pallas_call | solution.py:643
  266.6 13.8 %shard_map.207 = (bf16[1024,1408]{1,0:T(8,128)(2,1)S(1)}, f32[1024,1408]{1,0:T(8,128)S(1)}, f32[1024,1408]{1,0:T(8,128)S(1)}) custom-call(bf16[1024,2048]{1,0:T(8,128)(2,1)S(1)} %constant_dynamic-update-slice_fusion.10.act.left, bf16[1024,2816]{1,0:T(8,128)(2,1)} %collective-permute-done.31.gate.upward.other, ...), custom_call_target="tpu_custom_call" | custom-call | tf_op jit(solution)/shard_map/pallas_call | solution.py:665
  312.3 12.4 %shard_map.210.right.d_out = bf16[1024,2816]{1,0:T(8,128)(2,1)} custom-call(s32[1]{0:T(128)} %bitcast.core.flag, bf16[1024,2048]{1,0:T(8,128)(2,1)S(1)} %copy-done.7, bf16[704,2048]{1,0:T(8,128)(2,1)S(1)} %copy-done.22, bf16[704,2048]{1,0:T(8,128)(2,1)} %collective-permute-done.33.other, f32[1024,1408]{1,0:T(8,128)} %copy-done.35, f32[1024,1408]{1,0:T(8,128)} %copy-done.36), custom_call_target="tpu_custom_call" | custom-call | tf_op jit(solution)/shard_map/pallas_call | solution.py:706
  327.4 10.3 %shard_map.211 = bf16[1024,2816]{1,0:T(8,128)(2,1)} custom-call(bf16[1024,2048]{1,0:T(8,128)(2,1)S(1)} %copy-done.1, bf16[1024,2816]{1,0:T(8,128)(2,1)S(1)} %copy-done.3), custom_call_target="tpu_custom_call" | custom-call | tf_op jit(solution)/shard_map/pallas_call | solution.py:779
  338.0 21.4 %shard_map.212 = (f32[1,2048]{1,0:T(1,128)}, bf16[256,2048]{1,0:T(8,128)(2,1)S(1)}, bf16[2,128,2048]{2,1,0:T(8,128)(2,1)}, bf16[2,128,2048]{2,1,0:T(8,128)(2,1)}...) custom-call(bf16[1024,2816]{1,0:T(8,128)(2,1)} %shard_map.210.right.d_out, bf16[1024,2816]{1,0:T(8,128)(2,1)} %bitcast.146, ...), custom_call_target="tpu_custom_call" | custom-call | tf_op jit(solution)/shard_map/pallas_call | solution.py:741
  368.2 11.3 %shard_map.222 = bf16[1024,2816]{1,0:T(8,128)(2,1)S(1)} custom-call(bf16[1024,2048]{1,0:T(8,128)(2,1)S(1)} %copy-done.2, bf16[1024,2816]{1,0:T(8,128)(2,1)S(1)} %copy-done.4, bf16[1024,2816]{1,0:T(8,128)(2,1)} %collective-permute-done.57.refs_0_), custom_call_target="tpu_custom_call" | custom-call | tf_op jit(solution)/shard_map/pallas_call | solution.py:779
  395.4 7.2 %collective-permute-done.36.refs_3_ = bf16[128,2048]{1,0:T(8,128)(2,1)S(1)} collective-permute-done((bf16[128,2048]{1,0:T(8,128)(2,1)S(1)}, bf16[128,2048]{1,0:T(8,128)(2,1)S(1)}, u32[]{:S(2)}, u32[]{:S(2)}) %collective-permute-start.36) | collective-permute-done | bytes 524320 | tf_op jit(solution)/shard_map/ppermute | solution.py:40
  421.6 11.2 %shard_map.214 = (bf16[256,2048]{1,0:T(8,128)(2,1)S(1)}, bf16[2,128,2048]{2,1,0:T(8,128)(2,1)}, bf16[2,128,2048]{2,1,0:T(8,128)(2,1)}, bf16[128,2048]{1,0:T(8,128)(2,1)S(1)}, bf16[128,2048]{1,0:T(8,128)(2,1)S(1)}) custom-call(s32[1]{0:T(128)} %bitcast.core.flag, bf16[1024,1408]{1,0:T(8,128)(2,1)S(1)} %get-tuple-element.130.left, ...), custom_call_target="tpu_custom_call" | custom-call | tf_op jit(solution)/shard_map/pallas_call | solution.py:817
  434.9 16.4 %shard_map.215 = (bf16[4,256,1536]{2,1,0:T(8,128)(2,1)S(1)}, bf16[4,64,1024]{2,1,0:T(8,128)(2,1)}) custom-call(s32[1]{0:T(128)} %bitcast.core.flag, s32[4]{0:T(128)S(1)} %or_convert_fusion.preceded, bf16[4,256,1536]{2,1,0:T(8,128)(2,1)S(1)} %bitcast.161, bf16[4,64,1024]{2,1,0:T(8,128)(2,1)S(1)} %copy-done.38, bf16[4,256,512]{2,1,0:T(8,128)(2,1)S(1)} %pad_maximum_fusion.2.d_mixed), custom_call_target="tpu_custom_call" | custom-call | tf_op jit(solution)/shard_map/pallas_call | solution.py:385
  500.1 14.4 %shard_map.220 = (f32[1,2048]{1,0:T(1,128)S(1)}, bf16[256,2048]{1,0:T(8,128)(2,1)S(1)}, bf16[2,128,2048]{2,1,0:T(8,128)(2,1)}, bf16[2,128,2048]{2,1,0:T(8,128)(2...) custom-call(bf16[1024,1536]{1,0:T(8,128)(2,1)} %bitcast.153, bf16[1024,1664]{1,0:T(8,128)(2,1)} %bitcast.156, ...), custom_call_target="tpu_custom_call" | custom-call | tf_op jit(solution)/shard_map/pallas_call | solution.py:741
  524.2 16.3 %collective-permute-done.50 = bf16[2,128,2048]{2,1,0:T(8,128)(2,1)S(1)} collective-permute-done((bf16[2,128,2048]{2,1,0:T(8,128)(2,1)S(1)}, bf16[2,128,2048]{2,1,0:T(8,128)(2,1)S(1)}, u32[]{:S(2)}, u32[]{:S(2)}) %collective-permute-start.50) | collective-permute-done | bytes 1048608 | tf_op jit(solution)/shard_map/ppermute | solution.py:40
  560.8 15.7 %collective-permute-done.52 = bf16[2,128,2048]{2,1,0:T(8,128)(2,1)} collective-permute-done((bf16[2,128,2048]{2,1,0:T(8,128)(2,1)}, bf16[2,128,2048]{2,1,0:T(8,128)(2,1)}, u32[]{:S(2)}, u32[]{:S(2)}) %collective-permute-start.52) | collective-permute-done | bytes 1048608 | tf_op jit(solution)/shard_map/ppermute | solution.py:40
  588.5 8.1 %collective-permute-done.54.refs_3_ = bf16[128,2048]{1,0:T(8,128)(2,1)S(1)} collective-permute-done((bf16[128,2048]{1,0:T(8,128)(2,1)S(1)}, bf16[128,2048]{1,0:T(8,128)(2,1)S(1)}, u32[]{:S(2)}, u32[]{:S(2)}) %collective-permute-start.54) | collective-permute-done | bytes 524320 | tf_op jit(solution)/shard_map/ppermute | solution.py:40
  608.9 7.7 %reduce-scatter.9.cloned.1.call-done = bf16[4,64,1664]{2,1,0:T(8,128)(2,1)} async-done(((bf16[4,256,1664]{2,1,0:T(8,128)(2,1)}), bf16[4,64,1664]{2,1,0:T(8,128)(2,1)}) %reduce-scatter.9.cloned.1.call-update) | async-done | bytes 851984 | tf_op jit(solution)/shard_map/reduce_scatter | solution.py:186
  634.6 15.5 %reduce-scatter.11.cloned.1.call-done = bf16[64,2048]{1,0:T(8,128)(2,1)} async-done(((bf16[256,2048]{1,0:T(8,128)(2,1)}), bf16[64,2048]{1,0:T(8,128)(2,1)}) %reduce-scatter.11.cloned.1.call-update) | async-done | bytes 262160 | tf_op jit(solution)/shard_map/reduce_scatter | solution.py:186
  (429 shorter events, 337.9 us)
Async XLA Ops:
  7.2 38.5 %all-gather.5.cloned.1.call-start = ((), (), s32[]{:S(2)}) async-start(), calls=%async_computation.4 | async-start | bytes 1310720 | tf_op jit(solution)/shard_map/all_gather | solution.py:182
  15.9 98.7 %all-gather.7.cloned.1.call-start = ((), (), s32[]{:S(2)}) async-start(), calls=%async_computation.5 | async-start | bytes 4259840 | tf_op jit(solution)/shard_map/all_gather | solution.py:182
  45.7 187.4 %all-gather.9.cloned.1.call-start = ((), (), s32[]{:S(2)}) async-start(), calls=%async_computation.6 | async-start | bytes 7208960 | tf_op jit(solution)/shard_map/all_gather | solution.py:182
  85.1 23.5 %collective-permute-start.13 = (bf16[256,2048]{1,0:T(8,128)(2,1)}, bf16[256,2048]{1,0:T(8,128)(2,1)S(1)}, u32[]{:S(2)}, u32[]{:S(2)}) collective-permute-start(bf16[256,2048]{1,0:T(8,128)(2,1)} %all-gather.5.cloned.1.call-done), channel_id=1, source_target_pairs={{0,8},{4,12},{8,0},{12,4},{16,24},{20,28},{24,16},{28,20},{1,9},{5... | collective-permute-start | bytes 3145736 | tf_op jit(solution)/shard_map/ppermute | solution.py:40
  114.6 27.0 %collective-permute-start.15 = (bf16[1024,1664]{1,0:T(8,128)(2,1)}, bf16[1024,1664]{1,0:T(8,128)(2,1)}, u32[]{:S(2)}, u32[]{:S(2)}) collective-permute-start(bf16[1024,1664]{1,0:T(8,128)(2,1)} %bitcast.155), channel_id=1, source_target_pairs={{0,4},{4,0},{8,12},{12,8},{16,20},{20,16},{24,28},{28,24},{1,5},{5... | collective-permute-start | bytes 10223624 | tf_op jit(solution)/shard_map/ppermute | solution.py:40
  124.6 177.7 %all-gather.11.cloned.1.call-start = ((), (), s32[]{:S(2)}) async-start(), calls=%async_computation.7 | async-start | bytes 3604480 | tf_op jit(solution)/shard_map/all_gather | solution.py:182
  135.4 24.7 %collective-permute-start.19 = (bf16[256,2048]{1,0:T(8,128)(2,1)}, bf16[256,2048]{1,0:T(8,128)(2,1)S(1)}, u32[]{:S(2)}, u32[]{:S(2)}) collective-permute-start(bf16[256,2048]{1,0:T(8,128)(2,1)} %get-tuple-element.106), channel_id=1, source_target_pairs={{0,8},{4,12},{8,0},{12,4},{16,24},{20,28},{24,16},{28,20},{1,9},{5... | collective-permute-start | bytes 3145736 | tf_op jit(solution)/shard_map/ppermute | solution.py:40
  136.9 24.6 %collective-permute-start.20 = (bf16[256,2048]{1,0:T(8,128)(2,1)}, bf16[256,2048]{1,0:T(8,128)(2,1)S(1)}, u32[]{:S(2)}, u32[]{:S(2)}) collective-permute-start(bf16[256,2048]{1,0:T(8,128)(2,1)} %get-tuple-element.106), channel_id=1, source_target_pairs={{0,16},{4,20},{8,24},{12,28},{16,0},{20,4},{24,8},{28,12},{1,17},{... | collective-permute-start | bytes 3145736 | tf_op jit(solution)/shard_map/ppermute | solution.py:40
  204.1 24.9 %collective-permute-start.27 = (bf16[256,2048]{1,0:T(8,128)(2,1)S(1)}, bf16[256,2048]{1,0:T(8,128)(2,1)S(1)}, u32[]{:S(2)}, u32[]{:S(2)}) collective-permute-start(bf16[256,2048]{1,0:T(8,128)(2,1)S(1)} %get-tuple-element.112), channel_id=1, source_target_pairs={{0,8},{4,12},{8,0},{12,4},{16,24},{20,28},{24,16},{28,20},{1,9},{5... | collective-permute-start | bytes 3145736 | tf_op jit(solution)/shard_map/ppermute | solution.py:40
  205.0 25.4 %collective-permute-start.28 = (bf16[256,2048]{1,0:T(8,128)(2,1)S(1)}, bf16[256,2048]{1,0:T(8,128)(2,1)S(1)}, u32[]{:S(2)}, u32[]{:S(2)}) collective-permute-start(bf16[256,2048]{1,0:T(8,128)(2,1)S(1)} %get-tuple-element.112), channel_id=1, source_target_pairs={{0,16},{4,20},{8,24},{12,28},{16,0},{20,4},{24,8},{28,12},{1,17},{... | collective-permute-start | bytes 3145736 | tf_op jit(solution)/shard_map/ppermute | solution.py:40
  244.5 118.9 %reduce-scatter.5.cloned.1.call-start = ((), (), s32[]{:S(2)}) async-start(), calls=%async_computation.8 | async-start | bytes 3604480 | tf_op jit(solution)/shard_map/reduce_scatter | solution.py:186
  302.8 251.6 %reduce-scatter.7.cloned.1.call-start = ((), (), s32[]{:S(2)}) async-start(), calls=%async_computation.9 | async-start | bytes 7208960 | tf_op jit(solution)/shard_map/reduce_scatter | solution.py:186
  337.7 25.7 %collective-permute-start.57 = (bf16[1024,2816]{1,0:T(8,128)(2,1)}, bf16[1024,2816]{1,0:T(8,128)(2,1)}, u32[]{:S(2)}, u32[]{:S(2)}) collective-permute-start(bf16[1024,2816]{1,0:T(8,128)(2,1)} %shard_map.211), channel_id=1, source_target_pairs={{0,4},{4,0},{8,12},{12,8},{16,20},{20,16},{24,28},{28,24},{1,5},{5... | collective-permute-start | bytes 17301512 | tf_op jit(solution)/shard_map/ppermute | solution.py:40
  361.2 25.5 %collective-permute-start.34 = (bf16[2,128,2048]{2,1,0:T(8,128)(2,1)}, bf16[2,128,2048]{2,1,0:T(8,128)(2,1)}, u32[]{:S(2)}, u32[]{:S(2)}) collective-permute-start(bf16[2,128,2048]{2,1,0:T(8,128)(2,1)} %get-tuple-element.125), channel_id=1, source_target_pairs={{0,8},{4,12},{8,0},{12,4},{16,24},{20,28},{24,16},{28,20},{1,9},{5... | collective-permute-start | bytes 3145736 | tf_op jit(solution)/shard_map/ppermute | solution.py:40
  362.6 25.3 %collective-permute-start.35 = (bf16[2,128,2048]{2,1,0:T(8,128)(2,1)}, bf16[2,128,2048]{2,1,0:T(8,128)(2,1)}, u32[]{:S(2)}, u32[]{:S(2)}) collective-permute-start(bf16[2,128,2048]{2,1,0:T(8,128)(2,1)} %get-tuple-element.126), channel_id=1, source_target_pairs={{0,16},{4,20},{8,24},{12,28},{16,0},{20,4},{24,8},{28,12},{1,17},{... | collective-permute-start | bytes 3145736 | tf_op jit(solution)/shard_map/ppermute | solution.py:40
  387.9 228.7 %reduce-scatter.9.cloned.1.call-start = ((), (), s32[]{:S(2)}) async-start(), calls=%async_computation.10 | async-start | bytes 4259840 | tf_op jit(solution)/shard_map/reduce_scatter | solution.py:186
  432.8 24.6 %collective-permute-start.39 = (bf16[2,128,2048]{2,1,0:T(8,128)(2,1)}, bf16[2,128,2048]{2,1,0:T(8,128)(2,1)}, u32[]{:S(2)}, u32[]{:S(2)}) collective-permute-start(bf16[2,128,2048]{2,1,0:T(8,128)(2,1)} %get-tuple-element.133), channel_id=1, source_target_pairs={{0,16},{4,20},{8,24},{12,28},{16,0},{20,4},{24,8},{28,12},{1,17},{... | collective-permute-start | bytes 3145736 | tf_op jit(solution)/shard_map/ppermute | solution.py:40
  433.6 23.8 %collective-permute-start.38 = (bf16[2,128,2048]{2,1,0:T(8,128)(2,1)}, bf16[2,128,2048]{2,1,0:T(8,128)(2,1)}, u32[]{:S(2)}, u32[]{:S(2)}) collective-permute-start(bf16[2,128,2048]{2,1,0:T(8,128)(2,1)} %get-tuple-element.132), channel_id=1, source_target_pairs={{0,8},{4,12},{8,0},{12,4},{16,24},{20,28},{24,16},{28,20},{1,9},{5... | collective-permute-start | bytes 3145736 | tf_op jit(solution)/shard_map/ppermute | solution.py:40
  497.5 25.3 %collective-permute-start.48 = (bf16[2,128,2048]{2,1,0:T(8,128)(2,1)S(1)}, bf16[2,128,2048]{2,1,0:T(8,128)(2,1)S(1)}, u32[]{:S(2)}, u32[]{:S(2)}) collective-permute-start(bf16[2,128,2048]{2,1,0:T(8,128)(2,1)S(1)} %get-tuple-element.157), channel_id=1, source_target_pairs={{0,8},{4,12},{8,0},{12,4},{16,24},{20,28},{24,16},{28,20},{1,9},{5... | collective-permute-start | bytes 3145736 | tf_op jit(solution)/shard_map/ppermute | solution.py:40
  514.5 26.0 %collective-permute-start.50 = (bf16[2,128,2048]{2,1,0:T(8,128)(2,1)S(1)}, bf16[2,128,2048]{2,1,0:T(8,128)(2,1)S(1)}, u32[]{:S(2)}, u32[]{:S(2)}) collective-permute-start(bf16[2,128,2048]{2,1,0:T(8,128)(2,1)S(1)} %get-tuple-element.159), channel_id=1, source_target_pairs={{0,16},{4,20},{8,24},{12,28},{16,0},{20,4},{24,8},{28,12},{1,17},{... | collective-permute-start | bytes 3145736 | tf_op jit(solution)/shard_map/ppermute | solution.py:40
  516.6 25.2 %collective-permute-start.56 = (bf16[1024,128]{1,0:T(8,128)(2,1)S(1)}, bf16[1024,128]{1,0:T(8,128)(2,1)S(1)}, u32[]{:S(2)}, u32[]{:S(2)}) collective-permute-start(bf16[1024,128]{1,0:T(8,128)(2,1)S(1)} %fusion.12), channel_id=1, source_target_pairs={{0,4},{4,0},{8,12},{12,8},{16,20},{20,16},{24,28},{28,24},{1,5},{5... | collective-permute-start | bytes 786440 | tf_op jit(solution)/shard_map/ppermute | solution.py:40
  522.9 27.7 %collective-permute-start.49 = (bf16[128,2048]{1,0:T(8,128)(2,1)S(1)}, bf16[128,2048]{1,0:T(8,128)(2,1)S(1)}, u32[]{:S(2)}, u32[]{:S(2)}) collective-permute-start(bf16[128,2048]{1,0:T(8,128)(2,1)S(1)} %fusion.4), channel_id=1, source_target_pairs={{0,16},{4,20},{8,24},{12,28},{16,0},{20,4},{24,8},{28,12},{1,17},{... | collective-permute-start | bytes 1572872 | tf_op jit(solution)/shard_map/ppermute | solution.py:40
  554.4 95.6 %reduce-scatter.11.cloned.1.call-start = ((), (), s32[]{:S(2)}) async-start(), calls=%async_computation.11 | async-start | bytes 1310720 | tf_op jit(solution)/shard_map/reduce_scatter | solution.py:186
  555.6 24.2 %collective-permute-start.53 = (bf16[2,128,2048]{2,1,0:T(8,128)(2,1)}, bf16[2,128,2048]{2,1,0:T(8,128)(2,1)}, u32[]{:S(2)}, u32[]{:S(2)}) collective-permute-start(bf16[2,128,2048]{2,1,0:T(8,128)(2,1)} %copy-done.51), channel_id=1, source_target_pairs={{0,16},{4,20},{8,24},{12,28},{16,0},{20,4},{24,8},{28,12},{1,17},{... | collective-permute-start | bytes 3145736 | tf_op jit(solution)/shard_map/ppermute | solution.py:40
  (125 other events, 1534.2 us)
Sparse Core Ops, SparseCore 0:
  16.0 29.6 all-gather.4
  47.3 67.2 all-gather.6
  124.7 103.5 all-gather.8
  244.6 56.9 all-gather.10
  303.8 54.8 reduce-scatter.4
  388.1 99.8 reduce-scatter.6
  554.5 62.0 reduce-scatter.8
  622.7 27.3 reduce-scatter.10

commit v3 on v2

--- a/solution.py
+++ b/solution.py
@@ -35,9 +35,11 @@
     return lax.dot_general(left, right, COLS_DIMS, preferred_element_type=F32)
 
 
-def exchange(value, flip):
-    count = lax.axis_size("seq")
-    return lax.ppermute(value, "seq", [(place, place ^ flip) for place in range(count)])
+def exchange(value, flip, axis="seq"):
+    if flip == 0:
+        return value
+    count = lax.axis_size(axis)
+    return lax.ppermute(value, axis, [(place, place ^ flip) for place in range(count)])
 
 
 def swap_core(value):
@@ -125,6 +127,20 @@
     if block == 3:
         first[1, :, place] = value[:low]
         second[1, :, place] = value[low:]
+
+
+def spread(total, outs):
+    if len(outs) == 1:
+        outs[0][...] = total
+        return
+    tall = total.shape[0] // 4
+    for block in range(4):
+        spread_block(block, total[block * tall : (block + 1) * tall], outs)
+
+
+def column_spec(shape, tile):
+    lead = (0,) * (len(shape) - 1)
+    return pl.BlockSpec(shape[:-1] + (tile,), lambda i: lead + (i,))
 
 
 def spread_step(step, value, outs, place=slice(None)):
@@ -610,18 +626,18 @@
 
 
 def inner_first_kernel(act, gate, upward, out):
-    out[...] = matmul(act[...], jnp.concatenate([gate[...], upward[...]], axis=1))
+    out[...] = matmul(act[...], jnp.concatenate([gate[...], upward[...]], axis=1)).astype(LOW)
 
 
 def inner_second_kernel(act, gate, upward, first, hidden, slope_gate, slope_up):
     width = gate.shape[1]
-    both = first[...] + matmul(act[...], jnp.concatenate([gate[...], upward[...]], axis=1))
+    both = first[...].astype(F32) + matmul(act[...], jnp.concatenate([gate[...], upward[...]], axis=1))
     gate, upward = both[:, :width], both[:, width:]
     sigma = jax.nn.sigmoid(gate)
     silu = gate * sigma
     hidden[...] = (silu * upward).astype(LOW)
-    slope_gate[...] = upward * sigma * (1.0 + gate * (1.0 - sigma))
-    slope_up[...] = silu
+    slope_gate[...] = (upward * sigma * (1.0 + gate * (1.0 - sigma))).astype(LOW)
+    slope_up[...] = silu.astype(LOW)
 
 
 def inner_specs(act, weights, part):
@@ -638,14 +654,14 @@
 def inner_first(act, weights):
     rows, columns = act.shape[0], weights.shape[1]
     if columns % (2 * LANES):
-        return matmul(act[:, : weights.shape[0]], weights)
+        return matmul(act[:, : weights.shape[0]], weights).astype(LOW)
     tiles, specs = inner_specs(act, weights, 0)
     return pl.pallas_call(
         inner_first_kernel,
         grid=(tiles,),
         in_specs=specs,
         out_specs=pl.BlockSpec((rows, 2 * LANES), lambda i: (0, i)),
-        out_shape=jax.ShapeDtypeStruct((rows, columns), F32),
+        out_shape=jax.ShapeDtypeStruct((rows, columns), LOW),
         compiler_params=params(),
         cost_estimate=FREE,
     )(act, weights, weights)
@@ -655,11 +671,12 @@
     rows, columns = act.shape[0], weights.shape[1]
     width = columns // 2
     if columns % (2 * LANES):
-        both = first + matmul(act[:, weights.shape[0] :], weights)
+        both = first.astype(F32) + matmul(act[:, weights.shape[0] :], weights)
         gate, upward = both[:, :width], both[:, width:]
         sigma = jax.nn.sigmoid(gate)
         silu = gate * sigma
-        return (silu * upward).astype(LOW), upward * sigma * (1.0 + gate * (1.0 - sigma)), silu
+        slope = upward * sigma * (1.0 + gate * (1.0 - sigma))
+        return (silu * upward).astype(LOW), slope.astype(LOW), silu.astype(LOW)
     tiles, specs = inner_specs(act, weights, 1)
     tile = pl.BlockSpec((rows, LANES), lambda i: (0, i))
     return pl.pallas_call(
@@ -667,11 +684,7 @@
         grid=(tiles,),
         in_specs=specs + [pl.BlockSpec((rows, 2 * LANES), lambda i: (0, i))],
         out_specs=[tile] * 3,
-        out_shape=[
-            jax.ShapeDtypeStruct((rows, width), LOW),
-            jax.ShapeDtypeStruct((rows, width), F32),
-            jax.ShapeDtypeStruct((rows, width), F32),
-        ],
+        out_shape=[jax.ShapeDtypeStruct((rows, width), LOW)] * 3,
         compiler_params=params(),
         cost_estimate=FREE,
     )(act, weights, weights, first)
@@ -717,44 +730,55 @@
         out_specs=pl.BlockSpec((tall, 2 * width), lambda i: (i, 0)),
         out_shape=jax.ShapeDtypeStruct((rows, 2 * width), LOW),
         scratch_shapes=[pltpu.VMEM((width, features), LOW)],
-        compiler_params=params(44),
+        compiler_params=params(60),
         cost_estimate=FREE,
     )(flag, d_ffn, mine, other, slope_gate, slope_up)
 
 
-def back_project_kernel(d_out, mine, other, act, total, *outs):
-    half, columns = mine.shape[0], d_out.shape[1]
+def back_project_kernel(tiles, chips, d_out, mine, other, *refs):
+    act, outs, total = (refs[0], refs[1:-1], refs[-1]) if chips == 0 else (None, refs, None)
     step = pl.program_id(0)
-    for place, weights in ((slice(0, half), mine), (slice(half, 2 * half), other)):
+    columns = d_out.shape[1]
+
+    def work(weights):
         grad = matmul_cols(d_out[...], weights[:, :columns])
-        spread_step(step, grad.astype(LOW), outs, place)
-        part = jnp.sum(grad * act[:, place].astype(F32), axis=0, keepdims=True)
-        total[:, place] = part + jnp.where(step > 0, total[:, place], 0.0)
-
-
-def back_project(d_out, mine, other, act, chips):
+        if act is not None:
+            total[...] = jnp.sum(grad * act[...].astype(F32), axis=0, keepdims=True)
+        spread(grad.astype(LOW), outs)
+
+    @pl.when(step < tiles)
+    def _():
+        work(mine)
+
+    @pl.when(step >= tiles)
+    def _():
+        work(other)
+
+
+def back_project(d_out, mine, other, chips, *act):
     rows, columns = d_out.shape
-    features = 2 * mine.shape[0]
-    tall = rows // chips
-    shapes = spread_shapes(chips, rows, features)
-    flat = pl.BlockSpec((tall, features), lambda i: (i, 0))
-    total, *outs = pl.pallas_call(
-        back_project_kernel,
-        grid=(chips,),
+    half = mine.shape[0]
+    tile = 2 * LANES
+    tiles = half // tile
+    shapes = spread_shapes(chips, rows, 2 * half)
+    flat = pl.BlockSpec((rows, tile), lambda i: (0, i))
+    outs = pl.pallas_call(
+        functools.partial(back_project_kernel, tiles, 0 if act else 1),
+        grid=(2 * tiles,),
         in_specs=[
-            pl.BlockSpec((tall, columns), lambda i: (i, 0)),
-            whole(mine.shape),
-            whole(other.shape),
-            flat,
-        ],
-        out_specs=[whole((1, features))]
-        + ([flat] if len(shapes) == 1 else [whole(shape) for shape in shapes]),
-        out_shape=[jax.ShapeDtypeStruct((1, features), F32)]
-        + [jax.ShapeDtypeStruct(shape, LOW) for shape in shapes],
-        compiler_params=params(48),
-        cost_estimate=FREE,
-    )(d_out, mine, other, act)
-    return outs, total
+            whole(d_out.shape),
+            pl.BlockSpec((tile, mine.shape[1]), lambda i: (jnp.minimum(i, tiles - 1), 0)),
+            pl.BlockSpec((tile, mine.shape[1]), lambda i: (jnp.maximum(i - tiles, 0), 0)),
+        ]
+        + [flat for _ in act],
+        out_specs=[column_spec(shape, tile) for shape in shapes]
+        + [pl.BlockSpec((1, tile), lambda i: (0, i)) for _ in act],
+        out_shape=[jax.ShapeDtypeStruct(shape, LOW) for shape in shapes]
+        + [jax.ShapeDtypeStruct((1, 2 * half), F32) for _ in act],
+        compiler_params=params(40),
+        cost_estimate=FREE,
+    )(d_out, mine, other, *act)
+    return (outs[:-1], outs[-1]) if act else outs
 
 
 def turned_kernel(count, left, right, *refs):
@@ -762,13 +786,7 @@
     total = matmul_rows(left[...], right[...])
     if arrived:
         total = total + arrived[0][...].astype(F32)
-    total = total.astype(LOW)
-    if len(outs) == 1:
-        outs[0][...] = total
-        return
-    tall = total.shape[0] // 4
-    for block in range(4):
-        spread_block(block, total[block * tall : (block + 1) * tall], outs)
+    spread(total.astype(LOW), outs)
 
 
 def turned(left, part, right, *arrived, chips=1):
@@ -784,12 +802,9 @@
             pl.BlockSpec((rows, tile), lambda i: (0, i)),
         ]
         + [pl.BlockSpec((half, tile), lambda i: (0, i)) for _ in arrived],
-        out_specs=[
-            pl.BlockSpec(shape[:-1] + (tile,), lambda i, n=len(shape): (0,) * (n - 1) + (i,))
-            for shape in shapes
-        ],
+        out_specs=[column_spec(shape, tile) for shape in shapes],
         out_shape=[jax.ShapeDtypeStruct(shape, LOW) for shape in shapes],
-        compiler_params=params(),
+        compiler_params=params(60 if width > half * 2 else 32),
         cost_estimate=FREE,
     )(left, right, *arrived)
     return outs[0] if chips == 1 else outs
@@ -861,7 +876,7 @@
         + [pl.BlockSpec((half, tile), lambda i: (0, i)) for _ in arrived],
         out_specs=pl.BlockSpec((half, tile), lambda i: (0, i)),
         out_shape=jax.ShapeDtypeStruct((half, width), LOW),
-        compiler_params=params(),
+        compiler_params=params(60),
         cost_estimate=FREE,
     )(flag, left, right, *arrived)
 
@@ -918,20 +933,21 @@
     qkv_rows = rows_of_chips([query_weight, key_weight, value_weight], gains)
     qkv_mine = batch_gather(after(qkv_rows, out_mine), 1).reshape(half, -1)
     tokens_sent = after(tokens, qkv_rows, group_total)
-    tokens_near = gather_near(tokens_sent)
-    tokens_far = gather_far(tokens_near)
-    gathered = gathered_rows(tokens_sent, tokens_near, tokens_far)
-    gate_weight, up_weight = after((gate_weight, up_weight), *tokens_near, *tokens_far)
+    tokens_near = [exchange(tokens_sent, CORES * k) for k in range(1, chips)]
+    gathered = gathered_rows(tokens_sent, tokens_near, [])
+    gate_weight, up_weight = after((gate_weight, up_weight), gathered)
     inner_rows = rows_of_chips([gate_weight, up_weight])
     inner_mine = batch_gather(inner_rows, 1).reshape(half, -1)
     down_mine = batch_gather(after(down_weight, inner_rows), 0)
 
-    out_sent = after(out_mine, inner_rows)
+    ffn_sent = after(d_final.astype(LOW), inner_rows)
+    ffn_near = gather_near(ffn_sent)
+    qkv_mine = after(qkv_mine, *ffn_near)
+    ffn_far = gather_far(ffn_near)
+    out_sent = after(out_mine, *ffn_near)
     out_near = gather_near(out_sent)
-    qkv_mine = after(qkv_mine, *out_near)
     qkv_other = swap_core(qkv_mine)
     out_far = gather_far(out_near)
-    qkv_other = after(qkv_other, *out_far)
     columns = 3 * head_width
     gain_one, gain_two = (
         jnp.concatenate([qkv_mine[:, place], qkv_other[:, place]]).astype(F32)[None]
@@ -939,19 +955,16 @@
     )
     act_one, qkv = project(flag, gathered, gain_one, qkv_mine, qkv_other, columns, chips)
     qkv = qkv.reshape(chips, tok_count, columns)
-    ffn_sent = after(d_final.astype(LOW), *out_far)
-    ffn_near = gather_near(ffn_sent)
     place = chip ^ ids
     tails = swap_core(qkv[:, tok_count - WINDOW :, head_width:])
-    ffn_far = gather_far(ffn_near)
     before = jnp.where(core > 0, ids, chip ^ jnp.maximum(place - 1, 0))
     follow = jnp.where(core > 0, chip ^ jnp.minimum(place + 1, chips - 1), ids)
     preceded = ((core > 0) | (place > 0)).astype(jnp.int32)
     followed = (core == 0) | (place < chips - 1)
-    rims = jnp.take(after(tails, *ffn_near), before, axis=0)
+    rims = jnp.take(after(tails, *out_near), before, axis=0)
     mixed = attention(flag, preceded, qkv, rims)
 
-    mixed = after(mixed, *ffn_far)
+    mixed = after(mixed, *out_far, *ffn_far)
     mixed_own = chips_scatter([mixed[k] for k in range(chips)])
     cell = head_width // CORES
     mixed_own = jnp.concatenate(
@@ -964,28 +977,27 @@
         flag, mixed_own, out_half, out_other, tokens, gain_two, chips
     )
 
+    d_ffn = gathered_rows(ffn_sent, ffn_near, ffn_far)
+    act_two_own = after(act_two_own, d_ffn)
     act_near = gather_near(act_two_own)
-    act_far = gather_far(act_near)
+    act_far = gather_far(after(act_near, inner_mine))
     act_two = gathered_rows(act_two_own, act_near, act_far)
-    d_ffn = gathered_rows(ffn_sent, after(ffn_near, act_two_own), ffn_far)
-    inner_mine = after(inner_mine, *act_near, *act_far)
+    inner_mine = after(inner_mine, *act_near)
     inner_other = swap_core(inner_mine)
     hidden, slope_gate, slope_up = inner_second(
         act_two, inner_other, inner_first(act_two, inner_mine)
     )
     down_send = half_product(1 - flag, hidden, d_ffn)
     down_back = swap_core(down_send)
-    down_sum = half_product(flag, hidden, after(d_ffn, down_send), down_back)
-    down_mine = after(down_mine, down_sum)
+    down_mine = after(down_mine, down_send)
+    down_sum = half_product(flag, hidden, after(d_ffn, down_send, down_mine), down_back)
     down_other = swap_core(down_mine)
     down_grad = batch_scatter(down_sum, 0)
     d_gate_up = inner_back(
         flag, after(d_ffn, down_sum), down_mine, down_other, slope_gate, slope_up, chips
     )
     inner_send = turned(act_two, 1, d_gate_up)
-    act_parts, _ = back_project(
-        after(d_gate_up, inner_send), inner_mine, inner_other, act_two, chips
-    )
+    act_parts = back_project(after(d_gate_up, inner_send), inner_mine, inner_other, chips)
     act_near = chips_sum_near(act_parts)
     inner_sum = turned(
         act_two, 0, after(d_gate_up, act_parts[0], down_grad), swap_core(inner_send)
@@ -1017,31 +1029,37 @@
     block_far = chips_sum_far(block_parts, block_near)
     qkv_send = turned(act_one, 1, d_qkv)
     out_send = turned(mixed_own, 1, after(d_attn, qkv_send))
-    qkv_sum = turned(act_one, 0, after(d_qkv, out_send), swap_core(qkv_send))
+    d_act_parts, gain_one_part = back_project(
+        after(d_qkv, out_send), qkv_mine, qkv_other, chips, act_one
+    )
+    qkv_sum = turned(act_one, 0, after(d_qkv, d_act_parts[0]), swap_core(qkv_send))
     out_parts = turned(mixed_own, 0, after(d_attn, qkv_sum), swap_core(out_send), chips=chips)
     if chips == 1:
         out_parts = [out_parts]
-    out_parts = after(out_parts, *block_far)
+    d_act_near = after(chips_sum_near(d_act_parts), out_parts[0])
+    out_parts = after(out_parts, *d_act_near)
     out_near = chips_sum_near(out_parts)
-    out_far = chips_sum_far(out_parts, out_near)
-    d_act_parts, gain_one_part = back_project(
-        after(d_qkv, out_parts[0]), qkv_mine, qkv_other, act_one, chips
-    )
-    gain_one_part = gain_one_part / gain_one
-    gain_parts = jnp.concatenate(
-        [
-            jnp.broadcast_to(part.reshape(features, 1), (features, LANES // 2))
-            for part in (gain_one_part, gain_two_part)
-        ],
-        axis=1,
-    )
-    d_act_parts = after(d_act_parts, *out_far)
-    d_act_near = chips_sum_near(d_act_parts)
-    d_act_far = chips_sum_far(d_act_parts, d_act_near)
-    gain_sum = gain_parts[:half] + swap_core(gain_parts[half:].astype(LOW)).astype(F32)
-    qkv_sum = jnp.concatenate([qkv_sum, gain_sum.astype(LOW)], axis=1)
     qkv_sum = after(qkv_sum, inner_grad)
     qkv_grad = batch_scatter(qkv_sum.reshape(chips, half // chips, -1), 1)
+    out_far = chips_sum_far(out_parts, out_near)
+    d_act_near = after(d_act_near, qkv_grad, *out_far)
+    d_act_far = chips_sum_far(d_act_parts, d_act_near)
+    gain_parts = jnp.concatenate([gain_one_part / gain_one, gain_two_part], axis=0)
+    gain_parts = after(gain_parts, *d_act_far)
+    gain_grads = gain_parts[:, :half] + swap_core(gain_parts[:, half:])
+    gain_grads = gain_grads.reshape(2, chips, -1)
+    gain_grads = [
+        lax.dynamic_index_in_dim(gain_grads, chip ^ k, axis=1, keepdims=False)
+        for k in range(chips)
+    ]
+    gain_grads = sum(chips_scatter(gain_grads)).reshape(2, lax.axis_size("batch"), -1)
+    row = lax.axis_index("batch")
+    gain_grads = sum(
+        exchange(
+            lax.dynamic_index_in_dim(gain_grads, row ^ k, axis=1, keepdims=False), k, "batch"
+        )
+        for k in range(lax.axis_size("batch"))
+    )
     out_sum = summed(out_parts, out_near, out_far).astype(LOW)
     out_grad = batch_scatter(after(out_sum, qkv_grad), 0)
     tokens_grad = last(
@@ -1056,23 +1074,22 @@
         return in_order(chips_scatter(chip_rows))
 
     inner_grad = columns_of_chips(inner_grad)
-    qkv_grad = columns_of_chips(qkv_grad)
+    qkv_grad = columns_of_chips(after(qkv_grad, *d_act_far))
 
     def whole_columns(blocks, first, width):
         parts = [block[:, first : first + width] for block in blocks]
         return jnp.concatenate(parts, axis=1).astype(F32)
 
-    gain_grads = sum(block[:, columns:].astype(F32) for block in qkv_grad)
 
     return (
         block_out[None],
         tokens_grad[None],
-        gain_grads[:, 0],
+        gain_grads[0],
         whole_columns(qkv_grad, 0, head_width),
         whole_columns(qkv_grad, head_width, head_width),
         whole_columns(qkv_grad, 2 * head_width, head_width),
         out_grad.astype(F32),
-        gain_grads[:, LANES // 2],
+        gain_grads[1],
         whole_columns(inner_grad, 0, inner_width),
         whole_columns(inner_grad, inner_width, inner_width),
         down_grad.astype(F32),

time: 669 us -> 632 us (0.945)
  waiting for transfers between devices: 256 us -> 217 us
  local copies, waits for them, and re-layouts: 93.2 us -> 86 us
    ppermute x64 -> x69, waiting for transfers between devices: 214 us -> 169 us  [exchange(): lax.ppermute(value, axis, [(place, place ^ flip) for place in range(count)])]
    all_gather x4, waiting for transfers between devices: 19 us -> 44.9 us  [batch_gather(): return lax.all_gather(value, 'batch', axis=axis, tiled=True)]
    reduce_scatter x4, waiting for transfers between devices: 23.2 us -> 2.39 us  [batch_scatter(): return lax.psum_scatter(value, 'batch', scatter_dimension=axis, tiled=True)]
    pallas_call x2, Pallas kernels: 35.8 us -> 26.2 us  [back_project(): pl.pallas_call(functools.partial(back_project_kernel, tiles, 0 if act els...]
    pallas_call x6, Pallas kernels: 46.3 us -> 54 us  [turned(): pl.pallas_call(functools.partial(turned_kernel, len(arrived)), grid=(widt...]
    pallas_call x2, Pallas kernels: 12.3 us -> 19.8 us  [half_product(): pl.pallas_call(half_kernel, grid=(width // tile,), in_specs=[SCALAR, whol...]
    ppermute x64 -> x69, starting transfers between devices: 62.4 us -> 67.2 us  [exchange(): lax.ppermute(value, axis, [(place, place ^ flip) for place in range(count)])]
    unnamed x177 -> x201, local copies, waits for them, and re-layouts: 55.2 us -> 51.7 us
  transfers between devices with their start and end apart: 72 -> 77, of which waited for: 44 -> 40; matrix products, arithmetic and copies ran while one was open for 12% -> 12% of each run, Pallas kernels for 30% -> 32%
where the time goes in v3:
time: 632 us; the launch traced here: 621 us
  waiting for transfers between devices  217 us (34%)
  Pallas kernels  198 us (31%)
  local copies, waits for them, and re-layouts  86 us (14%)
  starting transfers between devices  67.9 us (11%)
  other arithmetic  35.9 us (6%)
  between operations  15.9 us (3%)
    ppermute x69, waiting for transfers between devices, exchange(): lax.ppermute(value, axis, [(place, place ^ flip) for place in range(count)])  169 us
    ppermute x69, starting transfers between devices, exchange(): lax.ppermute(value, axis, [(place, place ^ flip) for place in range(count)])  67.2 us
    pallas_call x6, Pallas kernels, turned(): pl.pallas_call(functools.partial(turned_kernel, len(arrived)), grid=(widt...  54 us
    unnamed x201, local copies, waits for them, and re-layouts  51.7 us
    all_gather x4, waiting for transfers between devices, batch_gather(): return lax.all_gather(value, 'batch', axis=axis, tiled=True)  44.9 us
    pallas_call x2, Pallas kernels, back_project(): pl.pallas_call(functools.partial(back_project_kernel, tiles, 0 if act els...  26.2 us
    pallas_call x2, Pallas kernels, half_product(): pl.pallas_call(half_kernel, grid=(width // tile,), in_specs=[SCALAR, whol...  19.8 us
    pallas_call x1, Pallas kernels, attention_back(): pl.pallas_call(attend_back_kernel, grid=(chips,), in_specs=[SCALAR, SCALA...  16.4 us
  transfers between devices with their start and end apart: 77, of which 40 were waited for; matrix products, arithmetic and copies ran while one was open for 12% of the time, Pallas kernels for 32%

profile of v3, /device:TPU:0, one launch (start us, length us, event | category | flops | bytes accessed | tf_op | source)
XLA Modules:
  0.0 620.7 jit_solution(14291602058061173048)
XLA Ops:
  33.5 13.2 %all-gather.5.cloned.1.call-done = bf16[256,2048]{1,0:T(8,128)(2,1)} async-done(((bf16[64,2048]{1,0:T(8,128)(2,1)}), bf16[256,2048]{1,0:T(8,128)(2,1)}) %all-gather.5.cloned.1.call-update) | async-done | bytes 1048592 | tf_op jit(solution)/shard_map/all_gather | solution.py:198
  47.9 8.0 %collective-permute-done.6 = bf16[256,2048]{1,0:T(8,128)(2,1)S(1)} collective-permute-done((bf16[256,2048]{1,0:T(8,128)(2,1)S(1)}, bf16[256,2048]{1,0:T(8,128)(2,1)S(1)}, u32[]{:S(2)}, u32[]{:S(2)}) %collective-permute-start.6) | collective-permute-done | bytes 1048608 | tf_op jit(solution)/shard_map/ppermute | solution.py:42
  57.1 19.4 %collective-permute-done.7 = bf16[256,2048]{1,0:T(8,128)(2,1)S(1)} collective-permute-done((bf16[256,2048]{1,0:T(8,128)(2,1)S(1)}, bf16[256,2048]{1,0:T(8,128)(2,1)S(1)}, u32[]{:S(2)}, u32[]{:S(2)}) %collective-permute-start.7) | collective-permute-done | bytes 1048608 | tf_op jit(solution)/shard_map/ppermute | solution.py:42
  98.1 21.3 %collective-permute-done.12 = bf16[256,2048]{1,0:T(8,128)(2,1)S(1)} collective-permute-done((bf16[256,2048]{1,0:T(8,128)(2,1)S(1)}, bf16[256,2048]{1,0:T(8,128)(2,1)S(1)}, u32[]{:S(2)}, u32[]{:S(2)}) %collective-permute-start.12) | collective-permute-done | bytes 1048608 | tf_op jit(solution)/shard_map/ppermute | solution.py:42
  130.4 11.4 %shard_map.203 = (bf16[1024,2048]{1,0:T(8,128)(2,1)S(1)}, bf16[1024,1536]{1,0:T(8,128)(2,1)S(1)}) custom-call(s32[1]{0:T(128)} %bitcast.core.flag, bf16[1024,2048]{1,0:T(8,128)(2,1)} %constant_dynamic-update-slice_fusion.tokens, f32[1,2048]{1,0:T(1,128)S(1)} %maximum_convert_fusion.5.gain.refs_6_, bf16[1024,1664]{1,0:T(8,128)(2,1)S(1)} %bitcast.171, ...), custom_call_target="tpu_custom_call" | custom-call | tf_op jit(solution)/shard_map/pallas_call | solution.py:255
  157.7 11.0 %shard_map.204 = bf16[4,256,512]{2,1,0:T(8,128)(2,1)S(1)} custom-call(s32[1]{0:T(128)} %bitcast.core.flag, s32[4]{0:T(128)S(1)} %or_convert_fusion.preceded, bf16[4,256,1536]{2,1,0:T(8,128)(2,1)S(1)} %bitcast.174, bf16[4,64,1024]{2,1,0:T(8,128)(2,1)S(1)} %broadcast_select_fusion.rim), custom_call_target="tpu_custom_call" | custom-call | tf_op jit(solution)/shard_map/pallas_call | solution.py:332
  199.0 28.3 %all-gather.9.cloned.1.call-done = bf16[4,256,2816]{2,1,0:T(8,128)(2,1)} async-done(((bf16[4,64,2816]{2,1,0:T(8,128)(2,1)}), bf16[4,256,2816]{2,1,0:T(8,128)(2,1)}) %all-gather.9.cloned.1.call-update) | async-done | bytes 5767184 | tf_op jit(solution)/shard_map/all_gather | solution.py:198
  231.0 11.0 %collective-permute-done.28 = bf16[128,2048]{1,0:T(8,128)(2,1)S(1)} collective-permute-done((bf16[128,2048]{1,0:T(8,128)(2,1)S(1)}, bf16[128,2048]{1,0:T(8,128)(2,1)S(1)}, u32[]{:S(2)}, u32[]{:S(2)}) %collective-permute-start.28) | collective-permute-done | bytes 524320 | tf_op jit(solution)/shard_map/ppermute | solution.py:42
  243.5 9.4 %shard_map.206.first = bf16[1024,2816]{1,0:T(8,128)(2,1)S(1)} custom-call(bf16[1024,2048]{1,0:T(8,128)(2,1)S(1)} %constant_dynamic-update-slice_fusion.14.act.left, bf16[1024,2816]{1,0:T(8,128)(2,1)S(1)} %bitcast.164, bf16[1024,2816]{1,0:T(8,128)(2,1)S(1)} %bitcast.165), custom_call_target="tpu_custom_call" | custom-call | tf_op jit(solution)/shard_map/pallas_call | solution.py:659
  255.4 12.9 %shard_map.207 = (bf16[1024,1408]{1,0:T(8,128)(2,1)S(1)}, bf16[1024,1408]{1,0:T(8,128)(2,1)S(1)}, bf16[1024,1408]{1,0:T(8,128)(2,1)S(1)}) custom-call(bf16[1024,2048]{1,0:T(8,128)(2,1)S(1)} %constant_dynamic-update-slice_fusion.14.act.left, bf16[1024,2816]{1,0:T(8,128)(2,1)} %collective-permute-done.30.gate.upward.other, ...), custom_call_target="tpu_custom_call" | custom-call | tf_op jit(solution)/shard_map/pallas_call | solution.py:682
  273.2 9.7 %shard_map.208 = bf16[704,2048]{1,0:T(8,128)(2,1)} custom-call(s32[1]{0:T(128)S(6)} %sub.16.flag, bf16[1024,1408]{1,0:T(8,128)(2,1)} %copy-done.6, bf16[1024,2048]{1,0:T(8,128)(2,1)} %copy-done.69), custom_call_target="tpu_custom_call" | custom-call | tf_op jit(solution)/shard_map/pallas_call | solution.py:872
  288.5 10.2 %shard_map.209 = bf16[704,2048]{1,0:T(8,128)(2,1)} custom-call(s32[1]{0:T(128)} %bitcast.core.flag, bf16[1024,1408]{1,0:T(8,128)(2,1)} %copy-done.6, bf16[1024,2048]{1,0:T(8,128)(2,1)} %copy-done.69, bf16[704,2048]{1,0:T(8,128)(2,1)} %collective-permute-done.31.refs_0_), custom_call_target="tpu_custom_call" | custom-call | tf_op jit(solution)/shard_map/pallas_call | solution.py:872
  300.3 13.6 %shard_map.210.right.d_out = bf16[1024,2816]{1,0:T(8,128)(2,1)} custom-call(s32[1]{0:T(128)} %bitcast.core.flag, bf16[1024,2048]{1,0:T(8,128)(2,1)} %copy-done.69, bf16[704,2048]{1,0:T(8,128)(2,1)} %all-gather.11.cloned.1.call-done.mine, bf16[704,2048]{1,0:T(8,128)(2,1)} %copy-done.23, bf16[1024,1408]{1,0:T(8,128)(2,1)} %copy-done.40, ...), custom_call_target="tpu_custom_call" | custom-call | tf_op jit(solution)/shard_map/pallas_call | solution.py:719
  313.9 13.7 %shard_map.211 = bf16[1024,2816]{1,0:T(8,128)(2,1)} custom-call(bf16[1024,2048]{1,0:T(8,128)(2,1)} %copy-done.1, bf16[1024,2816]{1,0:T(8,128)(2,1)} %shard_map.210.right.d_out), custom_call_target="tpu_custom_call" | custom-call | tf_op jit(solution)/shard_map/pallas_call | solution.py:797
  330.4 16.1 %shard_map.212 = (bf16[256,2048]{1,0:T(8,128)(2,1)S(1)}, bf16[2,128,2048]{2,1,0:T(8,128)(2,1)S(1)}, bf16[2,128,2048]{2,1,0:T(8,128)(2,1)S(1)}, bf16[128,2048]{1,0:T(8,128)(2,1)S(1)}, bf16[128,2048]{1,0:T(8,128)(2,1)S(1)}) custom-call(bf16[1024,2816]{1,0:T(8,128)(2,1)S(1)} %copy-done, bf16[1024,2816]{1,0:T(8,128)(2,1)} %bitcast.163, ...), custom_call_target="tpu_custom_call" | custom-call | tf_op jit(solution)/shard_map/pallas_call | solution.py:765
  352.4 14.6 %shard_map.221 = bf16[1024,2816]{1,0:T(8,128)(2,1)} custom-call(bf16[1024,2048]{1,0:T(8,128)(2,1)} %copy-done.1, bf16[1024,2816]{1,0:T(8,128)(2,1)} %shard_map.210.right.d_out, bf16[1024,2816]{1,0:T(8,128)(2,1)} %collective-permute-done.49.refs_0_), custom_call_target="tpu_custom_call" | custom-call | tf_op jit(solution)/shard_map/pallas_call | solution.py:797
  381.5 8.0 %collective-permute-done.35.refs_3_ = bf16[128,2048]{1,0:T(8,128)(2,1)S(1)} collective-permute-done((bf16[128,2048]{1,0:T(8,128)(2,1)S(1)}, bf16[128,2048]{1,0:T(8,128)(2,1)S(1)}, u32[]{:S(2)}, u32[]{:S(2)}) %collective-permute-start.35) | collective-permute-done | bytes 524320 | tf_op jit(solution)/shard_map/ppermute | solution.py:42
  406.9 9.3 %shard_map.214 = (bf16[256,2048]{1,0:T(8,128)(2,1)S(1)}, bf16[2,128,2048]{2,1,0:T(8,128)(2,1)}, bf16[2,128,2048]{2,1,0:T(8,128)(2,1)}, bf16[128,2048]{1,0:T(8,128)(2,1)S(1)}, bf16[128,2048]{1,0:T(8,128)(2,1)S(1)}) custom-call(s32[1]{0:T(128)} %bitcast.core.flag, bf16[1024,1408]{1,0:T(8,128)(2,1)S(1)} %copy-done.7, bf16[704,2048]{1,0:T(8,128)(2,1)S(1)} %copy-done.22, ...), custom_call_target="tpu_custom_call" | custom-call | tf_op jit(solution)/shard_map/pallas_call | solution.py:832
  418.3 16.4 %shard_map.215 = (bf16[4,256,1536]{2,1,0:T(8,128)(2,1)S(1)}, bf16[4,64,1024]{2,1,0:T(8,128)(2,1)}) custom-call(s32[1]{0:T(128)} %bitcast.core.flag, s32[4]{0:T(128)S(1)} %or_convert_fusion.preceded, bf16[4,256,1536]{2,1,0:T(8,128)(2,1)S(1)} %bitcast.175, bf16[4,64,1024]{2,1,0:T(8,128)(2,1)S(1)} %copy-done.36, bf16[4,256,512]{2,1,0:T(8,128)(2,1)S(1)} %pad_maximum_fusion.1.d_mixed), custom_call_target="tpu_custom_call" | custom-call | tf_op jit(solution)/shard_map/pallas_call | solution.py:401
  462.3 10.1 %shard_map.218 = (bf16[256,2048]{1,0:T(8,128)(2,1)S(1)}, bf16[2,128,2048]{2,1,0:T(8,128)(2,1)S(1)}, bf16[2,128,2048]{2,1,0:T(8,128)(2,1)S(1)}, bf16[128,2048]{1,...) custom-call(bf16[1024,1536]{1,0:T(8,128)(2,1)S(1)} %bitcast.167, ...), custom_call_target="tpu_custom_call" | custom-call | tf_op jit(solution)/shard_map/pallas_call | solution.py:765
  487.7 7.9 %shard_map.220 = (bf16[256,2048]{1,0:T(8,128)(2,1)S(1)}, bf16[2,128,2048]{2,1,0:T(8,128)(2,1)}, bf16[2,128,2048]{2,1,0:T(8,128)(2,1)}, bf16[128,2048]{1,0:T(8,128)(2,1)S(1)}, bf16[128,2048]{1,0:T(8,128)(2,1)S(1)}) custom-call(bf16[256,2048]{1,0:T(8,128)(2,1)S(1)} %copy-done.27, bf16[256,2048]{1,0:T(8,128)(2,1)S(1)} %copy-done.39, ...), custom_call_target="tpu_custom_call" | custom-call | tf_op jit(solution)/shard_map/pallas_call | solution.py:797
  502.0 8.7 %collective-permute-done.39 = bf16[128,2048]{1,0:T(8,128)(2,1)} collective-permute-done((bf16[128,2048]{1,0:T(8,128)(2,1)}, bf16[128,2048]{1,0:T(8,128)(2,1)}, u32[]{:S(2)}, u32[]{:S(2)}) %collective-permute-start.39) | collective-permute-done | bytes 524320 | tf_op jit(solution)/shard_map/ppermute | solution.py:42
  515.2 7.5 %collective-permute-done.50 = bf16[2,128,2048]{2,1,0:T(8,128)(2,1)} collective-permute-done((bf16[2,128,2048]{2,1,0:T(8,128)(2,1)}, bf16[2,128,2048]{2,1,0:T(8,128)(2,1)}, u32[]{:S(2)}, u32[]{:S(2)}) %collective-permute-start.50) | collective-permute-done | bytes 1048608 | tf_op jit(solution)/shard_map/ppermute | solution.py:42
  524.8 8.3 %collective-permute-done.52 = bf16[2,128,2048]{2,1,0:T(8,128)(2,1)} collective-permute-done((bf16[2,128,2048]{2,1,0:T(8,128)(2,1)}, bf16[2,128,2048]{2,1,0:T(8,128)(2,1)}, u32[]{:S(2)}, u32[]{:S(2)}) %collective-permute-start.52) | collective-permute-done | bytes 1048608 | tf_op jit(solution)/shard_map/ppermute | solution.py:42
  (463 shorter events, 304.7 us)
Async XLA Ops:
  7.2 39.6 %all-gather.5.cloned.1.call-start = ((), (), s32[]{:S(2)}) async-start(), calls=%async_computation.4 | async-start | bytes 1310720 | tf_op jit(solution)/shard_map/all_gather | solution.py:198
  16.8 103.6 %all-gather.7.cloned.1.call-start = ((), (), s32[]{:S(2)}) async-start(), calls=%async_computation.5 | async-start | bytes 4259840 | tf_op jit(solution)/shard_map/all_gather | solution.py:198
  29.9 26.1 %collective-permute-start.6 = (bf16[256,2048]{1,0:T(8,128)(2,1)S(1)}, bf16[256,2048]{1,0:T(8,128)(2,1)S(1)}, u32[]{:S(2)}, u32[]{:S(2)}) collective-permute-start(bf16[256,2048]{1,0:T(8,128)(2,1)S(1)} %bitcast.177), channel_id=1, source_target_pairs={{0,8},{4,12},{8,0},{12,4},{16,24},{20,28},{24,16},{28,20},{1,9},{5... | collective-permute-start | bytes 3145736 | tf_op jit(solution)/shard_map/ppermute | solution.py:42
  31.4 45.0 %collective-permute-start.7 = (bf16[256,2048]{1,0:T(8,128)(2,1)S(1)}, bf16[256,2048]{1,0:T(8,128)(2,1)S(1)}, u32[]{:S(2)}, u32[]{:S(2)}) collective-permute-start(bf16[256,2048]{1,0:T(8,128)(2,1)S(1)} %bitcast.178), channel_id=1, source_target_pairs={{0,16},{4,20},{8,24},{12,28},{16,0},{20,4},{24,8},{28,12},{1,17},{... | collective-permute-start | bytes 3145736 | tf_op jit(solution)/shard_map/ppermute | solution.py:42
  31.9 45.6 %collective-permute-start.8 = (bf16[256,2048]{1,0:T(8,128)(2,1)S(1)}, bf16[256,2048]{1,0:T(8,128)(2,1)}, u32[]{:S(2)}, u32[]{:S(2)}) collective-permute-start(bf16[256,2048]{1,0:T(8,128)(2,1)S(1)} %bitcast.179), channel_id=1, source_target_pairs={{0,24},{4,28},{8,16},{12,20},{16,8},{20,12},{24,0},{28,4},{1,25},{... | collective-permute-start | bytes 3145736 | tf_op jit(solution)/shard_map/ppermute | solution.py:42
  46.8 180.6 %all-gather.9.cloned.1.call-start = ((), (), s32[]{:S(2)}) async-start(), calls=%async_computation.6 | async-start | bytes 7208960 | tf_op jit(solution)/shard_map/all_gather | solution.py:198
  120.5 165.7 %all-gather.11.cloned.1.call-start = ((), (), s32[]{:S(2)}) async-start(), calls=%async_computation.7 | async-start | bytes 3604480 | tf_op jit(solution)/shard_map/all_gather | solution.py:198
  120.6 26.2 %collective-permute-start.16 = (bf16[256,2048]{1,0:T(8,128)(2,1)}, bf16[256,2048]{1,0:T(8,128)(2,1)}, u32[]{:S(2)}, u32[]{:S(2)}) collective-permute-start(bf16[256,2048]{1,0:T(8,128)(2,1)} %all-gather.5.cloned.1.call-done), channel_id=1, source_target_pairs={{0,8},{4,12},{8,0},{12,4},{16,24},{20,28},{24,16},{28,20},{1,9},{5... | collective-permute-start | bytes 3145736 | tf_op jit(solution)/shard_map/ppermute | solution.py:42
  121.5 28.2 %collective-permute-start.17 = (bf16[256,2048]{1,0:T(8,128)(2,1)}, bf16[256,2048]{1,0:T(8,128)(2,1)}, u32[]{:S(2)}, u32[]{:S(2)}) collective-permute-start(bf16[256,2048]{1,0:T(8,128)(2,1)} %all-gather.5.cloned.1.call-done), channel_id=1, source_target_pairs={{0,16},{4,20},{8,24},{12,28},{16,0},{20,4},{24,8},{28,12},{1,17},{... | collective-permute-start | bytes 3145736 | tf_op jit(solution)/shard_map/ppermute | solution.py:42
  142.2 26.6 %collective-permute-start.20 = (bf16[128,2048]{1,0:T(8,128)(2,1)S(1)}, bf16[128,2048]{1,0:T(8,128)(2,1)S(1)}, u32[]{:S(2)}, u32[]{:S(2)}) collective-permute-start(bf16[128,2048]{1,0:T(8,128)(2,1)S(1)} %slice.307), channel_id=1, source_target_pairs={{0,16},{4,20},{8,24},{12,28},{16,0},{20,4},{24,8},{28,12},{1,17},{... | collective-permute-start | bytes 1572872 | tf_op jit(solution)/shard_map/ppermute | solution.py:42
  197.3 30.0 %collective-permute-start.26 = (bf16[256,2048]{1,0:T(8,128)(2,1)S(1)}, bf16[256,2048]{1,0:T(8,128)(2,1)S(1)}, u32[]{:S(2)}, u32[]{:S(2)}) collective-permute-start(bf16[256,2048]{1,0:T(8,128)(2,1)S(1)} %get-tuple-element.113), channel_id=1, source_target_pairs={{0,8},{4,12},{8,0},{12,4},{16,24},{20,28},{24,16},{28,20},{1,9},{5... | collective-permute-start | bytes 3145736 | tf_op jit(solution)/shard_map/ppermute | solution.py:42
  198.4 29.0 %collective-permute-start.27 = (bf16[256,2048]{1,0:T(8,128)(2,1)S(1)}, bf16[256,2048]{1,0:T(8,128)(2,1)S(1)}, u32[]{:S(2)}, u32[]{:S(2)}) collective-permute-start(bf16[256,2048]{1,0:T(8,128)(2,1)S(1)} %get-tuple-element.113), channel_id=1, source_target_pairs={{0,16},{4,20},{8,24},{12,28},{16,0},{20,4},{24,8},{28,12},{1,17},{... | collective-permute-start | bytes 3145736 | tf_op jit(solution)/shard_map/ppermute | solution.py:42
  227.4 28.0 %collective-permute-start.30 = (bf16[1024,2816]{1,0:T(8,128)(2,1)}, bf16[1024,2816]{1,0:T(8,128)(2,1)}, u32[]{:S(2)}, u32[]{:S(2)}) collective-permute-start(bf16[1024,2816]{1,0:T(8,128)(2,1)} %bitcast.162), channel_id=1, source_target_pairs={{0,4},{4,0},{8,12},{12,8},{16,20},{20,16},{24,28},{28,24},{1,5},{5... | collective-permute-start | bytes 17301512 | tf_op jit(solution)/shard_map/ppermute | solution.py:42
  227.4 124.9 %reduce-scatter.5.cloned.1.call-start = ((), (), s32[]{:S(2)}) async-start(), calls=%async_computation.8 | async-start | bytes 3604480 | tf_op jit(solution)/shard_map/reduce_scatter | solution.py:202
  298.7 203.0 %reduce-scatter.7.cloned.1.call-start = ((), (), s32[]{:S(2)}) async-start(), calls=%async_computation.9 | async-start | bytes 7208960 | tf_op jit(solution)/shard_map/reduce_scatter | solution.py:202
  348.1 25.6 %collective-permute-start.33 = (bf16[2,128,2048]{2,1,0:T(8,128)(2,1)S(1)}, bf16[2,128,2048]{2,1,0:T(8,128)(2,1)}, u32[]{:S(2)}, u32[]{:S(2)}) collective-permute-start(bf16[2,128,2048]{2,1,0:T(8,128)(2,1)S(1)} %get-tuple-element.126), channel_id=1, source_target_pairs={{0,8},{4,12},{8,0},{12,4},{16,24},{20,28},{24,16},{28,20},{1,9},{5... | collective-permute-start | bytes 3145736 | tf_op jit(solution)/shard_map/ppermute | solution.py:42
  374.8 190.8 %reduce-scatter.9.cloned.1.call-start = ((), (), s32[]{:S(2)}) async-start(), calls=%async_computation.10 | async-start | bytes 3932160 | tf_op jit(solution)/shard_map/reduce_scatter | solution.py:202
  454.4 33.3 %collective-permute-start.48 = (bf16[1024,2048]{1,0:T(8,128)(2,1)}, bf16[1024,2048]{1,0:T(8,128)(2,1)}, u32[]{:S(2)}, u32[]{:S(2)}) collective-permute-start(bf16[1024,2048]{1,0:T(8,128)(2,1)} %shard_map.217), channel_id=1, source_target_pairs={{0,4},{4,0},{8,12},{12,8},{16,20},{20,16},{24,28},{28,24},{1,5},{5... | collective-permute-start | bytes 12582920 | tf_op jit(solution)/shard_map/ppermute | solution.py:42
  457.0 45.0 %collective-permute-start.40 = (bf16[128,2048]{1,0:T(8,128)(2,1)}, bf16[128,2048]{1,0:T(8,128)(2,1)}, u32[]{:S(2)}, u32[]{:S(2)}) collective-permute-start(bf16[128,2048]{1,0:T(8,128)(2,1)} %fusion.5), channel_id=1, source_target_pairs={{0,8},{4,12},{8,0},{12,4},{16,24},{20,28},{24,16},{28,20},{1,9},{5... | collective-permute-start | bytes 1572872 | tf_op jit(solution)/shard_map/ppermute | solution.py:42
  472.4 25.8 %collective-permute-start.45 = (bf16[2,128,2048]{2,1,0:T(8,128)(2,1)S(1)}, bf16[2,128,2048]{2,1,0:T(8,128)(2,1)S(1)}, u32[]{:S(2)}, u32[]{:S(2)}) collective-permute-start(bf16[2,128,2048]{2,1,0:T(8,128)(2,1)S(1)} %get-tuple-element.145), channel_id=1, source_target_pairs={{0,8},{4,12},{8,0},{12,4},{16,24},{20,28},{24,16},{28,20},{1,9},{5... | collective-permute-start | bytes 3145736 | tf_op jit(solution)/shard_map/ppermute | solution.py:42
  473.3 26.1 %collective-permute-start.46 = (bf16[2,128,2048]{2,1,0:T(8,128)(2,1)S(1)}, bf16[2,128,2048]{2,1,0:T(8,128)(2,1)S(1)}, u32[]{:S(2)}, u32[]{:S(2)}) collective-permute-start(bf16[2,128,2048]{2,1,0:T(8,128)(2,1)S(1)} %get-tuple-element.146), channel_id=1, source_target_pairs={{0,16},{4,20},{8,24},{12,28},{16,0},{20,4},{24,8},{28,12},{1,17},{... | collective-permute-start | bytes 3145736 | tf_op jit(solution)/shard_map/ppermute | solution.py:42
  479.9 30.8 %collective-permute-start.39 = (bf16[128,2048]{1,0:T(8,128)(2,1)}, bf16[128,2048]{1,0:T(8,128)(2,1)}, u32[]{:S(2)}, u32[]{:S(2)}) collective-permute-start(bf16[128,2048]{1,0:T(8,128)(2,1)} %fusion.6), channel_id=1, source_target_pairs={{0,16},{4,20},{8,24},{12,28},{16,0},{20,4},{24,8},{28,12},{1,17},{... | collective-permute-start | bytes 1572872 | tf_op jit(solution)/shard_map/ppermute | solution.py:42
  500.6 32.5 %collective-permute-start.52 = (bf16[2,128,2048]{2,1,0:T(8,128)(2,1)}, bf16[2,128,2048]{2,1,0:T(8,128)(2,1)}, u32[]{:S(2)}, u32[]{:S(2)}) collective-permute-start(bf16[2,128,2048]{2,1,0:T(8,128)(2,1)} %get-tuple-element.162), channel_id=1, source_target_pairs={{0,16},{4,20},{8,24},{12,28},{16,0},{20,4},{24,8},{28,12},{1,17},{... | collective-permute-start | bytes 3145736 | tf_op jit(solution)/shard_map/ppermute | solution.py:42
  501.7 109.9 %reduce-scatter.11.cloned.1.call-start = ((), (), s32[]{:S(2)}) async-start(), calls=%async_computation.11 | async-start | bytes 1310720 | tf_op jit(solution)/shard_map/reduce_scatter | solution.py:202
  (141 other events, 1570.2 us)
Sparse Core Ops, SparseCore 0:
  16.9 29.7 all-gather.4
  48.9 67.2 all-gather.6
  120.6 106.6 all-gather.8
  228.8 57.4 all-gather.10
  298.8 53.5 reduce-scatter.4
  375.0 98.6 reduce-scatter.6
  501.8 57.4 reduce-scatter.8
  580.7 25.1 reduce-scatter.10

commit v4 on v3

--- a/solution.py
+++ b/solution.py
@@ -86,12 +86,20 @@
     return [exchange(parts[1], CORES), exchange(parts[2], 2 * CORES)]
 
 
-def chips_sum_far(parts, near):
+def chips_sum_between(parts, near):
     if chip_count() != 4:
         return []
     on_second = (parts[3].astype(F32) + near[0][1].astype(F32)).astype(LOW)
     on_first = (parts[4].astype(F32) + near[1][1].astype(F32)).astype(LOW)
-    return [exchange(on_second, 2 * CORES), exchange(on_first, CORES)]
+    return [on_second, on_first]
+
+
+def chips_sum_far(parts, near):
+    return chips_sum_send(chips_sum_between(parts, near))
+
+
+def chips_sum_send(between):
+    return [exchange(part, step * CORES) for part, step in zip(between, (2, 1))]
 
 
 def summands(parts, near, far):
@@ -933,19 +941,20 @@
     qkv_rows = rows_of_chips([query_weight, key_weight, value_weight], gains)
     qkv_mine = batch_gather(after(qkv_rows, out_mine), 1).reshape(half, -1)
     tokens_sent = after(tokens, qkv_rows, group_total)
-    tokens_near = [exchange(tokens_sent, CORES * k) for k in range(1, chips)]
-    gathered = gathered_rows(tokens_sent, tokens_near, [])
+    tokens_near = gather_near(tokens_sent)
+    tokens_far = gather_far(tokens_near)
+    gathered = gathered_rows(tokens_sent, tokens_near, tokens_far)
+    ffn_sent = after(d_final.astype(LOW), *tokens_near, *tokens_far)
+    ffn_near = gather_near(ffn_sent)
     gate_weight, up_weight = after((gate_weight, up_weight), gathered)
     inner_rows = rows_of_chips([gate_weight, up_weight])
     inner_mine = batch_gather(inner_rows, 1).reshape(half, -1)
     down_mine = batch_gather(after(down_weight, inner_rows), 0)
 
-    ffn_sent = after(d_final.astype(LOW), inner_rows)
-    ffn_near = gather_near(ffn_sent)
-    qkv_mine = after(qkv_mine, *ffn_near)
     ffn_far = gather_far(ffn_near)
-    out_sent = after(out_mine, *ffn_near)
+    out_sent = after(out_mine, inner_rows)
     out_near = gather_near(out_sent)
+    qkv_mine = after(qkv_mine, inner_rows, *ffn_near)
     qkv_other = swap_core(qkv_mine)
     out_far = gather_far(out_near)
     columns = 3 * head_width
@@ -984,9 +993,8 @@
     act_two = gathered_rows(act_two_own, act_near, act_far)
     inner_mine = after(inner_mine, *act_near)
     inner_other = swap_core(inner_mine)
-    hidden, slope_gate, slope_up = inner_second(
-        act_two, inner_other, inner_first(act_two, inner_mine)
-    )
+    first = inner_first(act_two, inner_mine)
+    hidden, slope_gate, slope_up = inner_second(act_two, inner_other, first)
     down_send = half_product(1 - flag, hidden, d_ffn)
     down_back = swap_core(down_send)
     down_mine = after(down_mine, down_send)
@@ -996,7 +1004,7 @@
     d_gate_up = inner_back(
         flag, after(d_ffn, down_sum), down_mine, down_other, slope_gate, slope_up, chips
     )
-    inner_send = turned(act_two, 1, d_gate_up)
+    inner_send = matmul_rows(act_two[:, half:], d_gate_up).astype(LOW)
     act_parts = back_project(after(d_gate_up, inner_send), inner_mine, inner_other, chips)
     act_near = chips_sum_near(act_parts)
     inner_sum = turned(
@@ -1026,55 +1034,59 @@
     returned = jnp.where(followed[:, None, None], jnp.take(lent, follow, axis=0), 0)
     d_qkv = d_qkv.at[:, tok_count - WINDOW :, head_width:].add(returned)
     d_qkv = after(d_qkv.reshape(chips * tok_count, columns), *block_near)
-    block_far = chips_sum_far(block_parts, block_near)
     qkv_send = turned(act_one, 1, d_qkv)
     out_send = turned(mixed_own, 1, after(d_attn, qkv_send))
+    out_back = swap_core(out_send)
+    between = chips_sum_between(block_parts, after(block_near, qkv_send))
+    block_far = chips_sum_send(between)
+    qkv_sum = turned(act_one, 0, after(d_qkv, qkv_send, *between), swap_core(qkv_send))
     d_act_parts, gain_one_part = back_project(
-        after(d_qkv, out_send), qkv_mine, qkv_other, chips, act_one
-    )
-    qkv_sum = turned(act_one, 0, after(d_qkv, d_act_parts[0]), swap_core(qkv_send))
-    out_parts = turned(mixed_own, 0, after(d_attn, qkv_sum), swap_core(out_send), chips=chips)
-    if chips == 1:
-        out_parts = [out_parts]
-    d_act_near = after(chips_sum_near(d_act_parts), out_parts[0])
-    out_parts = after(out_parts, *d_act_near)
+        after(d_qkv, qkv_sum), qkv_mine, qkv_other, chips, act_one
+    )
+    qkv_sum = after(qkv_sum, inner_grad, d_act_parts[0])
+    qkv_grad = batch_scatter(qkv_sum.reshape(chips, half // chips, -1), 1)
+
+    out_parts = turned(mixed_own, 0, after(d_attn, d_act_parts[0]), out_back, chips=chips)
+    out_parts = out_parts if chips > 1 else [out_parts]
     out_near = chips_sum_near(out_parts)
-    qkv_sum = after(qkv_sum, inner_grad)
-    qkv_grad = batch_scatter(qkv_sum.reshape(chips, half // chips, -1), 1)
+    gain_parts = jnp.concatenate([gain_one_part / gain_one, gain_two_part], axis=0)
+    gain_core = swap_core(gain_parts[:, half:])
+    def columns_of_chips(grad):
+        chip_rows = [
+            lax.dynamic_index_in_dim(grad, chip ^ k, axis=0, keepdims=False) for k in range(chips)
+        ]
+        return chips_scatter(chip_rows)
+
     out_far = chips_sum_far(out_parts, out_near)
-    d_act_near = after(d_act_near, qkv_grad, *out_far)
+    inner_cells = columns_of_chips(after(inner_grad, *out_near))
+    out_sum = summed(out_parts, out_near, out_far).astype(LOW)
+    out_grad = batch_scatter(after(out_sum, qkv_grad), 0)
+    d_act_parts = after(d_act_parts, qkv_grad, *out_far, *inner_cells[1:])
+    d_act_near = chips_sum_near(d_act_parts)
+    gain_grads = (gain_parts[:, :half] + after(gain_core, qkv_grad)).reshape(2, chips, -1)
+    gain_grads = chips_scatter(
+        [
+            lax.dynamic_index_in_dim(gain_grads, chip ^ k, axis=1, keepdims=False)
+            for k in range(chips)
+        ]
+    )
     d_act_far = chips_sum_far(d_act_parts, d_act_near)
-    gain_parts = jnp.concatenate([gain_one_part / gain_one, gain_two_part], axis=0)
-    gain_parts = after(gain_parts, *d_act_far)
-    gain_grads = gain_parts[:, :half] + swap_core(gain_parts[:, half:])
-    gain_grads = gain_grads.reshape(2, chips, -1)
-    gain_grads = [
-        lax.dynamic_index_in_dim(gain_grads, chip ^ k, axis=1, keepdims=False)
-        for k in range(chips)
-    ]
-    gain_grads = sum(chips_scatter(gain_grads)).reshape(2, lax.axis_size("batch"), -1)
     row = lax.axis_index("batch")
+    gain_grads = sum(after(gain_grads, *d_act_near))
+    gain_grads = gain_grads.reshape(2, lax.axis_size("batch"), -1)
     gain_grads = sum(
         exchange(
             lax.dynamic_index_in_dim(gain_grads, row ^ k, axis=1, keepdims=False), k, "batch"
         )
         for k in range(lax.axis_size("batch"))
     )
-    out_sum = summed(out_parts, out_near, out_far).astype(LOW)
-    out_grad = batch_scatter(after(out_sum, qkv_grad), 0)
+    qkv_cells = columns_of_chips(after(qkv_grad, *d_act_near))
     tokens_grad = last(
         flag, *summands(d_act_parts, d_act_near, d_act_far), tokens, gain_one, d_resid, chips
     )
     block_out = (resid + summed(block_parts, block_near, block_far)).astype(LOW)
 
-    def columns_of_chips(grad):
-        chip_rows = [
-            lax.dynamic_index_in_dim(grad, chip ^ k, axis=0, keepdims=False) for k in range(chips)
-        ]
-        return in_order(chips_scatter(chip_rows))
-
-    inner_grad = columns_of_chips(inner_grad)
-    qkv_grad = columns_of_chips(after(qkv_grad, *d_act_far))
+    inner_grad, qkv_grad = in_order(inner_cells), in_order(qkv_cells)
 
     def whole_columns(blocks, first, width):
         parts = [block[:, first : first + width] for block in blocks]

time: 632 us -> 618 us (0.978)
  local copies, waits for them, and re-layouts: 86 us -> 65.7 us
  Pallas kernels: 198 us -> 186 us
  matrix products: 0 us -> 11.1 us
  waiting for transfers between devices: 217 us -> 226 us
    unnamed x201 -> x179, local copies, waits for them, and re-layouts: 51.7 us -> 36.7 us
    pallas_call x6 -> x5, Pallas kernels: 54 us -> 42.4 us  [turned(): pl.pallas_call(functools.partial(turned_kernel, len(arrived)), grid=(widt...]
    dot_general x0 -> x1, matrix products: none -> 11.1 us  [matmul_rows(): return lax.dot_general(left, right, ROWS_DIMS, preferred_element_type=F32)]
    ppermute x69 -> x70, waiting for transfers between devices: 169 us -> 173 us  [exchange(): lax.ppermute(value, axis, [(place, place ^ flip) for place in range(count)])]
    ppermute x69 -> x70, starting transfers between devices: 67.2 us -> 70.1 us  [exchange(): lax.ppermute(value, axis, [(place, place ^ flip) for place in range(count)])]
  transfers between devices with their start and end apart: 77 -> 78, of which waited for: 40 -> 40; matrix products, arithmetic and copies ran while one was open for 12% -> 13% of each run, Pallas kernels for 32% -> 31%
where the time goes in v4:
time: 618 us; the launch traced here: 608 us
  waiting for transfers between devices  226 us (37%)
  Pallas kernels  186 us (30%)
  starting transfers between devices  70.8 us (11%)
  local copies, waits for them, and re-layouts  65.7 us (11%)
  other arithmetic  32.1 us (5%)
  between operations  16.1 us (3%)
  matrix products  11.1 us (2%)
    ppermute x70, waiting for transfers between devices, exchange(): lax.ppermute(value, axis, [(place, place ^ flip) for place in range(count)])  173 us
    ppermute x70, starting transfers between devices, exchange(): lax.ppermute(value, axis, [(place, place ^ flip) for place in range(count)])  70.1 us
    all_gather x4, waiting for transfers between devices, batch_gather(): return lax.all_gather(value, 'batch', axis=axis, tiled=True)  44 us
    pallas_call x5, Pallas kernels, turned(): pl.pallas_call(functools.partial(turned_kernel, len(arrived)), grid=(widt...  42.4 us
    unnamed x179, local copies, waits for them, and re-layouts  36.7 us
    pallas_call x2, Pallas kernels, back_project(): pl.pallas_call(functools.partial(back_project_kernel, tiles, 0 if act els...  26.2 us
    pallas_call x2, Pallas kernels, half_product(): pl.pallas_call(half_kernel, grid=(width // tile,), in_specs=[SCALAR, whol...  19.8 us
    pallas_call x1, Pallas kernels, attention_back(): pl.pallas_call(attend_back_kernel, grid=(chips,), in_specs=[SCALAR, SCALA...  16.4 us
  transfers between devices with their start and end apart: 78, of which 40 were waited for; matrix products, arithmetic and copies ran while one was open for 13% of the time, Pallas kernels for 31%

profile of v4, /device:TPU:0, one launch (start us, length us, event | category | flops | bytes accessed | tf_op | source)
XLA Modules:
  0.0 607.9 jit_solution(14828011014912075918)
XLA Ops:
  32.6 7.8 %all-gather.5.cloned.1.call-done = bf16[256,2048]{1,0:T(8,128)(2,1)} async-done(((bf16[64,2048]{1,0:T(8,128)(2,1)}), bf16[256,2048]{1,0:T(8,128)(2,1)}) %all-gather.5.cloned.1.call-update) | async-done | bytes 1048592 | tf_op jit(solution)/shard_map/all_gather | solution.py:206
  40.6 13.3 %collective-permute-done.6 = bf16[256,2048]{1,0:T(8,128)(2,1)S(1)} collective-permute-done((bf16[256,2048]{1,0:T(8,128)(2,1)S(1)}, bf16[256,2048]{1,0:T(8,128)(2,1)S(1)}, u32[]{:S(2)}, u32[]{:S(2)}) %collective-permute-start.6) | collective-permute-done | bytes 1048608 | tf_op jit(solution)/shard_map/ppermute | solution.py:42
  89.5 17.0 %collective-permute-done.13 = bf16[256,2048]{1,0:T(8,128)(2,1)S(1)} collective-permute-done((bf16[256,2048]{1,0:T(8,128)(2,1)S(1)}, bf16[256,2048]{1,0:T(8,128)(2,1)S(1)}, u32[]{:S(2)}, u32[]{:S(2)}) %collective-permute-start.13) | collective-permute-done | bytes 1048608 | tf_op jit(solution)/shard_map/ppermute | solution.py:42
  119.7 11.4 %shard_map.203 = (bf16[1024,2048]{1,0:T(8,128)(2,1)S(1)}, bf16[1024,1536]{1,0:T(8,128)(2,1)S(1)}) custom-call(s32[1]{0:T(128)} %bitcast.core.flag, bf16[1024,2048]{1,0:T(8,128)(2,1)} %constant_dynamic-update-slice_fusion.tokens, f32[1,2048]{1,0:T(1,128)S(1)} %maximum_convert_fusion.5.gain.refs_6_, bf16[1024,1664]{1,0:T(8,128)(2,1)S(1)} %bitcast.169, ...), custom_call_target="tpu_custom_call" | custom-call | tf_op jit(solution)/shard_map/pallas_call | solution.py:263
  147.5 11.0 %shard_map.204 = bf16[4,256,512]{2,1,0:T(8,128)(2,1)S(1)} custom-call(s32[1]{0:T(128)} %bitcast.core.flag, s32[4]{0:T(128)S(1)} %or_convert_fusion.preceded, bf16[4,256,1536]{2,1,0:T(8,128)(2,1)S(1)} %bitcast.172, bf16[4,64,1024]{2,1,0:T(8,128)(2,1)S(1)} %broadcast_select_fusion.rim), custom_call_target="tpu_custom_call" | custom-call | tf_op jit(solution)/shard_map/pallas_call | solution.py:340
  187.2 30.1 %all-gather.9.cloned.1.call-done = bf16[4,256,2816]{2,1,0:T(8,128)(2,1)} async-done(((bf16[4,64,2816]{2,1,0:T(8,128)(2,1)}), bf16[4,256,2816]{2,1,0:T(8,128)(2,1)}) %all-gather.9.cloned.1.call-update) | async-done | bytes 5767184 | tf_op jit(solution)/shard_map/all_gather | solution.py:206
  221.0 11.0 %collective-permute-done.29 = bf16[128,2048]{1,0:T(8,128)(2,1)S(1)} collective-permute-done((bf16[128,2048]{1,0:T(8,128)(2,1)S(1)}, bf16[128,2048]{1,0:T(8,128)(2,1)S(1)}, u32[]{:S(2)}, u32[]{:S(2)}) %collective-permute-start.29) | collective-permute-done | bytes 524320 | tf_op jit(solution)/shard_map/ppermute | solution.py:42
  233.5 9.4 %shard_map.206.first = bf16[1024,2816]{1,0:T(8,128)(2,1)S(1)} custom-call(bf16[1024,2048]{1,0:T(8,128)(2,1)S(1)} %constant_dynamic-update-slice_fusion.15.act.left, bf16[1024,2816]{1,0:T(8,128)(2,1)S(1)} %bitcast.162, bf16[1024,2816]{1,0:T(8,128)(2,1)S(1)} %bitcast.163), custom_call_target="tpu_custom_call" | custom-call | tf_op jit(solution)/shard_map/pallas_call | solution.py:667
  245.3 12.9 %shard_map.207 = (bf16[1024,1408]{1,0:T(8,128)(2,1)S(1)}, bf16[1024,1408]{1,0:T(8,128)(2,1)S(1)}, bf16[1024,1408]{1,0:T(8,128)(2,1)S(1)}) custom-call(bf16[1024,2048]{1,0:T(8,128)(2,1)S(1)} %constant_dynamic-update-slice_fusion.15.act.left, bf16[1024,2816]{1,0:T(8,128)(2,1)} %collective-permute-done.31.gate.upward.other, ...), custom_call_target="tpu_custom_call" | custom-call | tf_op jit(solution)/shard_map/pallas_call | solution.py:690
  263.2 9.6 %shard_map.208 = bf16[704,2048]{1,0:T(8,128)(2,1)} custom-call(s32[1]{0:T(128)S(6)} %sub.16.flag, bf16[1024,1408]{1,0:T(8,128)(2,1)} %copy-done.6, bf16[1024,2048]{1,0:T(8,128)(2,1)} %copy-done.59), custom_call_target="tpu_custom_call" | custom-call | tf_op jit(solution)/shard_map/pallas_call | solution.py:880
  278.5 10.2 %shard_map.209 = bf16[704,2048]{1,0:T(8,128)(2,1)} custom-call(s32[1]{0:T(128)} %bitcast.core.flag, bf16[1024,1408]{1,0:T(8,128)(2,1)} %copy-done.6, bf16[1024,2048]{1,0:T(8,128)(2,1)} %copy-done.59, bf16[704,2048]{1,0:T(8,128)(2,1)} %collective-permute-done.32.refs_0_), custom_call_target="tpu_custom_call" | custom-call | tf_op jit(solution)/shard_map/pallas_call | solution.py:880
  290.2 13.6 %shard_map.210.d_out.right = bf16[1024,2816]{1,0:T(8,128)(2,1)} custom-call(s32[1]{0:T(128)} %bitcast.core.flag, bf16[1024,2048]{1,0:T(8,128)(2,1)} %copy-done.59, bf16[704,2048]{1,0:T(8,128)(2,1)} %all-gather.11.cloned.1.call-done.mine, bf16[704,2048]{1,0:T(8,128)(2,1)} %copy-done.22, bf16[1024,1408]{1,0:T(8,128)(2,1)} %copy-done.39, ...), custom_call_target="tpu_custom_call" | custom-call | tf_op jit(solution)/shard_map/pallas_call | solution.py:727
  303.8 11.1 %convolution_convert_fusion = bf16[1024,2816]{1,0:T(8,128)(2,1)} fusion(bf16[1024,2816]{1,0:T(8,128)(2,1)} %shard_map.210.d_out.right, bf16[1024,2048]{1,0:T(8,128)(2,1)} %copy-done.2), kind=kOutput, calls=%fused_computation.2 | convolution fusion | flops 5908463616 | bytes 13631488 | tf_op jit(solution)/shard_map/dot_general | solution.py:31
  315.1 16.1 %shard_map.211 = (bf16[256,2048]{1,0:T(8,128)(2,1)S(1)}, bf16[2,128,2048]{2,1,0:T(8,128)(2,1)S(1)}, bf16[2,128,2048]{2,1,0:T(8,128)(2,1)S(1)}, bf16[128,2048]{1,0:T(8,128)(2,1)S(1)}, bf16[128,2048]{1,0:T(8,128)(2,1)S(1)}) custom-call(bf16[1024,2816]{1,0:T(8,128)(2,1)S(1)} %copy-done.1, bf16[1024,2816]{1,0:T(8,128)(2,1)} %bitcast.161, ...), custom_call_target="tpu_custom_call" | custom-call | tf_op jit(solution)/shard_map/pallas_call | solution.py:773
  334.7 7.6 %reduce-scatter.5.cloned.1.call-done = bf16[176,2048]{1,0:T(8,128)(2,1)} async-done(((bf16[704,2048]{1,0:T(8,128)(2,1)}), bf16[176,2048]{1,0:T(8,128)(2,1)}) %reduce-scatter.5.cloned.1.call-update) | async-done | bytes 720912 | tf_op jit(solution)/shard_map/reduce_scatter | solution.py:210
  342.3 14.6 %shard_map.218 = bf16[1024,2816]{1,0:T(8,128)(2,1)} custom-call(bf16[1024,2048]{1,0:T(8,128)(2,1)} %copy-done.2, bf16[1024,2816]{1,0:T(8,128)(2,1)} %shard_map.210.d_out.right, bf16[1024,2816]{1,0:T(8,128)(2,1)} %collective-permute-done.47.refs_0_), custom_call_target="tpu_custom_call" | custom-call | tf_op jit(solution)/shard_map/pallas_call | solution.py:805
  366.0 8.6 %collective-permute-done.36.refs_3_ = bf16[128,2048]{1,0:T(8,128)(2,1)S(1)} collective-permute-done((bf16[128,2048]{1,0:T(8,128)(2,1)S(1)}, bf16[128,2048]{1,0:T(8,128)(2,1)S(1)}, u32[]{:S(2)}, u32[]{:S(2)}) %collective-permute-start.36) | collective-permute-done | bytes 524320 | tf_op jit(solution)/shard_map/ppermute | solution.py:42
  391.6 9.3 %shard_map.213 = (bf16[256,2048]{1,0:T(8,128)(2,1)S(1)}, bf16[2,128,2048]{2,1,0:T(8,128)(2,1)}, bf16[2,128,2048]{2,1,0:T(8,128)(2,1)}, bf16[128,2048]{1,0:T(8,128)(2,1)S(1)}, bf16[128,2048]{1,0:T(8,128)(2,1)S(1)}) custom-call(s32[1]{0:T(128)} %bitcast.core.flag, bf16[1024,1408]{1,0:T(8,128)(2,1)S(1)} %copy-done.7, bf16[704,2048]{1,0:T(8,128)(2,1)S(1)} %copy-done.21, ...), custom_call_target="tpu_custom_call" | custom-call | tf_op jit(solution)/shard_map/pallas_call | solution.py:840
  403.1 16.4 %shard_map.214 = (bf16[4,256,1536]{2,1,0:T(8,128)(2,1)S(1)}, bf16[4,64,1024]{2,1,0:T(8,128)(2,1)}) custom-call(s32[1]{0:T(128)} %bitcast.core.flag, s32[4]{0:T(128)S(1)} %or_convert_fusion.preceded, bf16[4,256,1536]{2,1,0:T(8,128)(2,1)S(1)} %bitcast.173, bf16[4,64,1024]{2,1,0:T(8,128)(2,1)S(1)} %copy-done.35, bf16[4,256,512]{2,1,0:T(8,128)(2,1)S(1)} %pad_maximum_fusion.1.d_mixed), custom_call_target="tpu_custom_call" | custom-call | tf_op jit(solution)/shard_map/pallas_call | solution.py:409
  451.3 7.6 %shard_map.216 = bf16[1024,1536]{1,0:T(8,128)(2,1)} custom-call(bf16[1024,2048]{1,0:T(8,128)(2,1)S(1)} %copy-done.5, bf16[1024,1536]{1,0:T(8,128)(2,1)S(1)} %bitcast.165, bf16[1024,1536]{1,0:T(8,128)(2,1)} %collective-permute-done.46.refs_0_), custom_call_target="tpu_custom_call" | custom-call | tf_op jit(solution)/shard_map/pallas_call | solution.py:805
  460.9 10.1 %shard_map.217 = (bf16[256,2048]{1,0:T(8,128)(2,1)S(1)}, bf16[2,128,2048]{2,1,0:T(8,128)(2,1)S(1)}, bf16[2,128,2048]{2,1,0:T(8,128)(2,1)S(1)}, bf16[128,2048]{1,...) custom-call(bf16[1024,1536]{1,0:T(8,128)(2,1)S(1)} %bitcast.166, ...), custom_call_target="tpu_custom_call" | custom-call | tf_op jit(solution)/shard_map/pallas_call | solution.py:773
  471.1 8.8 %shard_map.220 = (bf16[256,2048]{1,0:T(8,128)(2,1)S(1)}, bf16[2,128,2048]{2,1,0:T(8,128)(2,1)}, bf16[2,128,2048]{2,1,0:T(8,128)(2,1)S(1)}, bf16[128,2048]{1,0:T(8,128)(2,1)S(1)}, bf16[128,2048]{1,0:T(8,128)(2,1)S(1)}) custom-call(bf16[256,2048]{1,0:T(8,128)(2,1)S(1)} %copy-done.26, bf16[256,2048]{1,0:T(8,128)(2,1)S(1)} %copy-done.38, ...), custom_call_target="tpu_custom_call" | custom-call | tf_op jit(solution)/shard_map/pallas_call | solution.py:805
  485.3 20.1 %collective-permute-done.49 = bf16[2,128,2048]{2,1,0:T(8,128)(2,1)} collective-permute-done((bf16[2,128,2048]{2,1,0:T(8,128)(2,1)}, bf16[2,128,2048]{2,1,0:T(8,128)(2,1)}, u32[]{:S(2)}, u32[]{:S(2)}) %collective-permute-start.49) | collective-permute-done | bytes 1048608 | tf_op jit(solution)/shard_map/ppermute | solution.py:42
  552.1 16.0 %collective-permute-done.56 = bf16[2,128,2048]{2,1,0:T(8,128)(2,1)} collective-permute-done((bf16[2,128,2048]{2,1,0:T(8,128)(2,1)S(1)}, bf16[2,128,2048]{2,1,0:T(8,128)(2,1)}, u32[]{:S(2)}, u32[]{:S(2)}) %collective-permute-start.56) | collective-permute-done | bytes 1048608 | tf_op jit(solution)/shard_map/ppermute | solution.py:42
  (444 shorter events, 288.1 us)
Async XLA Ops:
  7.2 33.2 %all-gather.5.cloned.1.call-start = ((), (), s32[]{:S(2)}) async-start(), calls=%async_computation.4 | async-start | bytes 1310720 | tf_op jit(solution)/shard_map/all_gather | solution.py:206
  7.9 101.8 %all-gather.7.cloned.1.call-start = ((), (), s32[]{:S(2)}) async-start(), calls=%async_computation.5 | async-start | bytes 4259840 | tf_op jit(solution)/shard_map/all_gather | solution.py:206
  40.4 176.9 %all-gather.9.cloned.1.call-start = ((), (), s32[]{:S(2)}) async-start(), calls=%async_computation.6 | async-start | bytes 7208960 | tf_op jit(solution)/shard_map/all_gather | solution.py:206
  73.7 32.7 %collective-permute-start.13 = (bf16[256,2048]{1,0:T(8,128)(2,1)S(1)}, bf16[256,2048]{1,0:T(8,128)(2,1)S(1)}, u32[]{:S(2)}, u32[]{:S(2)}) collective-permute-start(bf16[256,2048]{1,0:T(8,128)(2,1)S(1)} %get-tuple-element.106), channel_id=1, source_target_pairs={{0,8},{4,12},{8,0},{12,4},{16,24},{20,28},{24,16},{28,20},{1,9},{5... | collective-permute-start | bytes 3145736 | tf_op jit(solution)/shard_map/ppermute | solution.py:42
  74.6 32.4 %collective-permute-start.14 = (bf16[256,2048]{1,0:T(8,128)(2,1)S(1)}, bf16[256,2048]{1,0:T(8,128)(2,1)S(1)}, u32[]{:S(2)}, u32[]{:S(2)}) collective-permute-start(bf16[256,2048]{1,0:T(8,128)(2,1)S(1)} %get-tuple-element.106), channel_id=1, source_target_pairs={{0,16},{4,20},{8,24},{12,28},{16,0},{20,4},{24,8},{28,12},{1,17},{... | collective-permute-start | bytes 3145736 | tf_op jit(solution)/shard_map/ppermute | solution.py:42
  109.8 166.4 %all-gather.11.cloned.1.call-start = ((), (), s32[]{:S(2)}) async-start(), calls=%async_computation.7 | async-start | bytes 3604480 | tf_op jit(solution)/shard_map/all_gather | solution.py:206
  109.8 25.9 %collective-permute-start.17 = (bf16[256,2048]{1,0:T(8,128)(2,1)}, bf16[256,2048]{1,0:T(8,128)(2,1)}, u32[]{:S(2)}, u32[]{:S(2)}) collective-permute-start(bf16[256,2048]{1,0:T(8,128)(2,1)} %all-gather.5.cloned.1.call-done), channel_id=1, source_target_pairs={{0,8},{4,12},{8,0},{12,4},{16,24},{20,28},{24,16},{28,20},{1,9},{5... | collective-permute-start | bytes 3145736 | tf_op jit(solution)/shard_map/ppermute | solution.py:42
  111.4 27.8 %collective-permute-start.18 = (bf16[256,2048]{1,0:T(8,128)(2,1)}, bf16[256,2048]{1,0:T(8,128)(2,1)}, u32[]{:S(2)}, u32[]{:S(2)}) collective-permute-start(bf16[256,2048]{1,0:T(8,128)(2,1)} %all-gather.5.cloned.1.call-done), channel_id=1, source_target_pairs={{0,16},{4,20},{8,24},{12,28},{16,0},{20,4},{24,8},{28,12},{1,17},{... | collective-permute-start | bytes 3145736 | tf_op jit(solution)/shard_map/ppermute | solution.py:42
  131.4 27.2 %collective-permute-start.21 = (bf16[128,2048]{1,0:T(8,128)(2,1)S(1)}, bf16[128,2048]{1,0:T(8,128)(2,1)S(1)}, u32[]{:S(2)}, u32[]{:S(2)}) collective-permute-start(bf16[128,2048]{1,0:T(8,128)(2,1)S(1)} %slice.321), channel_id=1, source_target_pairs={{0,16},{4,20},{8,24},{12,28},{16,0},{20,4},{24,8},{28,12},{1,17},{... | collective-permute-start | bytes 1572872 | tf_op jit(solution)/shard_map/ppermute | solution.py:42
  185.2 32.1 %collective-permute-start.27 = (bf16[256,2048]{1,0:T(8,128)(2,1)S(1)}, bf16[256,2048]{1,0:T(8,128)(2,1)S(1)}, u32[]{:S(2)}, u32[]{:S(2)}) collective-permute-start(bf16[256,2048]{1,0:T(8,128)(2,1)S(1)} %get-tuple-element.116), channel_id=1, source_target_pairs={{0,8},{4,12},{8,0},{12,4},{16,24},{20,28},{24,16},{28,20},{1,9},{5... | collective-permute-start | bytes 3145736 | tf_op jit(solution)/shard_map/ppermute | solution.py:42
  185.7 31.6 %collective-permute-start.28 = (bf16[256,2048]{1,0:T(8,128)(2,1)S(1)}, bf16[256,2048]{1,0:T(8,128)(2,1)S(1)}, u32[]{:S(2)}, u32[]{:S(2)}) collective-permute-start(bf16[256,2048]{1,0:T(8,128)(2,1)S(1)} %get-tuple-element.116), channel_id=1, source_target_pairs={{0,16},{4,20},{8,24},{12,28},{16,0},{20,4},{24,8},{28,12},{1,17},{... | collective-permute-start | bytes 3145736 | tf_op jit(solution)/shard_map/ppermute | solution.py:42
  217.3 28.0 %collective-permute-start.31 = (bf16[1024,2816]{1,0:T(8,128)(2,1)}, bf16[1024,2816]{1,0:T(8,128)(2,1)}, u32[]{:S(2)}, u32[]{:S(2)}) collective-permute-start(bf16[1024,2816]{1,0:T(8,128)(2,1)} %bitcast.160), channel_id=1, source_target_pairs={{0,4},{4,0},{8,12},{12,8},{16,20},{20,16},{24,28},{28,24},{1,5},{5... | collective-permute-start | bytes 17301512 | tf_op jit(solution)/shard_map/ppermute | solution.py:42
  217.4 124.9 %reduce-scatter.5.cloned.1.call-start = ((), (), s32[]{:S(2)}) async-start(), calls=%async_computation.8 | async-start | bytes 3604480 | tf_op jit(solution)/shard_map/reduce_scatter | solution.py:210
  288.6 196.5 %reduce-scatter.7.cloned.1.call-start = ((), (), s32[]{:S(2)}) async-start(), calls=%async_computation.9 | async-start | bytes 7208960 | tf_op jit(solution)/shard_map/reduce_scatter | solution.py:210
  315.0 27.4 %collective-permute-start.47 = (bf16[1024,2816]{1,0:T(8,128)(2,1)}, bf16[1024,2816]{1,0:T(8,128)(2,1)}, u32[]{:S(2)}, u32[]{:S(2)}) collective-permute-start(bf16[1024,2816]{1,0:T(8,128)(2,1)} %convolution_convert_fusion), channel_id=1, source_target_pairs={{0,4},{4,0},{8,12},{12,8},{16,20},{20,16},{24,28},{28,24},{1,5},{5... | collective-permute-start | bytes 17301512 | tf_op jit(solution)/shard_map/ppermute | solution.py:42
  359.6 184.3 %reduce-scatter.9.cloned.1.call-start = ((), (), s32[]{:S(2)}) async-start(), calls=%async_computation.10 | async-start | bytes 3932160 | tf_op jit(solution)/shard_map/reduce_scatter | solution.py:210
  439.3 31.8 %collective-permute-start.48 = (bf16[1024,2048]{1,0:T(8,128)(2,1)}, bf16[1024,2048]{1,0:T(8,128)(2,1)}, u32[]{:S(2)}, u32[]{:S(2)}) collective-permute-start(bf16[1024,2048]{1,0:T(8,128)(2,1)} %shard_map.219), channel_id=1, source_target_pairs={{0,4},{4,0},{8,12},{12,8},{16,20},{20,16},{24,28},{28,24},{1,5},{5... | collective-permute-start | bytes 12582920 | tf_op jit(solution)/shard_map/ppermute | solution.py:42
  441.3 40.1 %collective-permute-start.45 = (bf16[128,2048]{1,0:T(8,128)(2,1)S(1)}, bf16[128,2048]{1,0:T(8,128)(2,1)S(1)}, u32[]{:S(2)}, u32[]{:S(2)}) collective-permute-start(bf16[128,2048]{1,0:T(8,128)(2,1)S(1)} %fusion.6), channel_id=1, source_target_pairs={{0,8},{4,12},{8,0},{12,4},{16,24},{20,28},{24,16},{28,20},{1,9},{5... | collective-permute-start | bytes 1572872 | tf_op jit(solution)/shard_map/ppermute | solution.py:42
  444.2 37.2 %collective-permute-start.44 = (bf16[128,2048]{1,0:T(8,128)(2,1)S(1)}, bf16[128,2048]{1,0:T(8,128)(2,1)S(1)}, u32[]{:S(2)}, u32[]{:S(2)}) collective-permute-start(bf16[128,2048]{1,0:T(8,128)(2,1)S(1)} %fusion.7), channel_id=1, source_target_pairs={{0,16},{4,20},{8,24},{12,28},{16,0},{20,4},{24,8},{28,12},{1,17},{... | collective-permute-start | bytes 1572872 | tf_op jit(solution)/shard_map/ppermute | solution.py:42
  485.1 113.7 %reduce-scatter.11.cloned.1.call-start = ((), (), s32[]{:S(2)}) async-start(), calls=%async_computation.11 | async-start | bytes 1310720 | tf_op jit(solution)/shard_map/reduce_scatter | solution.py:210
  485.2 63.2 %collective-permute-start.60 = (f32[2,1024]{1,0:T(2,128)S(1)}, f32[2,1024]{1,0:T(2,128)S(1)}, u32[]{:S(2)}, u32[]{:S(2)}) collective-permute-start(f32[2,1024]{1,0:T(2,128)S(1)} %pad_maximum_fusion.7), channel_id=1, source_target_pairs={{0,4},{4,0},{8,12},{12,8},{16,20},{20,16},{24,28},{28,24},{1,5},{5... | collective-permute-start | bytes 24584 | tf_op jit(solution)/shard_map/ppermute | solution.py:42
  544.7 26.9 %collective-permute-start.57 = (bf16[2,128,2048]{2,1,0:T(8,128)(2,1)S(1)}, bf16[2,128,2048]{2,1,0:T(8,128)(2,1)}, u32[]{:S(2)}, u32[]{:S(2)}) collective-permute-start(bf16[2,128,2048]{2,1,0:T(8,128)(2,1)S(1)} %copy-done.56), channel_id=1, source_target_pairs={{0,16},{4,20},{8,24},{12,28},{16,0},{20,4},{24,8},{28,12},{1,17},{... | collective-permute-start | bytes 3145736 | tf_op jit(solution)/shard_map/ppermute | solution.py:42
  548.5 25.8 %collective-permute-start.61 = (f32[2,256]{1,0:T(2,128)S(1)}, f32[2,256]{1,0:T(2,128)S(1)}, u32[]{:S(2)}, u32[]{:S(2)}) collective-permute-start(f32[2,256]{1,0:T(2,128)S(1)} %bitcast.186), channel_id=1, source_target_pairs={{0,8},{4,12},{8,0},{12,4},{16,24},{20,28},{24,16},{28,20},{1,9},{5... | collective-permute-start | bytes 6152 | tf_op jit(solution)/shard_map/ppermute | solution.py:42
  570.1 25.8 %collective-permute-start.58 = (bf16[128,2048]{1,0:T(8,128)(2,1)}, bf16[128,2048]{1,0:T(8,128)(2,1)S(1)}, u32[]{:S(2)}, u32[]{:S(2)}) collective-permute-start(bf16[128,2048]{1,0:T(8,128)(2,1)} %fusion.3), channel_id=1, source_target_pairs={{0,16},{4,20},{8,24},{12,28},{16,0},{20,4},{24,8},{28,12},{1,17},{... | collective-permute-start | bytes 1572872 | tf_op jit(solution)/shard_map/ppermute | solution.py:42
  (130 other events, 1641.5 us)
Sparse Core Ops, SparseCore 0:
  9.6 30.7 all-gather.4
  42.5 67.1 all-gather.6
  111.9 105.3 all-gather.8
  218.7 57.4 all-gather.10
  288.7 53.5 reduce-scatter.4
  359.8 99.4 reduce-scatter.6
  485.2 57.8 reduce-scatter.8
  552.2 25.3 reduce-scatter.10

commit v5 on v4

--- a/solution.py
+++ b/solution.py
@@ -1028,6 +1028,8 @@
     d_mixed = jnp.stack(d_mixed_parts)
     d_qkv, lent = attention_back(flag, preceded, qkv, rims, d_mixed)
     lent = swap_core(lent)
+    out_send = turned(mixed_own, 1, after(d_attn, d_qkv))
+    out_back = swap_core(out_send)
     block_parts = inner_out(flag, after(hidden, d_mixed_own), down_mine, down_other, chips)
     block_near = chips_sum_near(block_parts)
 
@@ -1035,8 +1037,6 @@
     d_qkv = d_qkv.at[:, tok_count - WINDOW :, head_width:].add(returned)
     d_qkv = after(d_qkv.reshape(chips * tok_count, columns), *block_near)
     qkv_send = turned(act_one, 1, d_qkv)
-    out_send = turned(mixed_own, 1, after(d_attn, qkv_send))
-    out_back = swap_core(out_send)
     between = chips_sum_between(block_parts, after(block_near, qkv_send))
     block_far = chips_sum_send(between)
     qkv_sum = turned(act_one, 0, after(d_qkv, qkv_send, *between), swap_core(qkv_send))
@@ -1051,36 +1051,37 @@
     out_near = chips_sum_near(out_parts)
     gain_parts = jnp.concatenate([gain_one_part / gain_one, gain_two_part], axis=0)
     gain_core = swap_core(gain_parts[:, half:])
+    d_act_parts = after(d_act_parts, *out_near)
+    d_act_near = chips_sum_near(d_act_parts)
+    out_far = chips_sum_far(out_parts, out_near)
+    out_sum = summed(out_parts, out_near, out_far).astype(LOW)
+    out_grad = batch_scatter(after(out_sum, qkv_grad), 0)
+
     def columns_of_chips(grad):
         chip_rows = [
             lax.dynamic_index_in_dim(grad, chip ^ k, axis=0, keepdims=False) for k in range(chips)
         ]
         return chips_scatter(chip_rows)
 
-    out_far = chips_sum_far(out_parts, out_near)
-    inner_cells = columns_of_chips(after(inner_grad, *out_near))
-    out_sum = summed(out_parts, out_near, out_far).astype(LOW)
-    out_grad = batch_scatter(after(out_sum, qkv_grad), 0)
-    d_act_parts = after(d_act_parts, qkv_grad, *out_far, *inner_cells[1:])
-    d_act_near = chips_sum_near(d_act_parts)
-    gain_grads = (gain_parts[:, :half] + after(gain_core, qkv_grad)).reshape(2, chips, -1)
+    inner_cells = columns_of_chips(after(inner_grad, qkv_grad))
+    d_act_near = after(d_act_near, qkv_grad, *out_far)
+    d_act_far = chips_sum_far(d_act_parts, d_act_near)
+    qkv_cells = columns_of_chips(after(qkv_grad, *d_act_far))
+    gain_grads = (gain_parts[:, :half] + after(gain_core, *out_near)).reshape(2, chips, -1)
     gain_grads = chips_scatter(
         [
             lax.dynamic_index_in_dim(gain_grads, chip ^ k, axis=1, keepdims=False)
             for k in range(chips)
         ]
     )
-    d_act_far = chips_sum_far(d_act_parts, d_act_near)
     row = lax.axis_index("batch")
-    gain_grads = sum(after(gain_grads, *d_act_near))
-    gain_grads = gain_grads.reshape(2, lax.axis_size("batch"), -1)
+    gain_grads = sum(gain_grads).reshape(2, lax.axis_size("batch"), -1)
     gain_grads = sum(
         exchange(
             lax.dynamic_index_in_dim(gain_grads, row ^ k, axis=1, keepdims=False), k, "batch"
         )
         for k in range(lax.axis_size("batch"))
     )
-    qkv_cells = columns_of_chips(after(qkv_grad, *d_act_near))
     tokens_grad = last(
         flag, *summands(d_act_parts, d_act_near, d_act_far), tokens, gain_one, d_resid, chips
     )

time: 618 us -> 612 us (level)
    unnamed x179 -> x182, local copies, waits for them, and re-layouts: 36.7 us -> 41 us
  transfers between devices with their start and end apart: 78 -> 78, of which waited for: 40 -> 43; matrix products, arithmetic and copies ran while one was open for 13% -> 12% of each run, Pallas kernels for 31% -> 30%
where the time goes in v5:
time: 612 us; the launch traced here: 602 us
  waiting for transfers between devices  227 us (37%)
  Pallas kernels  182 us (30%)
  local copies, waits for them, and re-layouts  66.2 us (11%)
  starting transfers between devices  65.5 us (11%)
  other arithmetic  34.2 us (6%)
  between operations  16.1 us (3%)
  matrix products  11.1 us (2%)
    ppermute x70, waiting for transfers between devices, exchange(): lax.ppermute(value, axis, [(place, place ^ flip) for place in range(count)])  175 us
    ppermute x70, starting transfers between devices, exchange(): lax.ppermute(value, axis, [(place, place ^ flip) for place in range(count)])  64.6 us
    all_gather x4, waiting for transfers between devices, batch_gather(): return lax.all_gather(value, 'batch', axis=axis, tiled=True)  44 us
    unnamed x182, local copies, waits for them, and re-layouts  41 us
    pallas_call x5, Pallas kernels, turned(): pl.pallas_call(functools.partial(turned_kernel, len(arrived)), grid=(widt...  37.5 us
    pallas_call x2, Pallas kernels, back_project(): pl.pallas_call(functools.partial(back_project_kernel, tiles, 0 if act els...  26.6 us
    pallas_call x2, Pallas kernels, half_product(): pl.pallas_call(half_kernel, grid=(width // tile,), in_specs=[SCALAR, whol...  19.8 us
    pallas_call x1, Pallas kernels, attention_back(): pl.pallas_call(attend_back_kernel, grid=(chips,), in_specs=[SCALAR, SCALA...  16.4 us
  transfers between devices with their start and end apart: 78, of which 43 were waited for; matrix products, arithmetic and copies ran while one was open for 12% of the time, Pallas kernels for 30%

profile of v5, /device:TPU:0, one launch (start us, length us, event | category | flops | bytes accessed | tf_op | source)
XLA Modules:
  0.0 602.3 jit_solution(14340660294574998710)
XLA Ops:
  32.6 7.8 %all-gather.5.cloned.1.call-done = bf16[256,2048]{1,0:T(8,128)(2,1)} async-done(((bf16[64,2048]{1,0:T(8,128)(2,1)}), bf16[256,2048]{1,0:T(8,128)(2,1)}) %all-gather.5.cloned.1.call-update) | async-done | bytes 1048592 | tf_op jit(solution)/shard_map/all_gather | solution.py:206
  40.6 13.3 %collective-permute-done.6 = bf16[256,2048]{1,0:T(8,128)(2,1)S(1)} collective-permute-done((bf16[256,2048]{1,0:T(8,128)(2,1)S(1)}, bf16[256,2048]{1,0:T(8,128)(2,1)S(1)}, u32[]{:S(2)}, u32[]{:S(2)}) %collective-permute-start.6) | collective-permute-done | bytes 1048608 | tf_op jit(solution)/shard_map/ppermute | solution.py:42
  59.4 7.0 %collective-permute-done.8 = bf16[128,2048]{1,0:T(8,128)(2,1)S(1)} collective-permute-done((bf16[128,2048]{1,0:T(8,128)(2,1)S(1)}, bf16[128,2048]{1,0:T(8,128)(2,1)S(1)}, u32[]{:S(2)}, u32[]{:S(2)}) %collective-permute-start.8) | collective-permute-done | bytes 524320 | tf_op jit(solution)/shard_map/ppermute | solution.py:42
  89.5 16.9 %collective-permute-done.13 = bf16[256,2048]{1,0:T(8,128)(2,1)S(1)} collective-permute-done((bf16[256,2048]{1,0:T(8,128)(2,1)S(1)}, bf16[256,2048]{1,0:T(8,128)(2,1)S(1)}, u32[]{:S(2)}, u32[]{:S(2)}) %collective-permute-start.13) | collective-permute-done | bytes 1048608 | tf_op jit(solution)/shard_map/ppermute | solution.py:42
  119.7 11.4 %shard_map.203 = (bf16[1024,2048]{1,0:T(8,128)(2,1)S(1)}, bf16[1024,1536]{1,0:T(8,128)(2,1)S(1)}) custom-call(s32[1]{0:T(128)} %bitcast.core.flag, bf16[1024,2048]{1,0:T(8,128)(2,1)} %constant_dynamic-update-slice_fusion.tokens, f32[1,2048]{1,0:T(1,128)S(1)} %maximum_convert_fusion.5.gain.refs_6_, bf16[1024,1664]{1,0:T(8,128)(2,1)S(1)} %bitcast.168, ...), custom_call_target="tpu_custom_call" | custom-call | tf_op jit(solution)/shard_map/pallas_call | solution.py:263
  147.5 11.0 %shard_map.204 = bf16[4,256,512]{2,1,0:T(8,128)(2,1)S(1)} custom-call(s32[1]{0:T(128)} %bitcast.core.flag, s32[4]{0:T(128)S(1)} %or_convert_fusion.preceded, bf16[4,256,1536]{2,1,0:T(8,128)(2,1)S(1)} %bitcast.171, bf16[4,64,1024]{2,1,0:T(8,128)(2,1)S(1)} %broadcast_select_fusion.rim), custom_call_target="tpu_custom_call" | custom-call | tf_op jit(solution)/shard_map/pallas_call | solution.py:340
  187.2 30.1 %all-gather.9.cloned.1.call-done = bf16[4,256,2816]{2,1,0:T(8,128)(2,1)} async-done(((bf16[4,64,2816]{2,1,0:T(8,128)(2,1)}), bf16[4,256,2816]{2,1,0:T(8,128)(2,1)}) %all-gather.9.cloned.1.call-update) | async-done | bytes 5767184 | tf_op jit(solution)/shard_map/all_gather | solution.py:206
  221.0 11.0 %collective-permute-done.29 = bf16[128,2048]{1,0:T(8,128)(2,1)S(1)} collective-permute-done((bf16[128,2048]{1,0:T(8,128)(2,1)S(1)}, bf16[128,2048]{1,0:T(8,128)(2,1)S(1)}, u32[]{:S(2)}, u32[]{:S(2)}) %collective-permute-start.29) | collective-permute-done | bytes 524320 | tf_op jit(solution)/shard_map/ppermute | solution.py:42
  233.5 9.4 %shard_map.206.first = bf16[1024,2816]{1,0:T(8,128)(2,1)S(1)} custom-call(bf16[1024,2048]{1,0:T(8,128)(2,1)S(1)} %constant_dynamic-update-slice_fusion.15.act.left, bf16[1024,2816]{1,0:T(8,128)(2,1)S(1)} %bitcast.161, bf16[1024,2816]{1,0:T(8,128)(2,1)S(1)} %bitcast.162), custom_call_target="tpu_custom_call" | custom-call | tf_op jit(solution)/shard_map/pallas_call | solution.py:667
  245.3 12.9 %shard_map.207 = (bf16[1024,1408]{1,0:T(8,128)(2,1)S(1)}, bf16[1024,1408]{1,0:T(8,128)(2,1)S(1)}, bf16[1024,1408]{1,0:T(8,128)(2,1)S(1)}) custom-call(bf16[1024,2048]{1,0:T(8,128)(2,1)S(1)} %constant_dynamic-update-slice_fusion.15.act.left, bf16[1024,2816]{1,0:T(8,128)(2,1)} %collective-permute-done.31.gate.upward.other, ...), custom_call_target="tpu_custom_call" | custom-call | tf_op jit(solution)/shard_map/pallas_call | solution.py:690
  263.2 9.6 %shard_map.208 = bf16[704,2048]{1,0:T(8,128)(2,1)} custom-call(s32[1]{0:T(128)S(6)} %sub.16.flag, bf16[1024,1408]{1,0:T(8,128)(2,1)} %copy-done.6, bf16[1024,2048]{1,0:T(8,128)(2,1)} %copy-done.60), custom_call_target="tpu_custom_call" | custom-call | tf_op jit(solution)/shard_map/pallas_call | solution.py:880
  278.5 10.2 %shard_map.209 = bf16[704,2048]{1,0:T(8,128)(2,1)} custom-call(s32[1]{0:T(128)} %bitcast.core.flag, bf16[1024,1408]{1,0:T(8,128)(2,1)} %copy-done.6, bf16[1024,2048]{1,0:T(8,128)(2,1)} %copy-done.60, bf16[704,2048]{1,0:T(8,128)(2,1)} %collective-permute-done.32.refs_0_), custom_call_target="tpu_custom_call" | custom-call | tf_op jit(solution)/shard_map/pallas_call | solution.py:880
  290.3 13.6 %shard_map.210.d_out.right = bf16[1024,2816]{1,0:T(8,128)(2,1)} custom-call(s32[1]{0:T(128)} %bitcast.core.flag, bf16[1024,2048]{1,0:T(8,128)(2,1)} %copy-done.60, bf16[704,2048]{1,0:T(8,128)(2,1)} %all-gather.11.cloned.1.call-done.mine, bf16[704,2048]{1,0:T(8,128)(2,1)} %copy-done.23, bf16[1024,1408]{1,0:T(8,128)(2,1)} %copy-done.40, ...), custom_call_target="tpu_custom_call" | custom-call | tf_op jit(solution)/shard_map/pallas_call | solution.py:727
  303.9 11.1 %convolution_convert_fusion = bf16[1024,2816]{1,0:T(8,128)(2,1)} fusion(bf16[1024,2816]{1,0:T(8,128)(2,1)} %shard_map.210.d_out.right, bf16[1024,2048]{1,0:T(8,128)(2,1)} %copy-done.2), kind=kOutput, calls=%fused_computation.2 | convolution fusion | flops 5908463616 | bytes 13631488 | tf_op jit(solution)/shard_map/dot_general | solution.py:31
  315.1 16.1 %shard_map.211 = (bf16[256,2048]{1,0:T(8,128)(2,1)S(1)}, bf16[2,128,2048]{2,1,0:T(8,128)(2,1)S(1)}, bf16[2,128,2048]{2,1,0:T(8,128)(2,1)S(1)}, bf16[128,2048]{1,0:T(8,128)(2,1)S(1)}, bf16[128,2048]{1,0:T(8,128)(2,1)S(1)}) custom-call(bf16[1024,2816]{1,0:T(8,128)(2,1)S(1)} %copy-done.1, bf16[1024,2816]{1,0:T(8,128)(2,1)} %bitcast.160, ...), custom_call_target="tpu_custom_call" | custom-call | tf_op jit(solution)/shard_map/pallas_call | solution.py:773
  334.7 7.6 %reduce-scatter.5.cloned.1.call-done = bf16[176,2048]{1,0:T(8,128)(2,1)} async-done(((bf16[704,2048]{1,0:T(8,128)(2,1)}), bf16[176,2048]{1,0:T(8,128)(2,1)}) %reduce-scatter.5.cloned.1.call-update) | async-done | bytes 720912 | tf_op jit(solution)/shard_map/reduce_scatter | solution.py:210
  342.3 14.6 %shard_map.220 = bf16[1024,2816]{1,0:T(8,128)(2,1)} custom-call(bf16[1024,2048]{1,0:T(8,128)(2,1)} %copy-done.2, bf16[1024,2816]{1,0:T(8,128)(2,1)} %shard_map.210.d_out.right, bf16[1024,2816]{1,0:T(8,128)(2,1)} %collective-permute-done.52.refs_0_), custom_call_target="tpu_custom_call" | custom-call | tf_op jit(solution)/shard_map/pallas_call | solution.py:805
  366.1 8.6 %collective-permute-done.36.refs_3_ = bf16[128,2048]{1,0:T(8,128)(2,1)S(1)} collective-permute-done((bf16[128,2048]{1,0:T(8,128)(2,1)S(1)}, bf16[128,2048]{1,0:T(8,128)(2,1)S(1)}, u32[]{:S(2)}, u32[]{:S(2)}) %collective-permute-start.36) | collective-permute-done | bytes 524320 | tf_op jit(solution)/shard_map/ppermute | solution.py:42
  391.5 9.3 %shard_map.213 = (bf16[256,2048]{1,0:T(8,128)(2,1)S(1)}, bf16[2,128,2048]{2,1,0:T(8,128)(2,1)}, bf16[2,128,2048]{2,1,0:T(8,128)(2,1)}, bf16[128,2048]{1,0:T(8,128)(2,1)S(1)}, bf16[128,2048]{1,0:T(8,128)(2,1)S(1)}) custom-call(s32[1]{0:T(128)} %bitcast.core.flag, bf16[1024,1408]{1,0:T(8,128)(2,1)S(1)} %copy-done.7, bf16[704,2048]{1,0:T(8,128)(2,1)S(1)} %copy-done.22, ...), custom_call_target="tpu_custom_call" | custom-call | tf_op jit(solution)/shard_map/pallas_call | solution.py:840
  403.1 16.4 %shard_map.214 = (bf16[4,256,1536]{2,1,0:T(8,128)(2,1)S(1)}, bf16[4,64,1024]{2,1,0:T(8,128)(2,1)}) custom-call(s32[1]{0:T(128)} %bitcast.core.flag, s32[4]{0:T(128)S(1)} %or_convert_fusion.preceded, bf16[4,256,1536]{2,1,0:T(8,128)(2,1)S(1)} %bitcast.172, bf16[4,64,1024]{2,1,0:T(8,128)(2,1)S(1)} %copy-done.36, bf16[4,256,512]{2,1,0:T(8,128)(2,1)S(1)} %pad_maximum_fusion.1.d_mixed), custom_call_target="tpu_custom_call" | custom-call | tf_op jit(solution)/shard_map/pallas_call | solution.py:409
  452.3 10.5 %shard_map.217 = (bf16[256,2048]{1,0:T(8,128)(2,1)S(1)}, bf16[2,128,2048]{2,1,0:T(8,128)(2,1)}, bf16[2,128,2048]{2,1,0:T(8,128)(2,1)}, bf16[128,2048]{1,0:T(8,12...) custom-call(bf16[1024,1536]{1,0:T(8,128)(2,1)S(1)} %bitcast.165, bf16[1024,1664]{1,0:T(8,128)(2,1)S(1)} %bitcast.169, ...), custom_call_target="tpu_custom_call" | custom-call | tf_op jit(solution)/shard_map/pallas_call | solution.py:773
  485.2 17.2 %collective-permute-done.48 = bf16[2,128,2048]{2,1,0:T(8,128)(2,1)S(1)} collective-permute-done((bf16[2,128,2048]{2,1,0:T(8,128)(2,1)S(1)}, bf16[2,128,2048]{2,1,0:T(8,128)(2,1)S(1)}, u32[]{:S(2)}, u32[]{:S(2)}) %collective-permute-start.48) | collective-permute-done | bytes 1048608 | tf_op jit(solution)/shard_map/ppermute | solution.py:42
  512.4 16.0 %collective-permute-done.60 = f32[2,256]{1,0:T(2,128)S(1)} collective-permute-done((f32[2,256]{1,0:T(2,128)S(1)}, f32[2,256]{1,0:T(2,128)S(1)}, u32[]{:S(2)}, u32[]{:S(2)}) %collective-permute-start.60) | collective-permute-done | bytes 2080 | tf_op jit(solution)/shard_map/ppermute | solution.py:42
  559.7 15.9 %collective-permute-done.67 = bf16[64,2816]{1,0:T(8,128)(2,1)S(1)} collective-permute-done((bf16[64,2816]{1,0:T(8,128)(2,1)S(1)}, bf16[64,2816]{1,0:T(8,128)(2,1)S(1)}, u32[]{:S(2)}, u32[]{:S(2)}) %collective-permute-start.67) | collective-permute-done | bytes 360480 | tf_op jit(solution)/shard_map/ppermute | solution.py:42
  (447 shorter events, 278.4 us)
Async XLA Ops:
  7.2 33.2 %all-gather.5.cloned.1.call-start = ((), (), s32[]{:S(2)}) async-start(), calls=%async_computation.4 | async-start | bytes 1310720 | tf_op jit(solution)/shard_map/all_gather | solution.py:206
  7.9 101.8 %all-gather.7.cloned.1.call-start = ((), (), s32[]{:S(2)}) async-start(), calls=%async_computation.5 | async-start | bytes 4259840 | tf_op jit(solution)/shard_map/all_gather | solution.py:206
  40.4 176.9 %all-gather.9.cloned.1.call-start = ((), (), s32[]{:S(2)}) async-start(), calls=%async_computation.6 | async-start | bytes 7208960 | tf_op jit(solution)/shard_map/all_gather | solution.py:206
  73.7 32.7 %collective-permute-start.13 = (bf16[256,2048]{1,0:T(8,128)(2,1)S(1)}, bf16[256,2048]{1,0:T(8,128)(2,1)S(1)}, u32[]{:S(2)}, u32[]{:S(2)}) collective-permute-start(bf16[256,2048]{1,0:T(8,128)(2,1)S(1)} %get-tuple-element.104), channel_id=1, source_target_pairs={{0,8},{4,12},{8,0},{12,4},{16,24},{20,28},{24,16},{28,20},{1,9},{5... | collective-permute-start | bytes 3145736 | tf_op jit(solution)/shard_map/ppermute | solution.py:42
  74.6 32.4 %collective-permute-start.14 = (bf16[256,2048]{1,0:T(8,128)(2,1)S(1)}, bf16[256,2048]{1,0:T(8,128)(2,1)S(1)}, u32[]{:S(2)}, u32[]{:S(2)}) collective-permute-start(bf16[256,2048]{1,0:T(8,128)(2,1)S(1)} %get-tuple-element.104), channel_id=1, source_target_pairs={{0,16},{4,20},{8,24},{12,28},{16,0},{20,4},{24,8},{28,12},{1,17},{... | collective-permute-start | bytes 3145736 | tf_op jit(solution)/shard_map/ppermute | solution.py:42
  109.8 166.4 %all-gather.11.cloned.1.call-start = ((), (), s32[]{:S(2)}) async-start(), calls=%async_computation.7 | async-start | bytes 3604480 | tf_op jit(solution)/shard_map/all_gather | solution.py:206
  109.8 25.9 %collective-permute-start.17 = (bf16[256,2048]{1,0:T(8,128)(2,1)}, bf16[256,2048]{1,0:T(8,128)(2,1)}, u32[]{:S(2)}, u32[]{:S(2)}) collective-permute-start(bf16[256,2048]{1,0:T(8,128)(2,1)} %all-gather.5.cloned.1.call-done), channel_id=1, source_target_pairs={{0,8},{4,12},{8,0},{12,4},{16,24},{20,28},{24,16},{28,20},{1,9},{5... | collective-permute-start | bytes 3145736 | tf_op jit(solution)/shard_map/ppermute | solution.py:42
  111.4 27.8 %collective-permute-start.18 = (bf16[256,2048]{1,0:T(8,128)(2,1)}, bf16[256,2048]{1,0:T(8,128)(2,1)}, u32[]{:S(2)}, u32[]{:S(2)}) collective-permute-start(bf16[256,2048]{1,0:T(8,128)(2,1)} %all-gather.5.cloned.1.call-done), channel_id=1, source_target_pairs={{0,16},{4,20},{8,24},{12,28},{16,0},{20,4},{24,8},{28,12},{1,17},{... | collective-permute-start | bytes 3145736 | tf_op jit(solution)/shard_map/ppermute | solution.py:42
  131.4 27.2 %collective-permute-start.21 = (bf16[128,2048]{1,0:T(8,128)(2,1)S(1)}, bf16[128,2048]{1,0:T(8,128)(2,1)S(1)}, u32[]{:S(2)}, u32[]{:S(2)}) collective-permute-start(bf16[128,2048]{1,0:T(8,128)(2,1)S(1)} %slice.321), channel_id=1, source_target_pairs={{0,16},{4,20},{8,24},{12,28},{16,0},{20,4},{24,8},{28,12},{1,17},{... | collective-permute-start | bytes 1572872 | tf_op jit(solution)/shard_map/ppermute | solution.py:42
  185.2 32.1 %collective-permute-start.27 = (bf16[256,2048]{1,0:T(8,128)(2,1)S(1)}, bf16[256,2048]{1,0:T(8,128)(2,1)S(1)}, u32[]{:S(2)}, u32[]{:S(2)}) collective-permute-start(bf16[256,2048]{1,0:T(8,128)(2,1)S(1)} %get-tuple-element.114), channel_id=1, source_target_pairs={{0,8},{4,12},{8,0},{12,4},{16,24},{20,28},{24,16},{28,20},{1,9},{5... | collective-permute-start | bytes 3145736 | tf_op jit(solution)/shard_map/ppermute | solution.py:42
  185.7 31.6 %collective-permute-start.28 = (bf16[256,2048]{1,0:T(8,128)(2,1)S(1)}, bf16[256,2048]{1,0:T(8,128)(2,1)S(1)}, u32[]{:S(2)}, u32[]{:S(2)}) collective-permute-start(bf16[256,2048]{1,0:T(8,128)(2,1)S(1)} %get-tuple-element.114), channel_id=1, source_target_pairs={{0,16},{4,20},{8,24},{12,28},{16,0},{20,4},{24,8},{28,12},{1,17},{... | collective-permute-start | bytes 3145736 | tf_op jit(solution)/shard_map/ppermute | solution.py:42
  217.3 28.0 %collective-permute-start.31 = (bf16[1024,2816]{1,0:T(8,128)(2,1)}, bf16[1024,2816]{1,0:T(8,128)(2,1)}, u32[]{:S(2)}, u32[]{:S(2)}) collective-permute-start(bf16[1024,2816]{1,0:T(8,128)(2,1)} %bitcast.159), channel_id=1, source_target_pairs={{0,4},{4,0},{8,12},{12,8},{16,20},{20,16},{24,28},{28,24},{1,5},{5... | collective-permute-start | bytes 17301512 | tf_op jit(solution)/shard_map/ppermute | solution.py:42
  217.4 124.9 %reduce-scatter.5.cloned.1.call-start = ((), (), s32[]{:S(2)}) async-start(), calls=%async_computation.8 | async-start | bytes 3604480 | tf_op jit(solution)/shard_map/reduce_scatter | solution.py:210
  288.6 176.7 %reduce-scatter.7.cloned.1.call-start = ((), (), s32[]{:S(2)}) async-start(), calls=%async_computation.9 | async-start | bytes 7208960 | tf_op jit(solution)/shard_map/reduce_scatter | solution.py:210
  315.0 27.3 %collective-permute-start.52 = (bf16[1024,2816]{1,0:T(8,128)(2,1)}, bf16[1024,2816]{1,0:T(8,128)(2,1)}, u32[]{:S(2)}, u32[]{:S(2)}) collective-permute-start(bf16[1024,2816]{1,0:T(8,128)(2,1)} %convolution_convert_fusion), channel_id=1, source_target_pairs={{0,4},{4,0},{8,12},{12,8},{16,20},{20,16},{24,28},{28,24},{1,5},{5... | collective-permute-start | bytes 17301512 | tf_op jit(solution)/shard_map/ppermute | solution.py:42
  359.7 188.4 %reduce-scatter.9.cloned.1.call-start = ((), (), s32[]{:S(2)}) async-start(), calls=%async_computation.10 | async-start | bytes 3932160 | tf_op jit(solution)/shard_map/reduce_scatter | solution.py:210
  438.8 31.3 %collective-permute-start.47 = (bf16[1024,2048]{1,0:T(8,128)(2,1)}, bf16[1024,2048]{1,0:T(8,128)(2,1)}, u32[]{:S(2)}, u32[]{:S(2)}) collective-permute-start(bf16[1024,2048]{1,0:T(8,128)(2,1)} %shard_map.218), channel_id=1, source_target_pairs={{0,4},{4,0},{8,12},{12,8},{16,20},{20,16},{24,28},{28,24},{1,5},{5... | collective-permute-start | bytes 12582920 | tf_op jit(solution)/shard_map/ppermute | solution.py:42
  465.4 127.9 %reduce-scatter.11.cloned.1.call-start = ((), (), s32[]{:S(2)}) async-start(), calls=%async_computation.11 | async-start | bytes 1310720 | tf_op jit(solution)/shard_map/reduce_scatter | solution.py:210
  477.5 26.1 %collective-permute-start.49 = (bf16[2,128,2048]{2,1,0:T(8,128)(2,1)S(1)}, bf16[2,128,2048]{2,1,0:T(8,128)(2,1)S(1)}, u32[]{:S(2)}, u32[]{:S(2)}) collective-permute-start(bf16[2,128,2048]{2,1,0:T(8,128)(2,1)S(1)} %get-tuple-element.155), channel_id=1, source_target_pairs={{0,16},{4,20},{8,24},{12,28},{16,0},{20,4},{24,8},{28,12},{1,17},{... | collective-permute-start | bytes 3145736 | tf_op jit(solution)/shard_map/ppermute | solution.py:42
  479.0 25.8 %collective-permute-start.57 = (f32[2,1024]{1,0:T(2,128)S(1)}, f32[2,1024]{1,0:T(2,128)S(1)}, u32[]{:S(2)}, u32[]{:S(2)}) collective-permute-start(f32[2,1024]{1,0:T(2,128)S(1)} %pad_maximum_fusion.7), channel_id=1, source_target_pairs={{0,4},{4,0},{8,12},{12,8},{16,20},{20,16},{24,28},{28,24},{1,5},{5... | collective-permute-start | bytes 24584 | tf_op jit(solution)/shard_map/ppermute | solution.py:42
  503.6 44.4 %collective-permute-start.50 = (bf16[2,128,2048]{2,1,0:T(8,128)(2,1)}, bf16[2,128,2048]{2,1,0:T(8,128)(2,1)}, u32[]{:S(2)}, u32[]{:S(2)}) collective-permute-start(bf16[2,128,2048]{2,1,0:T(8,128)(2,1)} %get-tuple-element.157), channel_id=1, source_target_pairs={{0,8},{4,12},{8,0},{12,4},{16,24},{20,28},{24,16},{28,20},{1,9},{5... | collective-permute-start | bytes 3145736 | tf_op jit(solution)/shard_map/ppermute | solution.py:42
  504.2 43.9 %collective-permute-start.51 = (bf16[2,128,2048]{2,1,0:T(8,128)(2,1)}, bf16[2,128,2048]{2,1,0:T(8,128)(2,1)}, u32[]{:S(2)}, u32[]{:S(2)}) collective-permute-start(bf16[2,128,2048]{2,1,0:T(8,128)(2,1)} %get-tuple-element.158), channel_id=1, source_target_pairs={{0,16},{4,20},{8,24},{12,28},{16,0},{20,4},{24,8},{28,12},{1,17},{... | collective-permute-start | bytes 3145736 | tf_op jit(solution)/shard_map/ppermute | solution.py:42
  551.2 30.5 %collective-permute-start.55 = (bf16[128,2048]{1,0:T(8,128)(2,1)}, bf16[128,2048]{1,0:T(8,128)(2,1)S(1)}, u32[]{:S(2)}, u32[]{:S(2)}) collective-permute-start(bf16[128,2048]{1,0:T(8,128)(2,1)} %fusion.3), channel_id=1, source_target_pairs={{0,16},{4,20},{8,24},{12,28},{16,0},{20,4},{24,8},{28,12},{1,17},{... | collective-permute-start | bytes 1572872 | tf_op jit(solution)/shard_map/ppermute | solution.py:42
  554.3 27.5 %collective-permute-start.56 = (bf16[128,2048]{1,0:T(8,128)(2,1)}, bf16[128,2048]{1,0:T(8,128)(2,1)S(1)}, u32[]{:S(2)}, u32[]{:S(2)}) collective-permute-start(bf16[128,2048]{1,0:T(8,128)(2,1)} %fusion.2), channel_id=1, source_target_pairs={{0,8},{4,12},{8,0},{12,4},{16,24},{20,28},{24,16},{28,20},{1,9},{5... | collective-permute-start | bytes 1572872 | tf_op jit(solution)/shard_map/ppermute | solution.py:42
  (132 other events, 1493.1 us)
Sparse Core Ops, SparseCore 0:
  9.6 30.7 all-gather.4
  42.5 67.1 all-gather.6
  111.9 105.3 all-gather.8
  218.7 57.4 all-gather.10
  288.8 53.5 reduce-scatter.4
  359.8 99.3 reduce-scatter.6
  465.5 57.8 reduce-scatter.8
  555.1 24.8 reduce-scatter.10
